TPU v7x, 128 devices: a whole 4x4x4 slice. The times are simulated.
128 devices in a mesh: dp: 4 (over z), section: 2 (over core), seq: 16 (over x, y).
Axes of the slice: x: 4, y: 4, z: 4, core: 2. Of those that a mesh axis runs over, the one named last changes fastest.
Arguments:
- inputs: bfloat16 [2, 4, 2048, 1024], P(None, 'dp', 'seq'), may hold values from -6 to 6
- out_grad: bfloat16 [2, 4, 2048, 1024], P(None, 'dp', 'seq'), may hold values from -6 to 6
- norm_gain: bfloat16 [2, 1024], P('section', ('dp', 'seq')), may hold values from 0.5 to 1.5
- w_in: bfloat16 [2, 1024, 4384], P('section', ('dp', 'seq')), may hold values from -0.1875 to 0.1875
- conv_w: bfloat16 [2, 4, 2304], P('section', None, ('dp', 'seq')), may hold values from -3 to 3
- conv_b: bfloat16 [2, 2304], P('section', ('dp', 'seq')), may hold values from -3 to 3
- dt_bias: float32 [2, 32], P('section'), may hold values from -7 to -3
- a_log: float32 [2, 32], P('section'), may hold values from -1 to 2
- d_skip: float32 [2, 32], P('section'), may hold values from 0.25 to 1
- gnorm_gain: bfloat16 [2, 2048], P('section', ('dp', 'seq')), may hold values from 0.5 to 1.5
- w_out: bfloat16 [2, 2048, 1024], P('section', ('dp', 'seq')), may hold values from -0.125 to 0.125
Outputs:
- outputs: bfloat16 [2, 4, 2048, 1024], P(None, 'dp', 'seq', 'section')
- in_grad: float32 [2, 4, 2048, 1024], P(None, 'dp', 'seq', 'section')
- grad_norm_gain: float32 [2, 1024], P('section', ('dp', 'seq'))
- grad_w_in: float32 [2, 1024, 4384], P('section', ('dp', 'seq'))
- grad_conv_w: float32 [2, 4, 2304], P('section', None, ('dp', 'seq'))
- grad_conv_b: float32 [2, 2304], P('section', ('dp', 'seq'))
- grad_dt_bias: float32 [2, 32], P('section')
- grad_a_log: float32 [2, 32], P('section')
- grad_d_skip: float32 [2, 32], P('section')
- grad_gnorm_gain: float32 [2, 2048], P('section', ('dp', 'seq'))
- grad_w_out: float32 [2, 2048, 1024], P('section', ('dp', 'seq'))
All inputs are finite; a program needn't handle non-finite values.
Results may differ from a plain program's by a relative error of at most 0.035.
Values may be sent and summed in bfloat16 or wider, within the bound.
No kernel may reach another device: no remote copies, remote signals or barrier semaphores. Data moves between devices by JAX's collectives and lax.ppermute only.
A program may use at most 256 MiB of HBM per device.

v0:
```python
import jax
import jax.numpy as jnp
from jax import lax
from jax.experimental import pallas as pl
from jax.experimental.pallas import tpu as pltpu
from jax.sharding import PartitionSpec as P

DIN = 2048
HEADS = 32
STATE = 128
KW = 4
EIN = 4384
EINP = 4480
CONV_CH = 2304
DT_COL = 2 * DIN + 2 * STATE
T = 128
D = 1024
TILE = 512
XBC = 2560
DT = 2304
WIDE = DIN + XBC
PAIRS = 16
PAY = STATE + 16

f32 = jnp.float32
bf16 = jnp.bfloat16
epsilon = 1e-05
highest = lax.Precision.HIGHEST
both = ("dp", "seq")


def dot(a, b, precision=None):
    return jnp.dot(a, b, preferred_element_type=f32, precision=precision)


def dot_nt(a, b):
    return lax.dot_general(a, b, (((1,), (1,)), ((), ())), preferred_element_type=f32)


def dot_tn(a, b):
    return lax.dot_general(a, b, (((0,), (0,)), ((), ())), preferred_element_type=f32)


def low_half():
    return lax.broadcasted_iota(jnp.int32, (1, T), 1) < 64


def lower_triangle():
    rows = lax.broadcasted_iota(jnp.int32, (T, T), 0)
    columns = lax.broadcasted_iota(jnp.int32, (T, T), 1)
    return rows >= columns


def sigmoid(v):
    return 1.0 / (1.0 + jnp.exp(-v))


def silu_and_slope(v):
    s = sigmoid(v)
    return v * s, s * (1.0 + v * (1.0 - s))


def spread(table, j):
    return jnp.where(low_half(), table[:, 2 * j : 2 * j + 1], table[:, 2 * j + 1 : 2 * j + 2])


def block(j):
    return slice(j * T, (j + 1) * T)


def conv_block(padded, taps, j):
    total = taps[KW : KW + 1, block(j)] + taps[0:1, block(j)] * padded[13 : 13 + T, block(j)]
    for k in range(1, KW):
        total = total + taps[k : k + 1, block(j)] * padded[13 + k : 13 + k + T, block(j)]
    return total


def load_padded(padded, xbc, halo):
    padded[0:16, :] = halo[...].astype(f32)
    padded[16 : 16 + T, :] = xbc[:, 0:DT].astype(f32)


def put_payload(payload, j, state, totals):
    payload[j, 0:STATE, :] = state.astype(bf16)
    factor = spread(totals, j)
    high = factor.astype(bf16).astype(f32)
    rest = factor - high
    row = lax.broadcasted_iota(jnp.int32, (16, T), 0)
    extra = jnp.where(row == 0, high, jnp.where(row == 1, rest, 0.0))
    payload[j, STATE:PAY, :] = extra.astype(bf16)


def shuffle():
    source = lax.broadcasted_iota(jnp.int32, (256, 256), 0)
    target = lax.broadcasted_iota(jnp.int32, (256, 256), 1)
    k, i, r = source >> 5, (source >> 4) & 1, source & 15
    return jnp.where(target == i * T + k * 16 + r, 1.0, 0.0).astype(bf16)


def front_kernel(xbc, halo, taps, heads, xs, bc, delta, cum, payload, padded):
    load_padded(padded, xbc, halo)
    lane = lax.broadcasted_iota(jnp.int32, (1, T), 1)
    raw = xbc[:, DT : DT + T].astype(f32) + heads[0:1, :]
    soft = jnp.maximum(raw, 0.0) + jnp.log1p(jnp.exp(-jnp.abs(raw)))
    steps = jnp.where(lane < HEADS, soft, 0.0)
    delta[...] = steps
    logs = steps * -jnp.exp(heads[1:2, :])
    sums = dot(lower_triangle().astype(f32), logs, highest)
    cum[...] = sums
    last = sums[T - 1 : T, :]
    weight = jnp.exp(last - sums) * steps
    totals = jnp.exp(last)
    b_pre = conv_block(padded, taps, PAIRS)
    c_pre = conv_block(padded, taps, PAIRS + 1)
    keys = b_pre * sigmoid(b_pre)
    bc[:, 0:STATE] = keys.astype(bf16)
    bc[:, STATE:] = (c_pre * sigmoid(c_pre)).astype(bf16)
    keys_t = keys.T.astype(bf16)
    for j in range(PAIRS):
        pre = conv_block(padded, taps, j)
        x = pre * sigmoid(pre)
        xs[:, block(j)] = x
        put_payload(payload, j, dot(keys_t, (spread(weight, j) * x).astype(bf16)), totals)


def scan_kernel(backward, payload, entering):
    carried = jnp.zeros((STATE, T), f32)
    order = range(PAIRS - 1, -1, -1) if backward else range(PAIRS)
    for k in order:
        entering[k] = carried.astype(bf16)
        extra = payload[k, STATE:PAY, :].astype(f32)
        factor = extra[0:1, :] + extra[1:2, :]
        carried = factor * carried + payload[k, 0:STATE, :].astype(f32)


def decay(cum, cum_t, h, causal):
    return jnp.where(causal, jnp.exp(cum[:, h : h + 1] - cum_t[h : h + 1, :]), 0.0)


def halves(v):
    return jnp.concatenate(
        [jnp.where(low_half(), v, 0.0), jnp.where(low_half(), 0.0, v)], axis=0
    ).astype(bf16)


def within_kernel(xs, bc, delta, cum, heads, local):
    causal = lower_triangle()
    cums = cum[...]
    cum_t = cums.T
    steps = delta[...]
    skips = heads[2:3, :]
    scores = dot_nt(bc[:, STATE:], bc[:, 0:STATE])
    for j in range(PAIRS):
        x = xs[:, block(j)]
        mixing = jnp.concatenate(
            [scores * decay(cums, cum_t, 2 * j + i, causal) for i in range(2)], axis=1
        ).astype(bf16)
        local[:, block(j)] = dot(mixing, halves(spread(steps, j) * x)) + spread(skips, j) * x


def project_kernel(stream, gain, weight, hidden, projected):
    @pl.when(pl.program_id(0) == 0)
    def _():
        values = stream[...]
        inverse = lax.rsqrt(jnp.sum(values * values, axis=1, keepdims=True) / D + epsilon)
        hidden[...] = (values * inverse * gain[...]).astype(bf16)

    projected[...] = dot(hidden[...], weight[...]).astype(bf16)


def finish_kernel(
    local, bc, cum, entering, gates, gain, stream, weight_0, weight_1, mixed, normed, result, gated,
    shuffled,
):
    @pl.when(pl.program_id(0) == 0)
    def _():
        growth = jnp.exp(cum[...])
        queries = bc[:, STATE:]
        squares = jnp.zeros((T, T), f32)
        for j in range(PAIRS):
            whole = local[:, block(j)] + spread(growth, j) * dot(queries, entering[j])
            rounded = whole.astype(bf16)
            mixed[:, block(j)] = rounded
            gate = gates[:, block(j)].astype(f32)
            u = rounded.astype(f32) * (gate * sigmoid(gate))
            gated[:, block(j)] = u
            squares = squares + u * u
        scale = lax.rsqrt(jnp.sum(squares, axis=1, keepdims=True) / DIN + epsilon)
        for j in range(PAIRS):
            normed[:, block(j)] = (gated[:, block(j)] * scale * gain[0:1, block(j)]).astype(bf16)

        order = shuffle()
        for b in range(8):
            moved = dot(normed[:, b * 256 : (b + 1) * 256], order)
            shuffled[0, :, block(b)] = moved[:, 0:T]
            shuffled[1, :, block(b)] = moved[:, T:]

    result[...] = (
        stream[...]
        + dot(shuffled[0].astype(bf16), weight_0[...])
        + dot(shuffled[1].astype(bf16), weight_1[...])
    )


def top_kernel(
    upstream, weight, mixed, gates, gain, bc, cum, d_mixed, d_gate, d_gain, payload, d_shuffled,
    d_normed, gated,
):
    step = pl.program_id(0)
    d_shuffled[step] = dot_nt(upstream[...], weight[...])

    def part(j):
        return d_normed[:, block(j)]

    @pl.when(step == 1)
    def _():
        order = shuffle()
        for b in range(8):
            value = jnp.concatenate([d_shuffled[0, :, block(b)], d_shuffled[1, :, block(b)]], axis=1)
            high = value.astype(bf16)
            rest = (value - high.astype(f32)).astype(bf16)
            d_normed[:, b * 256 : (b + 1) * 256] = dot_nt(high, order) + dot_nt(rest, order)
        squares = jnp.zeros((T, T), f32)
        products = jnp.zeros((T, T), f32)
        for j in range(PAIRS):
            gate = gates[:, block(j)].astype(f32)
            u = mixed[:, block(j)].astype(f32) * (gate * sigmoid(gate))
            gated[:, block(j)] = u
            squares = squares + u * u
            products = products + part(j) * gain[0:1, block(j)] * u
        scale = lax.rsqrt(jnp.sum(squares, axis=1, keepdims=True) / DIN + epsilon)
        pull = scale * scale * scale * (jnp.sum(products, axis=1, keepdims=True) / DIN)
        cums = cum[...]
        growth = jnp.exp(cums)
        totals = growth[T - 1 : T, :]
        queries_t = bc[:, STATE:].astype(f32).T.astype(bf16)
        for j in range(PAIRS):
            gate = gates[:, block(j)].astype(f32)
            act, slope = silu_and_slope(gate)
            u = gated[:, block(j)]
            up = part(j)
            d_gain[:, block(j)] = jnp.broadcast_to(
                jnp.sum(up * u * scale, axis=0, keepdims=True), (8, T)
            )
            du = up * gain[0:1, block(j)] * scale - u * pull
            dm = (du * act).astype(bf16)
            d_mixed[:, block(j)] = dm
            d_gate[:, block(j)] = (du * mixed[:, block(j)].astype(f32) * slope).astype(bf16)
            put_payload(
                payload, j, dot(queries_t, (spread(growth, j) * dm.astype(f32)).astype(bf16)), totals
            )


def inner_kernel(xs, bc, delta, cum, d_mixed, entering, d_scaled, d_bc, d_cum, rows, columns):
    causal = lower_triangle()
    cums = cum[...]
    cum_t = cums.T
    steps = delta[...]
    growth = jnp.exp(cums)
    keys = bc[:, 0:STATE]
    queries = bc[:, STATE:]
    scores = dot_nt(queries, keys)
    rows[...] = jnp.zeros((T, T), f32)
    columns[...] = jnp.zeros((T, T), f32)
    d_scores = jnp.zeros((T, T), f32)
    d_queries = jnp.zeros((T, STATE), f32)
    for j in range(PAIRS):
        dy_low = d_mixed[:, block(j)]
        dy = dy_low.astype(f32)
        scaled = halves(spread(steps, j) * xs[:, block(j)])
        d_mixing = dot_nt(dy_low, scaled)
        grown = spread(growth, j) * dy
        across = grown * dot(queries, entering[j])
        d_queries = d_queries + dot_nt(grown.astype(bf16), entering[j])
        mixings = []
        for i in range(2):
            h = 2 * j + i
            fall = decay(cums, cum_t, h, causal)
            d_part = d_mixing[:, i * T : (i + 1) * T] * fall
            d_scores = d_scores + d_part
            mixings.append(scores * fall)
            logs = d_part * scores
            own = jnp.where(low_half(), across, 0.0) if i == 0 else jnp.where(low_half(), 0.0, across)
            rows[:, h : h + 1] = jnp.sum(logs + own, axis=1, keepdims=True)
            columns[h : h + 1, :] = jnp.sum(logs, axis=0, keepdims=True)
        d_scaled[:, block(j)] = dot_tn(
            jnp.concatenate(mixings, axis=0).astype(bf16), halves(dy)
        )
    d_low = d_scores.astype(bf16)
    d_bc[:, 0:STATE] = dot_tn(d_low, queries)
    d_bc[:, STATE:] = d_queries + dot(d_low, keys)
    d_cum[...] = rows[...] - columns[...].T


def outer_kernel(
    xbc, halo, taps, heads, xs, bc, delta, cum, d_mixed, d_scaled, d_bc, d_cum, entering,
    leaving, d_conv, d_dt, d_taps, d_heads, padded, falls, direct, rest,
):
    load_padded(padded, xbc, halo)
    lane = lax.broadcasted_iota(jnp.int32, (1, T), 1)
    cums = cum[...]
    steps = delta[...]
    last = cums[T - 1 : T, :]
    weight = jnp.exp(last - cums)
    totals = jnp.exp(last)
    skips = heads[2:3, :]
    keys = bc[:, 0:STATE]
    falls[...] = jnp.zeros((T, T), f32)
    direct[...] = jnp.zeros((T, T), f32)
    rest[...] = jnp.zeros((8, T), f32)
    low = low_half()

    def conv_back(j, grad):
        pre = conv_block(padded, taps, j)
        d_pre = grad * silu_and_slope(pre)[1]
        d_conv[:, block(j)] = d_pre
        for k in range(KW):
            d_taps[k : k + 1, block(j)] = jnp.sum(
                d_pre * padded[13 + k : 13 + k + T, block(j)], axis=0, keepdims=True
            )
        d_taps[KW : KW + 1, block(j)] = jnp.sum(d_pre, axis=0, keepdims=True)

    d_taps[KW + 1 : 8, :] = jnp.zeros((8 - KW - 1, CONV_CH), f32)
    d_keys = d_bc[:, 0:STATE]
    for j in range(PAIRS):
        x = xs[:, block(j)]
        dy = d_mixed[:, block(j)].astype(f32)
        step = spread(steps, j)
        fall = spread(weight, j)
        weighted = fall * (step * x)
        back = dot(keys, leaving[j])
        d_keys = d_keys + dot_nt(weighted.astype(bf16), leaving[j])
        ds = d_scaled[:, block(j)] + fall * back
        flow = weighted * back
        touch = ds * x
        kept = jnp.sum(leaving[j].astype(f32) * entering[j].astype(f32), axis=0, keepdims=True)
        kept = kept * spread(totals, j)
        skipped = jnp.sum(dy * x, axis=0, keepdims=True)
        for i in range(2):
            h = 2 * j + i
            pick = (lambda v: jnp.where(low, v, 0.0)) if i == 0 else (lambda v: jnp.where(low, 0.0, v))
            falls[:, h : h + 1] = jnp.sum(pick(flow), axis=1, keepdims=True)
            direct[:, h : h + 1] = jnp.sum(pick(touch), axis=1, keepdims=True)
            rest[0:1, h : h + 1] = jnp.sum(pick(kept), axis=1, keepdims=True)
            rest[1:2, h : h + 1] = jnp.sum(pick(skipped), axis=1, keepdims=True)
        conv_back(j, step * ds + spread(skips, j) * dy)
    conv_back(PAIRS, d_keys)
    conv_back(PAIRS + 1, d_bc[:, STATE:])
    flows = falls[...]
    gained = rest[0:1, :] + jnp.sum(flows, axis=0, keepdims=True)
    row = lax.broadcasted_iota(jnp.int32, (T, T), 0)
    d_sums = d_cum[...] - flows + jnp.where(row == T - 1, gained, 0.0)
    upper = lower_triangle().astype(f32).T
    d_logs = dot(upper, d_sums, highest)
    rate = -jnp.exp(heads[1:2, :])
    d_delta = direct[...] + d_logs * rate
    slope = sigmoid(xbc[:, DT : DT + T].astype(f32) + heads[0:1, :])
    grad = jnp.where(lane < HEADS, d_delta * slope, 0.0)
    d_dt[...] = grad
    d_heads[...] = jnp.zeros((8, T), f32)
    d_heads[0:1, :] = jnp.sum(grad, axis=0, keepdims=True)
    d_heads[1:2, :] = jnp.sum(d_logs * steps, axis=0, keepdims=True) * rate
    d_heads[2:3, :] = rest[1:2, :]


def bottom_kernel(
    d_conv, halo, taps, d_gate, d_dt, weight, stream, norm, upstream, d_projected, result, d_norm,
    padded, total,
):
    step = pl.program_id(0)

    @pl.when(step == 0)
    def _():
        padded[0:T, :] = d_conv[...]
        padded[T : T + 8, :] = halo[...]
        d_projected[:, 0:DIN] = d_gate[...]
        for j in range(CONV_CH // T):
            value = taps[KW - 1 : KW, block(j)] * padded[0:T, block(j)]
            for k in range(KW - 1):
                shift = KW - 1 - k
                value = value + taps[k : k + 1, block(j)] * padded[shift : shift + T, block(j)]
            d_projected[:, DIN + j * T : DIN + (j + 1) * T] = value.astype(bf16)
        d_projected[:, DT_COL:EINP] = d_dt[...].astype(bf16)
        d_projected[:, EINP:WIDE] = jnp.zeros((T, T), bf16)
        total[...] = jnp.zeros((T, D), f32)

    columns = pl.ds(pl.multiple_of(step * TILE, T), TILE)
    total[...] += dot_nt(d_projected[:, columns], weight[...])

    @pl.when(step == WIDE // TILE - 1)
    def _():
        values = stream[...]
        d_hidden = total[...]
        inverse = lax.rsqrt(jnp.sum(values * values, axis=1, keepdims=True) / D + epsilon)
        d_norm[...] = jnp.broadcast_to(
            jnp.sum(d_hidden * values * inverse, axis=0, keepdims=True), (8, D)
        )
        scaled = d_hidden * norm[...]
        mean = jnp.sum(scaled * values, axis=1, keepdims=True) / D
        pull = inverse * inverse * inverse * mean
        result[...] = upstream[...] + scaled * inverse - values * pull


def dropping(kernel, count, extra):
    return lambda *refs: kernel(*refs[:count], *refs[count + extra :])


def call(kernel, outs, scratch, name, micros, *args, after=()):
    return pl.pallas_call(
        dropping(kernel, len(args), len(after)),
        out_shape=[jax.ShapeDtypeStruct(shape, dtype) for shape, dtype in outs],
        scratch_shapes=[pltpu.VMEM(shape, f32) for shape in scratch],
        compiler_params=pltpu.CompilerParams(vmem_limit_bytes=40 * 2**20),
        in_specs=[pl.BlockSpec(memory_space=pltpu.VMEM)] * len(args)
        + [pl.BlockSpec(memory_space=pl.ANY)] * len(after),
        cost_estimate=cost(micros),
        name=name,
    )(*args, *after)


def cost(micros):
    return pl.CostEstimate(flops=0, transcendentals=0, bytes_accessed=int(micros * 3.5e6))


def whole(array):
    rank = len(array.shape)
    return pl.BlockSpec(array.shape, lambda n: (0,) * rank)


def call_tiled(kernel, steps, args, specs, outs, scratch, name, micros, after=()):
    shapes = [jax.ShapeDtypeStruct(shape, dtype) for shape, dtype, _ in outs]
    return pl.pallas_call(
        dropping(kernel, len(args), len(after)),
        grid=(steps,),
        in_specs=[whole(v) if spec is None else spec for v, spec in zip(args, specs)]
        + [pl.BlockSpec(memory_space=pl.ANY) for _ in after],
        out_specs=[whole(v) if o[2] is None else o[2] for v, o in zip(shapes, outs)],
        out_shape=shapes,
        scratch_shapes=[pltpu.VMEM(shape, f32) for shape in scratch],
        compiler_params=pltpu.CompilerParams(vmem_limit_bytes=44 * 2**20),
        cost_estimate=cost(micros),
        name=name,
    )(*args, *after)


def swap(value):
    return lax.ppermute(value, "section", [(0, 1), (1, 0)])


def to_owners(value):
    came = lax.all_to_all(value, "seq", split_axis=0, concat_axis=0, tiled=True)
    return jnp.sum(came.astype(f32), axis=0)


def to_layers(value):
    me = lax.axis_index("dp")

    def piece(steps):
        return lax.dynamic_index_in_dim(value, (me + steps) % 4, 0, keepdims=False)

    total = piece(0).astype(f32)
    for steps in (1, -1, 2):
        moved = lax.ppermute(piece(steps), "dp", [(i, (i + steps) % 4) for i in range(4)])
        total = total + moved.astype(f32)
    return total


def to_layers_in_order(value):
    me = lax.axis_index("dp")
    came = [lax.dynamic_index_in_dim(value, me, 0, keepdims=False)]
    for steps in (1, 2, 3):
        part = lax.dynamic_index_in_dim(value, (me + steps) % 4, 0, keepdims=False)
        came.append(lax.ppermute(part, "dp", [(i, (i + steps) % 4) for i in range(4)]))
    came = jnp.stack(came)
    total = lax.dynamic_index_in_dim(came, me, 0, keepdims=False)
    for source in (1, 2, 3):
        total = total + lax.dynamic_index_in_dim(came, (me - source) % 4, 0, keepdims=False)
    return total


def in_chip(grad, rows):
    columns = grad.shape[1]
    shaped = grad.reshape(64, 2, rows // 2, columns)
    section = lax.axis_index("section")
    mine = lax.dynamic_index_in_dim(shaped, section, 1, keepdims=False)
    theirs = lax.dynamic_index_in_dim(shaped, 1 - section, 1, keepdims=False)
    total = (mine.astype(f32) + swap(theirs).astype(f32)).astype(bf16)
    return total.reshape(4, 16, rows // 2, columns)


def own_layer(halves_of, first):
    keep = jnp.where(first, halves_of[0], halves_of[1])
    give = jnp.where(first, halves_of[1], halves_of[0])
    came = swap(give.astype(f32))
    keep = keep.astype(f32)
    return jnp.where(
        first, jnp.concatenate([keep, came], axis=0), jnp.concatenate([came, keep], axis=0)
    )


def exchange(payload, backward):
    moved = lax.all_to_all(payload, "seq", split_axis=0, concat_axis=0, tiled=True)
    (entering,) = call(
        lambda *refs: scan_kernel(backward, *refs),
        [((PAIRS, STATE, T), bf16)],
        [],
        "scan_back" if backward else "scan",
        2,
        moved,
    )
    return lax.all_to_all(entering, "seq", split_axis=0, concat_axis=0, tiled=True)


def forward_layer(stream, w):
    l = w["layer"]
    columns = DIN if w["xbc"] is not None else WIDE
    hidden, projected = call_tiled(
        project_kernel,
        columns // TILE,
        (stream, w["norm"], w["all"]),
        (None, None, pl.BlockSpec((D, TILE), lambda n: (l, 4 + n))),
        [((T, D), bf16, None), ((T, columns), bf16, pl.BlockSpec((T, TILE), lambda n: (0, n)))],
        [],
        "project",
        4,
    )
    gates = projected[:, :DIN]
    xbc = projected[:, DIN:] if w["xbc"] is None else w["xbc"]
    halo = lax.ppermute(xbc[T - 16 :, :DT], "seq", [(i, i + 1) for i in range(15)])
    xs, bc, delta, cum, payload = call(
        front_kernel,
        [((T, DIN), f32), ((T, 2 * STATE), bf16), ((T, T), f32), ((T, T), f32), ((PAIRS, PAY, T), bf16)],
        [(T + 16, CONV_CH)],
        "front",
        2,
        xbc,
        halo,
        w["taps"],
        w["heads"],
    )
    entering = exchange(payload, False)
    (local,) = call(within_kernel, [((T, DIN), f32)], [], "within", 2, xs, bc, delta, cum, w["heads"])
    narrow = pl.BlockSpec((T, 512), lambda n: (0, n))
    mixed, normed, result = call_tiled(
        finish_kernel,
        2,
        (local, bc, cum, entering, gates, w["gnorm"], stream, w["all"], w["all"]),
        (None,) * 6
        + (narrow, pl.BlockSpec((D, 512), lambda n: (l, n)), pl.BlockSpec((D, 512), lambda n: (l, 2 + n))),
        [((T, DIN), bf16, None), ((T, DIN), bf16, None), ((T, D), f32, narrow)],
        [(T, DIN), (2, T, D)],
        "finish",
        5,
    )
    return (stream, hidden, gates, xbc, halo, xs, bc, delta, cum, entering, mixed, normed), result


def backward_layer(kept, upstream, w, earlier=None, outputs=()):
    stream, hidden, gates, xbc, halo, xs, bc, delta, cum, entering, mixed, normed = kept
    upstream_low = upstream.astype(bf16)
    l = w["layer"]
    d_mixed, d_gate, d_gain, payload = call_tiled(
        top_kernel,
        2,
        (upstream_low, w["all"], mixed, gates, w["gnorm"], bc, cum),
        (None, pl.BlockSpec((D, D), lambda n: (l, n))) + (None,) * 5,
        [
            ((T, DIN), bf16, None),
            ((T, DIN), bf16, None),
            ((8, DIN), f32, None),
            ((PAIRS, PAY, T), bf16, None),
        ],
        [(2, T, D), (T, DIN), (T, DIN)],
        "top",
        5,
    )
    grad_out = dot_tn(normed, upstream_low).astype(bf16)
    leaving = exchange(payload, True)
    out_total = in_chip(grad_out, 32)
    grad_out = to_layers(out_total).astype(bf16)
    ordered = (grad_out,)
    if earlier is not None:
        leaving, earlier = lax.optimization_barrier((leaving, earlier))
        ordered = (grad_out, earlier)
    d_scaled, d_bc, d_cum = call(
        inner_kernel,
        [((T, DIN), f32), ((T, 2 * STATE), f32), ((T, T), f32)],
        [(T, T), (T, T)],
        "inner",
        8,
        xs,
        bc,
        delta,
        cum,
        d_mixed,
        entering,
    )
    d_conv, d_dt, d_taps, d_heads = call(
        outer_kernel,
        [((T, CONV_CH), f32), ((T, T), f32), ((8, CONV_CH), f32), ((8, T), f32)],
        [(T + 16, CONV_CH), (T, T), (T, T), (8, T)],
        "outer",
        5,
        xbc,
        halo,
        w["taps"],
        w["heads"],
        xs,
        bc,
        delta,
        cum,
        d_mixed,
        d_scaled,
        d_bc,
        d_cum,
        entering,
        leaving,
        after=(out_total, *outputs),
    )
    halo_back = lax.ppermute(d_conv[0:8], "seq", [(i + 1, i) for i in range(15)])
    d_projected, result, d_norm = call_tiled(
        bottom_kernel,
        WIDE // TILE,
        (d_conv, halo_back, w["taps"], d_gate, d_dt, w["all"], stream, w["norm"], upstream),
        (None,) * 5 + (pl.BlockSpec((D, TILE), lambda n: (l, 4 + n)),) + (None,) * 3,
        [((T, WIDE), bf16, None), ((T, D), f32, None), ((8, D), f32, None)],
        [(T + 8, CONV_CH), (T, D)],
        "bottom",
        6,
        ordered,
    )
    grad_in = dot_tn(hidden, d_projected[:, :EINP]).astype(bf16)
    small = pack_small(d_norm[0], d_taps, d_gain[0], d_heads)
    return result, grad_in, grad_out, small, earlier


def pack_small(grad_norm, d_taps, d_gain, d_heads):
    def padded(v):
        return jnp.pad(v, ((0, 0), (0, T - v.shape[1])))

    rows = [padded(d_taps[k].reshape(64, 36)) for k in range(KW + 1)]
    rows.append(padded(grad_norm.reshape(64, 16)))
    rows.append(padded(d_gain.reshape(64, 32)))
    heads = d_heads[0:3, 0:HEADS].reshape(1, 3 * HEADS)
    rows.append(jnp.broadcast_to(padded(heads), (64, T)))
    return jnp.stack(rows, axis=1)


def turned(value, axis, steps):
    if axis == "z":
        return lax.ppermute(value, "dp", [(i, (i + steps) % 4) for i in range(4)])
    pairs = []
    for i in range(16):
        x, y = divmod(i, 4)
        if axis == "x":
            pairs.append((i, (x + steps) % 4 * 4 + y))
        else:
            pairs.append((i, x * 4 + (y + steps) % 4))
    return lax.ppermute(value, "seq", pairs)


def gathered_along(value, axis):
    seq = lax.axis_index("seq")
    me = {"z": lax.axis_index("dp"), "x": seq // 4, "y": seq % 4}[axis]
    out = jnp.zeros((4,) + value.shape, value.dtype)
    came = [value] + [turned(value, axis, steps) for steps in (1, 2, 3)]
    for steps, part in enumerate(came):
        start = ((me - steps) % 4,) + (0,) * value.ndim
        out = lax.dynamic_update_slice(out, part[None], start)
    return out


def normalised(stream):
    return stream * lax.rsqrt(jnp.mean(stream * stream, axis=-1, keepdims=True) + epsilon)


def first_projection(stream, shard, first):
    came = lax.ppermute(shard[8:16], "section", [(0, 1)])
    half = jnp.where(first, shard[0:8], came)
    for axis in ("y", "x", "z"):
        half = gathered_along(half, axis)
    half = half.reshape(512, XBC)
    other = swap(half)
    small = jnp.where(first, half[:, XBC - T :], other[:, XBC - T :]).reshape(64, 8, T)
    parts = normalised(stream).reshape(T, 64, 2, 8)
    parts = parts[:, :, 0, :].reshape(T, 512), parts[:, :, 1, :].reshape(T, 512)
    gain = small[:, 5, :16].astype(f32)
    gains = gain[:, :8].reshape(1, 512), gain[:, 8:].reshape(1, 512)
    low, high = [(part * g).astype(bf16) for part, g in zip(parts, gains)]
    xbc = dot(jnp.where(first, low, high), half) + dot(jnp.where(first, high, low), other)
    return xbc.astype(bf16), small


def gathered_weights(
    stream, norm_gain, w_in, conv_w, conv_b, dt_bias, a_log, d_skip, gnorm_gain, w_out
):
    def tail(v):
        return jnp.pad(v, ((0, 0), (0, T - v.shape[1])))

    first = lax.axis_index("section") == 0
    small = jnp.concatenate(
        [tail(conv_w[0]), tail(conv_b), tail(norm_gain), tail(gnorm_gain), jnp.zeros((9, T), bf16)],
        axis=0,
    )
    mixer_part = jnp.concatenate([jnp.pad(w_in[0, :, DIN:], ((0, 0), (0, EINP - EIN))), small], axis=1)
    payload = jnp.concatenate([w_out[0, 0:16], w_out[0, 16:32], w_in[0, :, :DIN], mixer_part], axis=1)
    everything = lax.all_gather(payload, ("section", "dp", "seq"), axis=0, tiled=True)
    xbc, small_0 = first_projection(stream, mixer_part, first)
    small_1 = everything[D:, payload.shape[1] - T :].reshape(64, 16, T)
    heads = jnp.pad(jnp.concatenate([dt_bias, a_log, d_skip], axis=0), ((0, 5), (0, T - HEADS)))
    other = swap(heads)
    layers = []
    for l, part in enumerate((small_0, small_1)):
        taps = jnp.stack([part[:, k, :36].reshape(CONV_CH) for k in range(KW + 1)]).astype(f32)
        layers.append(
            {
                "layer": l,
                "all": everything,
                "xbc": xbc if l == 0 else None,
                "taps": jnp.pad(taps, ((0, 8 - KW - 1), (0, 0))),
                "norm": part[:, 5, :16].reshape(1, 1024).astype(f32),
                "gnorm": part[:, 6, :32].reshape(1, DIN).astype(f32),
                "heads": jnp.where(first == (l == 0), heads, other),
            }
        )
    return layers


def shards(
    inputs, out_grad, norm_gain, w_in, conv_w, conv_b, dt_bias, a_log, d_skip, gnorm_gain, w_out
):
    section = lax.axis_index("section")
    first = section == 0
    stream = lax.dynamic_index_in_dim(inputs, section, 0, keepdims=False)[0].astype(f32)
    layers = gathered_weights(
        stream, norm_gain, w_in, conv_w, conv_b, dt_bias, a_log, d_skip, gnorm_gain, w_out
    )
    g = lax.dynamic_index_in_dim(out_grad, section, 0, keepdims=False)[0].astype(f32)
    kept = []
    for l in range(2):
        saved, stream = forward_layer(stream, layers[l])
        kept.append(saved)
    outputs = stream.astype(bf16)
    half = outputs.shape[1] // 2

    def by_features(value):
        low, high = value[:, :half], value[:, half:]
        came = swap(jnp.where(first, high, low).astype(bf16)).astype(value.dtype)
        keep = jnp.where(first, low, high)
        return jnp.where(first, jnp.stack([keep, came]), jnp.stack([came, keep]))[:, None]

    out_part = by_features(outputs)
    g, grad_in, out_1, small_1, _ = backward_layer(
        kept[1], g, layers[1], None, (out_part,)
    )
    in_1 = to_layers(in_chip(grad_in, 16)).astype(bf16)
    g, grad_in, out_0, small_0, in_1 = backward_layer(kept[0], g, layers[0], in_1)
    in_1 = to_owners(in_1)
    total_in = in_chip(grad_in, 16)
    total_in, out_0, out_1 = lax.optimization_barrier((total_in, out_0, out_1))
    in_1, small_0, small_1 = lax.optimization_barrier((in_1, small_0, small_1))
    smalls = (small_0, small_1)
    in_halves = (to_owners(to_layers(total_in).astype(bf16)), in_1)
    outs = to_owners(jnp.concatenate([out_0, out_1], axis=1))
    out_halves = (outs[0:16], outs[16:32])
    grad_w_in = own_layer(in_halves, first)[:, :EIN]
    grad_w_out = own_layer(out_halves, first)
    small = jnp.where(first, smalls[0], smalls[1]) + swap(jnp.where(first, smalls[1], smalls[0]))
    small = to_layers_in_order(to_owners(jnp.swapaxes(small.reshape(4, 16, 8, T), 0, 1)))

    return (
        out_part,
        by_features(g),
        small[5:6, :16],
        grad_w_in[None],
        small[None, 0:KW, :36],
        small[KW : KW + 1, :36],
        small[7:8, 0:HEADS],
        small[7:8, HEADS : 2 * HEADS],
        small[7:8, 2 * HEADS : 3 * HEADS],
        small[6:7, :32],
        grad_w_out[None],
    )


def solution(mesh):
    in_specs = (
        P(None, "dp", "seq", None),
        P(None, "dp", "seq", None),
        P("section", both),
        P("section", both, None),
        P("section", None, both),
        P("section", both),
        P("section", None),
        P("section", None),
        P("section", None),
        P("section", both),
        P("section", both, None),
    )
    out_specs = (
        P(None, "dp", "seq", "section"),
        P(None, "dp", "seq", "section"),
        P("section", both),
        P("section", both, None),
        P("section", None, both),
        P("section", both),
        P("section", None),
        P("section", None),
        P("section", None),
        P("section", both),
        P("section", both, None),
    )
    return jax.shard_map(shards, mesh=mesh, in_specs=in_specs, out_specs=out_specs, check_vma=False)
```

profile of v0, /device:TPU:1, one launch (start us, length us, event | category | flops | bytes accessed | tf_op | source)
XLA Modules:
  0.0 547.6 jit_solution(4312343552077383742)
XLA Ops:
  30.4 4.9 collective-permute-done.5
  37.7 4.3 collective-permute-start.8
  42.6 11.6 %collective-permute-done.7 = bf16[4,4,8,2560]{3,2,1,0:T(8,128)(2,1)S(1)} collective-permute-done((bf16[4,4,8,2560]{3,2,1,0:T(8,128)(2,1)S(1)}, bf16[4,4,8,2560]{3,2,1,0:T(8,128)(2,1)S(1)}, u32[]{:S(2)}, u32[]{:S(2)}) %collective-permute-start.7) | collective-permute-done | bytes 655392 | tf_op jit(solution)/shard_map/ppermute | solution.py:651
  54.2 22.9 %collective-permute-done.8 = bf16[4,4,8,2560]{3,2,1,0:T(8,128)(2,1)S(1)} collective-permute-done((bf16[4,4,8,2560]{3,2,1,0:T(8,128)(2,1)S(1)}, bf16[4,4,8,2560]{3,2,1,0:T(8,128)(2,1)S(1)}, u32[]{:S(2)}, u32[]{:S(2)}) %collective-permute-start.8) | collective-permute-done | bytes 655392 | tf_op jit(solution)/shard_map/ppermute | solution.py:651
  106.3 8.8 %all-to-all-start = ((bf16[16,144,128]{2,1,0:T(8,128)(2,1)}), bf16[16,144,128]{2,1,0:T(8,128)(2,1)S(1)}, u32[]{:S(2)}, u32[]{:S(2)}) async-start(bf16[16,144,128]{2,1,0:T(8,128)(2,1)} %copy-done.45), calls=%async_computation | async-start | bytes 1179648 | tf_op jit(solution)/shard_map/all_to_all | solution.py:502
  115.9 14.7 %all-to-all-done.refs_0_ = bf16[16,144,128]{2,1,0:T(8,128)(2,1)S(1)} async-done(((bf16[16,144,128]{2,1,0:T(8,128)(2,1)}), bf16[16,144,128]{2,1,0:T(8,128)(2,1)S(1)}, u32[]{:S(2)}, u32[]{:S(2)}) %all-to-all-start) | async-done | bytes 589856 | tf_op jit(solution)/shard_map/all_to_all | solution.py:502
  131.5 6.2 %all-to-all-start.1 = ((bf16[16,128,128]{2,1,0:T(8,128)(2,1)}), bf16[16,128,128]{2,1,0:T(8,128)(2,1)S(1)}, u32[]{:S(2)}, u32[]{:S(2)}) async-start(bf16[16,128,128]{2,1,0:T(8,128)(2,1)} %scan.2), calls=%async_computation.1 | async-start | bytes 1048576 | tf_op jit(solution)/shard_map/all_to_all | solution.py:511
  142.0 3.7 project.2
  147.6 3.9 finish.2
  153.2 8.3 %project.3 = (bf16[128,1024]{1,0:T(8,128)(2,1)S(1)}, bf16[128,4608]{1,0:T(8,128)(2,1)S(1)}) custom-call(f32[128,1024]{1,0:T(8,128)S(1)} %get-tuple-element.73.refs_0_.refs_6_, f32[1,1024]{1,0:T(1,128)S(1)} %reshape.376.refs_1_.refs_7_, bf16[2048,6656]{1,0:T(8,128)(2,1)} %all-gather.2.cloned.1.call-done.refs_2_.refs_7_.refs_8_.refs_1_.refs_5_), custom_call_target="tpu_custom_call" | custom-call | bytes 14000000 | tf_op jit(solution)/shard_map/project/pallas_call | solution.py:432
  162.1 3.4 collective-permute-start.13
  169.3 16.3 %all_to_all.60.refs_0_ = bf16[16,144,128]{2,1,0:T(8,128)(2,1)S(1)} all-to-all(bf16[16,144,128]{2,1,0:T(8,128)(2,1)S(1)} %get-tuple-element.79), channel_id=1, replica_groups=mesh['dp'=4,'section'=2,'seq'=16] {'seq'}, dimensions={0} | all-to-all | bytes 1179648 | tf_op jit(solution)/shard_map/all_to_all | solution.py:502
  186.5 3.6 all-to-all-start.3
  195.7 3.3 all-to-all-done.3.refs_3_.refs_5_.refs_12_
  200.2 4.0 finish.3
  207.1 16.3 %collective-permute-start.15 = (bf16[64,16,1024]{2,1,0:T(8,128)(2,1)}, bf16[64,16,1024]{2,1,0:T(8,128)(2,1)}, u32[]{:S(2)}, u32[]{:S(2)}) collective-permute-start(bf16[64,16,1024]{2,1,0:T(8,128)(2,1)} %dynamic-slice_bitcast_fusion.3), channel_id=1, source_target_pairs={{0,16},{16,0},{1,17},{17,1},{2,18},{18,2},{3,19},{19,3},{4,20},{20... | collective-permute-start | bytes 6291464 | tf_op jit(solution)/shard_map/ppermute | solution.py:447
  223.4 6.4 %top.2 = (bf16[128,2048]{1,0:T(8,128)(2,1)S(1)}, bf16[128,2048]{1,0:T(8,128)(2,1)S(1)}, f32[8,2048]{1,0:T(8,128)S(1)}, bf16[16,144,128]{2,1,0:T(8,128)(2,1)}) custom-call(bf16[128,1024]{1,0:T(8,128)(2,1)S(1)} %get-tuple-element.144.refs_0_, bf16[2048,6656]{1,0:T(8,128)(2,1)} %all-gather.2.cloned.1.call-done.refs_2_.refs_7_.refs_8_.refs_1_.refs_5_, ...), custom_call_target="tpu_custom_call" | custom-call | bytes 17500000 | tf_op jit(solution)/shard_map/top/pallas_call | solution.py:432
  231.4 4.2 all-to-all-start.4
  235.7 3.2 fusion.3
  244.0 3.4 all-to-all-done.4.refs_0_
  249.4 4.2 all-to-all-start.5
  259.2 7.6 %inner.2 = (f32[128,2048]{1,0:T(8,128)S(1)}, f32[128,256]{1,0:T(8,128)S(1)}, f32[128,128]{1,0:T(8,128)S(1)}) custom-call(f32[128,2048]{1,0:T(8,128)S(1)} %get-tuple-element.75.refs_0_.refs_4_, bf16[128,256]{1,0:T(8,128)(2,1)S(1)} %get-tuple-element.76.refs_1_.refs_5_, f32[128,128]{1,0:T(8,128)S(1)} %copy-done.42, ...), custom_call_target="tpu_custom_call" | custom-call | bytes 28000000 | tf_op jit(solution)/shard_map/inner/pallas_call | solution.py:409
  279.3 5.2 outer.2
  290.6 9.7 %bottom.2 = (bf16[128,4608]{1,0:T(8,128)(2,1)S(1)}, f32[128,1024]{1,0:T(8,128)S(1)}, f32[8,1024]{1,0:T(8,128)S(1)}) custom-call(f32[128,2304]{1,0:T(8,128)S(1)} %get-tuple-element.88.refs_0_, f32[8,2304]{1,0:T(8,128)S(1)} %collective-permute-done.16.refs_1_, f32[8,2304]{1,0:T(8,128)S(1)} %pad_convert_fusion.refs_2_, bf16[128,2048]{1,0:T(8,128)(2,1)S(1)} %copy-done.49, ...), custom_call_target="tpu_custom_call" | custom-call | bytes 21000000 | tf_op jit(solution)/shard_map/bottom/pallas_call | solution.py:432
  307.9 3.9 collective-permute-done.20
  311.8 5.6 %fusion.1 = bf16[64,8,4480]{2,1,0:T(8,128)(2,1)} fusion(bf16[64,8,4480]{2,1,0:T(8,128)(2,1)} %collective-permute-done.20, bf16[64,2,8,4480]{3,2,1,0:T(8,128)(2,1)S(1)} %bitcast.202, s32[]{:T(128)S(6)} %select_n.352), kind=kLoop, calls=%fused_computation.5 | loop fusion | flops 9175040 | bytes 13762564 | tf_op jit(solution)/shard_map/convert_element_type | solution.py:487
  317.4 3.9 dynamic-slice_bitcast_fusion.9
  325.3 5.7 %top.3 = (bf16[128,2048]{1,0:T(8,128)(2,1)S(1)}, bf16[128,2048]{1,0:T(8,128)(2,1)S(1)}, f32[8,2048]{1,0:T(8,128)S(1)}, bf16[16,144,128]{2,1,0:T(8,128)(2,1)S(1)}) custom-call(bf16[128,1024]{1,0:T(8,128)(2,1)S(1)} %convert_element_type.274.refs_0_, bf16[2048,6656]{1,0:T(8,128)(2,1)} %all-gather.2.cloned.1.call-done.refs_2_.refs_7_.refs_8_.refs_1_.refs_5_, ...), custom_call_target="tpu_custom_call" | custom-call | bytes 17500000 | tf_op jit(solution)/shard_map/top/pallas_call | solution.py:432
  332.6 8.8 %all-to-all-start.6 = ((bf16[16,144,128]{2,1,0:T(8,128)(2,1)}), bf16[16,144,128]{2,1,0:T(8,128)(2,1)S(1)}, u32[]{:S(2)}, u32[]{:S(2)}) async-start(bf16[16,144,128]{2,1,0:T(8,128)(2,1)} %copy-done.44), calls=%async_computation.6 | async-start | bytes 1179648 | tf_op jit(solution)/shard_map/all_to_all | solution.py:502
  341.5 7.6 %inner.3 = (f32[128,2048]{1,0:T(8,128)S(1)}, f32[128,256]{1,0:T(8,128)S(1)}, f32[128,128]{1,0:T(8,128)S(1)}) custom-call(f32[128,2048]{1,0:T(8,128)S(1)} %copy-done.1, bf16[128,256]{1,0:T(8,128)(2,1)S(1)} %get-tuple-element.68.refs_1_.refs_5_, f32[128,128]{1,0:T(8,128)S(1)} %copy-done.40, f32[128,128]{1,0:T(8,128)S(1)} %get-tuple-element.70.refs_3_.refs_2_.refs_6_.refs_7_, ...), custom_call_target="tpu_custom_call" | custom-call | bytes 28000000 | tf_op jit(solution)/shard_map/inner/pallas_call | solution.py:409
  352.6 5.2 all-to-all-start.7
  357.9 3.2 fusion.2
  365.5 9.0 %collective-permute-done.22 = bf16[16,8,4480]{2,1,0:T(8,128)(2,1)} collective-permute-done((bf16[16,8,4480]{2,1,0:T(8,128)(2,1)}, bf16[16,8,4480]{2,1,0:T(8,128)(2,1)}, u32[]{:S(2)}, u32[]{:S(2)}) %collective-permute-start.22) | collective-permute-done | bytes 1146912 | tf_op jit(solution)/shard_map/ppermute | solution.py:463
  375.6 3.9 fusion.10.refs_10_
  385.5 5.2 outer.3
  392.4 4.6 collective-permute-done.27
  399.2 9.7 %bottom.3 = (bf16[128,4608]{1,0:T(8,128)(2,1)S(1)}, f32[128,1024]{1,0:T(8,128)S(1)}, f32[8,1024]{1,0:T(8,128)S(1)}) custom-call(f32[128,2304]{1,0:T(8,128)S(1)} %get-tuple-element.102.refs_0_, f32[8,2304]{1,0:T(8,128)S(1)} %collective-permute-done.25.refs_1_, f32[8,2304]{1,0:T(8,128)S(1)} %pad_convert_fusion.1.refs_2_, bf16[128,2048]{1,0:T(8,128)(2,1)S(1)} %copy-done.51, ...), custom_call_target="tpu_custom_call" | custom-call | bytes 21000000 | tf_op jit(solution)/shard_map/bottom/pallas_call | solution.py:432
  421.1 8.8 %all-to-all-start.8 = ((bf16[16,8,4480]{2,1,0:T(8,128)(2,1)}), bf16[16,8,4480]{2,1,0:T(8,128)(2,1)S(1)}, u32[]{:S(2)}, u32[]{:S(2)}) async-start(bf16[16,8,4480]{2,1,0:T(8,128)(2,1)} %fusion.10.refs_10_), calls=%async_computation.8 | async-start | bytes 2293760 | tf_op jit(solution)/shard_map/all_to_all | solution.py:451
  430.9 17.2 %all-to-all-done.8 = bf16[16,8,4480]{2,1,0:T(8,128)(2,1)S(1)} async-done(((bf16[16,8,4480]{2,1,0:T(8,128)(2,1)}), bf16[16,8,4480]{2,1,0:T(8,128)(2,1)S(1)}, u32[]{:S(2)}, u32[]{:S(2)}) %all-to-all-start.8) | async-done | bytes 1146912 | tf_op jit(solution)/shard_map/all_to_all | solution.py:451
  448.3 4.8 fusion
  464.7 3.5 all-to-all-start.9
  468.3 7.6 %all-to-all-done.9 = f32[16,4,8,128]{3,1,2,0:T(4,128)S(1)} async-done(((f32[16,4,8,128]{3,1,2,0:T(4,128)}), f32[16,4,8,128]{3,1,2,0:T(4,128)S(1)}, u32[]{:S(2)}, u32[]{:S(2)}) %all-to-all-start.9) | async-done | bytes 262176 | tf_op jit(solution)/shard_map/all_to_all | solution.py:451
  477.1 3.9 all-to-all-start.11
  483.1 25.7 %collective-permute-done.36 = bf16[16,8,4480]{2,1,0:T(8,128)(2,1)} collective-permute-done((bf16[16,8,4480]{2,1,0:T(8,128)(2,1)}, bf16[16,8,4480]{2,1,0:T(8,128)(2,1)}, u32[]{:S(2)}, u32[]{:S(2)}) %collective-permute-start.36) | collective-permute-done | bytes 1146912 | tf_op jit(solution)/shard_map/ppermute | solution.py:463
  509.8 3.9 fusion.7
  513.7 3.7 all-to-all-start.10
  527.4 6.7 %all-to-all-done.10 = bf16[16,8,4480]{2,1,0:T(8,128)(2,1)S(1)} async-done(((bf16[16,8,4480]{2,1,0:T(8,128)(2,1)}), bf16[16,8,4480]{2,1,0:T(8,128)(2,1)S(1)}, u32[]{:S(2)}, u32[]{:S(2)}) %all-to-all-start.10) | async-done | bytes 1146912 | tf_op jit(solution)/shard_map/all_to_all | solution.py:451
  534.2 3.3 collective-permute-start.38
  (457 shorter events, 186.0 us)
Async XLA Ops:
  7.2 133.0 %all-gather.2.cloned.1.call-start = ((), (), s32[]{:S(2)}) async-start(), calls=%async_computation.12 | async-start | bytes 27475968 | tf_op jit(solution)/shard_map/all_gather | solution.py:707
  17.5 5.6 %collective-permute-start.1 = (bf16[8,2560]{1,0:T(8,128)(2,1)S(1)}, bf16[8,2560]{1,0:T(8,128)(2,1)S(1)}, u32[]{:S(2)}, u32[]{:S(2)}) collective-permute-start(bf16[8,2560]{1,0:T(8,128)(2,1)S(1)} %get-tuple-element.146), channel_id=1, source_target_pairs={{0,1},{1,2},{2,3},{3,0},{4,5},{5,6},{6,7},{7,4},{8,9},{9,10},{10,1... | collective-permute-start | bytes 122888 | tf_op jit(solution)/shard_map/ppermute | solution.py:659
  19.4 4.8 collective-permute-start.2
  25.0 5.4 collective-permute-start.4
  26.2 9.1 %collective-permute-start.5 = (bf16[4,8,2560]{2,1,0:T(8,128)(2,1)S(1)}, bf16[4,8,2560]{2,1,0:T(8,128)(2,1)S(1)}, u32[]{:S(2)}, u32[]{:S(2)}) collective-permute-start(bf16[4,8,2560]{2,1,0:T(8,128)(2,1)S(1)} %bitcast_dynamic-update-slice_fusion.9), channel_id=1, source_target_pairs={{0,8},{1,9},{2,10},{3,11},{4,12},{5,13},{6,14},{7,15},{8,0},{9,1},... | collective-permute-start | bytes 491528 | tf_op jit(solution)/shard_map/ppermute | solution.py:659
  28.7 7.3 %collective-permute-start.6 = (bf16[4,8,2560]{2,1,0:T(8,128)(2,1)S(1)}, bf16[4,8,2560]{2,1,0:T(8,128)(2,1)S(1)}, u32[]{:S(2)}, u32[]{:S(2)}) collective-permute-start(bf16[4,8,2560]{2,1,0:T(8,128)(2,1)S(1)} %bitcast_dynamic-update-slice_fusion.9), channel_id=1, source_target_pairs={{0,12},{1,13},{2,14},{3,15},{4,0},{5,1},{6,2},{7,3},{8,4},{9,5},{1... | collective-permute-start | bytes 491528 | tf_op jit(solution)/shard_map/ppermute | solution.py:659
  36.0 18.2 %collective-permute-start.7 = (bf16[4,4,8,2560]{3,2,1,0:T(8,128)(2,1)S(1)}, bf16[4,4,8,2560]{3,2,1,0:T(8,128)(2,1)S(1)}, u32[]{:S(2)}, u32[]{:S(2)}) collective-permute-start(bf16[4,4,8,2560]{3,2,1,0:T(8,128)(2,1)S(1)} %bitcast_dynamic-update-slice_fusion.4), channel_id=1, source_target_pairs={{0,32},{32,64},{64,96},{96,0},{1,33},{33,65},{65,97},{97,1},{2,34}... | collective-permute-start | bytes 1966088 | tf_op jit(solution)/shard_map/ppermute | solution.py:651
  37.7 39.5 %collective-permute-start.8 = (bf16[4,4,8,2560]{3,2,1,0:T(8,128)(2,1)S(1)}, bf16[4,4,8,2560]{3,2,1,0:T(8,128)(2,1)S(1)}, u32[]{:S(2)}, u32[]{:S(2)}) collective-permute-start(bf16[4,4,8,2560]{3,2,1,0:T(8,128)(2,1)S(1)} %bitcast_dynamic-update-slice_fusion.4), channel_id=1, source_target_pairs={{0,64},{32,96},{64,0},{96,32},{1,65},{33,97},{65,1},{97,33},{2,66}... | collective-permute-start | bytes 1966088 | tf_op jit(solution)/shard_map/ppermute | solution.py:651
  42.0 36.8 %collective-permute-start.9 = (bf16[4,4,8,2560]{3,2,1,0:T(8,128)(2,1)S(1)}, bf16[4,4,8,2560]{3,2,1,0:T(8,128)(2,1)S(1)}, u32[]{:S(2)}, u32[]{:S(2)}) collective-permute-start(bf16[4,4,8,2560]{3,2,1,0:T(8,128)(2,1)S(1)} %bitcast_dynamic-update-slice_fusion.4), channel_id=1, source_target_pairs={{0,96},{32,0},{64,32},{96,64},{1,97},{33,1},{65,33},{97,65},{2,98}... | collective-permute-start | bytes 1966088 | tf_op jit(solution)/shard_map/ppermute | solution.py:651
  78.8 13.6 %collective-permute-start.10 = (bf16[512,2560]{1,0:T(8,128)(2,1)S(1)}, bf16[512,2560]{1,0:T(8,128)(2,1)}, u32[]{:S(2)}, u32[]{:S(2)}) collective-permute-start(bf16[512,2560]{1,0:T(8,128)(2,1)S(1)} %bitcast.211), channel_id=1, source_target_pairs={{0,16},{16,0},{1,17},{17,1},{2,18},{18,2},{3,19},{19,3},{4,20},{20... | collective-permute-start | bytes 7864328 | tf_op jit(solution)/shard_map/ppermute | solution.py:447
  81.1 10.7 %collective-permute-start.12 = (f32[8,128]{1,0:T(8,128)S(1)}, f32[8,128]{1,0:T(8,128)S(1)}, u32[]{:S(2)}, u32[]{:S(2)}) collective-permute-start(f32[8,128]{1,0:T(8,128)S(1)} %select_maximum_fusion), channel_id=1, source_target_pairs={{0,16},{16,0},{1,17},{17,1},{2,18},{18,2},{3,19},{19,3},{4,20},{20... | collective-permute-start | bytes 12296 | tf_op jit(solution)/shard_map/ppermute | solution.py:447
  99.4 4.6 collective-permute-start.11
  106.3 24.2 %all-to-all-start = ((bf16[16,144,128]{2,1,0:T(8,128)(2,1)}), bf16[16,144,128]{2,1,0:T(8,128)(2,1)S(1)}, u32[]{:S(2)}, u32[]{:S(2)}) async-start(bf16[16,144,128]{2,1,0:T(8,128)(2,1)} %copy-done.45), calls=%async_computation | async-start | bytes 1179648 | tf_op jit(solution)/shard_map/all_to_all | solution.py:502
  131.5 16.1 %all-to-all-start.1 = ((bf16[16,128,128]{2,1,0:T(8,128)(2,1)}), bf16[16,128,128]{2,1,0:T(8,128)(2,1)S(1)}, u32[]{:S(2)}, u32[]{:S(2)}) async-start(bf16[16,128,128]{2,1,0:T(8,128)(2,1)} %scan.2), calls=%async_computation.1 | async-start | bytes 1048576 | tf_op jit(solution)/shard_map/all_to_all | solution.py:511
  162.1 4.8 collective-permute-start.13
  186.5 12.5 %all-to-all-start.3 = ((bf16[16,128,128]{2,1,0:T(8,128)(2,1)}), bf16[16,128,128]{2,1,0:T(8,128)(2,1)S(1)}, u32[]{:S(2)}, u32[]{:S(2)}) async-start(bf16[16,128,128]{2,1,0:T(8,128)(2,1)} %scan.3), calls=%async_computation.3 | async-start | bytes 1048576 | tf_op jit(solution)/shard_map/all_to_all | solution.py:511
  207.1 28.6 %collective-permute-start.15 = (bf16[64,16,1024]{2,1,0:T(8,128)(2,1)}, bf16[64,16,1024]{2,1,0:T(8,128)(2,1)}, u32[]{:S(2)}, u32[]{:S(2)}) collective-permute-start(bf16[64,16,1024]{2,1,0:T(8,128)(2,1)} %dynamic-slice_bitcast_fusion.3), channel_id=1, source_target_pairs={{0,16},{16,0},{1,17},{17,1},{2,18},{18,2},{3,19},{19,3},{4,20},{20... | collective-permute-start | bytes 6291464 | tf_op jit(solution)/shard_map/ppermute | solution.py:447
  231.4 16.0 %all-to-all-start.4 = ((bf16[16,144,128]{2,1,0:T(8,128)(2,1)}), bf16[16,144,128]{2,1,0:T(8,128)(2,1)}, u32[]{:S(2)}, u32[]{:S(2)}) async-start(bf16[16,144,128]{2,1,0:T(8,128)(2,1)} %get-tuple-element.86), calls=%async_computation.4 | async-start | bytes 1179648 | tf_op jit(solution)/shard_map/all_to_all | solution.py:502
  240.1 46.3 %collective-permute-start.19 = (bf16[16,16,1024]{2,1,0:T(8,128)(2,1)}, bf16[16,16,1024]{2,1,0:T(8,128)(2,1)}, u32[]{:S(2)}, u32[]{:S(2)}) collective-permute-start(bf16[16,16,1024]{2,1,0:T(8,128)(2,1)} %get-tuple-element.157), channel_id=1, source_target_pairs={{0,64},{32,96},{64,0},{96,32},{1,65},{33,97},{65,1},{97,33},{2,66}... | collective-permute-start | bytes 1572872 | tf_op jit(solution)/shard_map/ppermute | solution.py:463
  242.6 43.9 %collective-permute-start.18 = (bf16[16,16,1024]{2,1,0:T(8,128)(2,1)}, bf16[16,16,1024]{2,1,0:T(8,128)(2,1)}, u32[]{:S(2)}, u32[]{:S(2)}) collective-permute-start(bf16[16,16,1024]{2,1,0:T(8,128)(2,1)} %get-tuple-element.158), channel_id=1, source_target_pairs={{0,96},{32,0},{64,32},{96,64},{1,97},{33,1},{65,33},{97,65},{2,98}... | collective-permute-start | bytes 1572872 | tf_op jit(solution)/shard_map/ppermute | solution.py:463
  243.8 42.7 %collective-permute-start.17 = (bf16[16,16,1024]{2,1,0:T(8,128)(2,1)}, bf16[16,16,1024]{2,1,0:T(8,128)(2,1)}, u32[]{:S(2)}, u32[]{:S(2)}) collective-permute-start(bf16[16,16,1024]{2,1,0:T(8,128)(2,1)} %get-tuple-element.156), channel_id=1, source_target_pairs={{0,32},{32,64},{64,96},{96,0},{1,33},{33,65},{65,97},{97,1},{2,34}... | collective-permute-start | bytes 1572872 | tf_op jit(solution)/shard_map/ppermute | solution.py:463
  249.4 20.5 %all-to-all-start.5 = ((bf16[16,128,128]{2,1,0:T(8,128)(2,1)}), bf16[16,128,128]{2,1,0:T(8,128)(2,1)}, u32[]{:S(2)}, u32[]{:S(2)}) async-start(bf16[16,128,128]{2,1,0:T(8,128)(2,1)} %copy-done.30), calls=%async_computation.5 | async-start | bytes 1048576 | tf_op jit(solution)/shard_map/all_to_all | solution.py:511
  254.7 14.4 %collective-permute-start.14 = (bf16[128,512]{1,0:T(8,128)(2,1)S(1)}, bf16[128,512]{1,0:T(8,128)(2,1)S(1)}, u32[]{:S(2)}, u32[]{:S(2)}) collective-permute-start(bf16[128,512]{1,0:T(8,128)(2,1)S(1)} %get-tuple-element.166), channel_id=1, source_target_pairs={{0,16},{16,0},{1,17},{17,1},{2,18},{18,2},{3,19},{19,3},{4,20},{20... | collective-permute-start | bytes 393224 | tf_op jit(solution)/shard_map/ppermute | solution.py:447
  284.6 5.9 %collective-permute-start.16 = (f32[8,2304]{1,0:T(8,128)S(1)}, f32[8,2304]{1,0:T(8,128)S(1)}, u32[]{:S(2)}, u32[]{:S(2)}) collective-permute-start(f32[8,2304]{1,0:T(8,128)S(1)} %slice.230), channel_id=1, source_target_pairs={{1,0},{2,1},{3,2},{4,3},{5,4},{6,5},{7,6},{8,7},{9,8},{10,9},{11,1... | collective-permute-start | bytes 221192 | tf_op jit(solution)/shard_map/ppermute | solution.py:620
  303.5 8.3 %collective-permute-start.20 = (bf16[64,8,4480]{2,1,0:T(8,128)(2,1)S(1)}, bf16[64,8,4480]{2,1,0:T(8,128)(2,1)}, u32[]{:S(2)}, u32[]{:S(2)}) collective-permute-start(bf16[64,8,4480]{2,1,0:T(8,128)(2,1)S(1)} %dynamic-slice_bitcast_fusion.1), channel_id=1, source_target_pairs={{0,16},{16,0},{1,17},{17,1},{2,18},{18,2},{3,19},{19,3},{4,20},{20... | collective-permute-start | bytes 13762568 | tf_op jit(solution)/shard_map/ppermute | solution.py:447
  307.3 50.6 %collective-permute-start.24 = (bf16[64,16,1024]{2,1,0:T(8,128)(2,1)}, bf16[64,16,1024]{2,1,0:T(8,128)(2,1)}, u32[]{:S(2)}, u32[]{:S(2)}) collective-permute-start(bf16[64,16,1024]{2,1,0:T(8,128)(2,1)} %dynamic-slice_bitcast_fusion.2), channel_id=1, source_target_pairs={{0,16},{16,0},{1,17},{17,1},{2,18},{18,2},{3,19},{19,3},{4,20},{20... | collective-permute-start | bytes 6291464 | tf_op jit(solution)/shard_map/ppermute | solution.py:447
  321.4 44.1 %collective-permute-start.23 = (bf16[16,8,4480]{2,1,0:T(8,128)(2,1)}, bf16[16,8,4480]{2,1,0:T(8,128)(2,1)}, u32[]{:S(2)}, u32[]{:S(2)}) collective-permute-start(bf16[16,8,4480]{2,1,0:T(8,128)(2,1)} %get-tuple-element.151), channel_id=1, source_target_pairs={{0,64},{32,96},{64,0},{96,32},{1,65},{33,97},{65,1},{97,33},{2,66}... | collective-permute-start | bytes 3440648 | tf_op jit(solution)/shard_map/ppermute | solution.py:463
  323.8 50.6 %collective-permute-start.22 = (bf16[16,8,4480]{2,1,0:T(8,128)(2,1)}, bf16[16,8,4480]{2,1,0:T(8,128)(2,1)}, u32[]{:S(2)}, u32[]{:S(2)}) collective-permute-start(bf16[16,8,4480]{2,1,0:T(8,128)(2,1)} %get-tuple-element.152), channel_id=1, source_target_pairs={{0,96},{32,0},{64,32},{96,64},{1,97},{33,1},{65,33},{97,65},{2,98}... | collective-permute-start | bytes 3440648 | tf_op jit(solution)/shard_map/ppermute | solution.py:463
  325.0 50.6 %collective-permute-start.21 = (bf16[16,8,4480]{2,1,0:T(8,128)(2,1)}, bf16[16,8,4480]{2,1,0:T(8,128)(2,1)}, u32[]{:S(2)}, u32[]{:S(2)}) collective-permute-start(bf16[16,8,4480]{2,1,0:T(8,128)(2,1)} %get-tuple-element.150), channel_id=1, source_target_pairs={{0,32},{32,64},{64,96},{96,0},{1,33},{33,65},{65,97},{97,1},{2,34}... | collective-permute-start | bytes 3440648 | tf_op jit(solution)/shard_map/ppermute | solution.py:463
  332.6 19.0 %all-to-all-start.6 = ((bf16[16,144,128]{2,1,0:T(8,128)(2,1)}), bf16[16,144,128]{2,1,0:T(8,128)(2,1)S(1)}, u32[]{:S(2)}, u32[]{:S(2)}) async-start(bf16[16,144,128]{2,1,0:T(8,128)(2,1)} %copy-done.44), calls=%async_computation.6 | async-start | bytes 1179648 | tf_op jit(solution)/shard_map/all_to_all | solution.py:502
  352.6 26.9 %all-to-all-start.7 = ((bf16[16,128,128]{2,1,0:T(8,128)(2,1)}), bf16[16,128,128]{2,1,0:T(8,128)(2,1)}, u32[]{:S(2)}, u32[]{:S(2)}) async-start(bf16[16,128,128]{2,1,0:T(8,128)(2,1)} %scan_back.3), calls=%async_computation.7 | async-start | bytes 1048576 | tf_op jit(solution)/shard_map/all_to_all | solution.py:511
  362.3 30.1 %collective-permute-start.28 = (bf16[16,16,1024]{2,1,0:T(8,128)(2,1)}, bf16[16,16,1024]{2,1,0:T(8,128)(2,1)}, u32[]{:S(2)}, u32[]{:S(2)}) collective-permute-start(bf16[16,16,1024]{2,1,0:T(8,128)(2,1)} %get-tuple-element.154), channel_id=1, source_target_pairs={{0,64},{32,96},{64,0},{96,32},{1,65},{33,97},{65,1},{97,33},{2,66}... | collective-permute-start | bytes 1572872 | tf_op jit(solution)/shard_map/ppermute | solution.py:463
  363.4 33.6 %collective-permute-start.27 = (bf16[16,16,1024]{2,1,0:T(8,128)(2,1)}, bf16[16,16,1024]{2,1,0:T(8,128)(2,1)}, u32[]{:S(2)}, u32[]{:S(2)}) collective-permute-start(bf16[16,16,1024]{2,1,0:T(8,128)(2,1)} %get-tuple-element.155), channel_id=1, source_target_pairs={{0,96},{32,0},{64,32},{96,64},{1,97},{33,1},{65,33},{97,65},{2,98}... | collective-permute-start | bytes 1572872 | tf_op jit(solution)/shard_map/ppermute | solution.py:463
  365.5 32.0 %collective-permute-start.26 = (bf16[16,16,1024]{2,1,0:T(8,128)(2,1)}, bf16[16,16,1024]{2,1,0:T(8,128)(2,1)}, u32[]{:S(2)}, u32[]{:S(2)}) collective-permute-start(bf16[16,16,1024]{2,1,0:T(8,128)(2,1)} %get-tuple-element.153), channel_id=1, source_target_pairs={{0,32},{32,64},{64,96},{96,0},{1,33},{33,65},{65,97},{97,1},{2,34}... | collective-permute-start | bytes 1572872 | tf_op jit(solution)/shard_map/ppermute | solution.py:463
  390.7 8.4 %collective-permute-start.25 = (f32[8,2304]{1,0:T(8,128)S(1)}, f32[8,2304]{1,0:T(8,128)S(1)}, u32[]{:S(2)}, u32[]{:S(2)}) collective-permute-start(f32[8,2304]{1,0:T(8,128)S(1)} %slice.232), channel_id=1, source_target_pairs={{1,0},{2,1},{3,2},{4,3},{5,4},{6,5},{7,6},{8,7},{9,8},{10,9},{11,1... | collective-permute-start | bytes 221192 | tf_op jit(solution)/shard_map/ppermute | solution.py:620
  416.8 31.5 %collective-permute-start.34 = (bf16[64,8,4480]{2,1,0:T(8,128)(2,1)}, bf16[64,8,4480]{2,1,0:T(8,128)(2,1)}, u32[]{:S(2)}, u32[]{:S(2)}) collective-permute-start(bf16[64,8,4480]{2,1,0:T(8,128)(2,1)} %dynamic-slice_bitcast_fusion), channel_id=1, source_target_pairs={{0,16},{16,0},{1,17},{17,1},{2,18},{18,2},{3,19},{19,3},{4,20},{20... | collective-permute-start | bytes 13762568 | tf_op jit(solution)/shard_map/ppermute | solution.py:447
  421.1 27.0 %all-to-all-start.8 = ((bf16[16,8,4480]{2,1,0:T(8,128)(2,1)}), bf16[16,8,4480]{2,1,0:T(8,128)(2,1)S(1)}, u32[]{:S(2)}, u32[]{:S(2)}) async-start(bf16[16,8,4480]{2,1,0:T(8,128)(2,1)} %fusion.10.refs_10_), calls=%async_computation.8 | async-start | bytes 2293760 | tf_op jit(solution)/shard_map/all_to_all | solution.py:451
  456.2 26.9 %collective-permute-start.37 = (bf16[16,8,4480]{2,1,0:T(8,128)(2,1)}, bf16[16,8,4480]{2,1,0:T(8,128)(2,1)}, u32[]{:S(2)}, u32[]{:S(2)}) collective-permute-start(bf16[16,8,4480]{2,1,0:T(8,128)(2,1)} %get-tuple-element.148), channel_id=1, source_target_pairs={{0,64},{32,96},{64,0},{96,32},{1,65},{33,97},{65,1},{97,33},{2,66}... | collective-permute-start | bytes 3440648 | tf_op jit(solution)/shard_map/ppermute | solution.py:463
  458.5 50.3 %collective-permute-start.36 = (bf16[16,8,4480]{2,1,0:T(8,128)(2,1)}, bf16[16,8,4480]{2,1,0:T(8,128)(2,1)}, u32[]{:S(2)}, u32[]{:S(2)}) collective-permute-start(bf16[16,8,4480]{2,1,0:T(8,128)(2,1)} %get-tuple-element.149), channel_id=1, source_target_pairs={{0,96},{32,0},{64,32},{96,64},{1,97},{33,1},{65,33},{97,65},{2,98}... | collective-permute-start | bytes 3440648 | tf_op jit(solution)/shard_map/ppermute | solution.py:463
  459.7 50.1 %collective-permute-start.35 = (bf16[16,8,4480]{2,1,0:T(8,128)(2,1)}, bf16[16,8,4480]{2,1,0:T(8,128)(2,1)}, u32[]{:S(2)}, u32[]{:S(2)}) collective-permute-start(bf16[16,8,4480]{2,1,0:T(8,128)(2,1)} %get-tuple-element.147), channel_id=1, source_target_pairs={{0,32},{32,64},{64,96},{96,0},{1,33},{33,65},{65,97},{97,1},{2,34}... | collective-permute-start | bytes 3440648 | tf_op jit(solution)/shard_map/ppermute | solution.py:463
  462.7 5.6 %collective-permute-start.29 = (bf16[128,512]{1,0:T(8,128)(2,1)S(1)}, bf16[128,512]{1,0:T(8,128)(2,1)S(1)}, u32[]{:S(2)}, u32[]{:S(2)}) collective-permute-start(bf16[128,512]{1,0:T(8,128)(2,1)S(1)} %select_convert_fusion), channel_id=1, source_target_pairs={{0,16},{16,0},{1,17},{17,1},{2,18},{18,2},{3,19},{19,3},{4,20},{20... | collective-permute-start | bytes 393224 | tf_op jit(solution)/shard_map/ppermute | solution.py:447
  464.7 11.3 %all-to-all-start.9 = ((f32[16,4,8,128]{3,1,2,0:T(4,128)}), f32[16,4,8,128]{3,1,2,0:T(4,128)S(1)}, u32[]{:S(2)}, u32[]{:S(2)}) async-start(f32[16,4,8,128]{3,1,2,0:T(4,128)} %bitcast.192), calls=%async_computation.9 | async-start | bytes 524288 | tf_op jit(solution)/shard_map/all_to_all | solution.py:451
  477.1 36.6 %all-to-all-start.11 = ((bf16[16,32,1024]{2,1,0:T(8,128)(2,1)}), bf16[16,32,1024]{2,1,0:T(8,128)(2,1)S(1)}, u32[]{:S(2)}, u32[]{:S(2)}) async-start(bf16[16,32,1024]{2,1,0:T(8,128)(2,1)} %pad_maximum_fusion), calls=%async_computation.11 | async-start | bytes 2097152 | tf_op jit(solution)/shard_map/all_to_all | solution.py:451
  513.7 20.3 %all-to-all-start.10 = ((bf16[16,8,4480]{2,1,0:T(8,128)(2,1)}), bf16[16,8,4480]{2,1,0:T(8,128)(2,1)S(1)}, u32[]{:S(2)}, u32[]{:S(2)}) async-start(bf16[16,8,4480]{2,1,0:T(8,128)(2,1)} %fusion.7), calls=%async_computation.10 | async-start | bytes 2293760 | tf_op jit(solution)/shard_map/all_to_all | solution.py:451
  517.5 4.1 collective-permute-start.33
  520.4 4.0 collective-permute-start.31
  525.3 13.9 %collective-permute-start.39 = (f32[16,1024]{1,0:T(8,128)S(1)}, f32[16,1024]{1,0:T(8,128)S(1)}, u32[]{:S(2)}, u32[]{:S(2)}) collective-permute-start(f32[16,1024]{1,0:T(8,128)S(1)} %get-tuple-element.168), channel_id=1, source_target_pairs={{0,16},{16,0},{1,17},{17,1},{2,18},{18,2},{3,19},{19,3},{4,20},{20... | collective-permute-start | bytes 196616 | tf_op jit(solution)/shard_map/ppermute | solution.py:447
  534.2 5.6 %collective-permute-start.38 = (f32[8,4480]{1,0:T(8,128)S(1)}, f32[8,4480]{1,0:T(8,128)S(1)}, u32[]{:S(2)}, u32[]{:S(2)}) collective-permute-start(f32[8,4480]{1,0:T(8,128)S(1)} %get-tuple-element.164), channel_id=1, source_target_pairs={{0,16},{16,0},{1,17},{17,1},{2,18},{18,2},{3,19},{19,3},{4,20},{20... | collective-permute-start | bytes 430088 | tf_op jit(solution)/shard_map/ppermute | solution.py:447
  (110 other events, 941.6 us)
Sparse Core Ops, SparseCore 0:
  14.2 119.9 all-gather.1
where the time goes:
time: 554 us; the launch traced here: 548 us
  waiting for transfers between devices  157 us (28%)
  starting transfers between devices  136 us (25%)
  Pallas kernels  87.1 us (16%)
  local copies, waits for them, and re-layouts  80.4 us (15%)
  other arithmetic  40.9 us (7%)
  blocking collectives  16.3 us (3%)
  between operations  16.2 us (3%)
  matrix products  13.8 us (2%)
    pallas_call x8, Pallas kernels, call_tiled(): pl.pallas_call(dropping(kernel, len(args), len(after)), grid=(steps,), in...  51.4 us
    ppermute x12, waiting for transfers between devices, to_layers(): lax.ppermute(piece(steps), 'dp', [(i, (i + steps) % 4) for i in range(4)])  44 us
    unnamed x230, local copies, waits for them, and re-layouts  41.7 us
    ppermute x3, waiting for transfers between devices, turned(): return lax.ppermute(value, 'dp', [(i, (i + steps) % 4) for i in range(4)])  36.1 us
    pallas_call x12, Pallas kernels, call(): pl.pallas_call(dropping(kernel, len(args), len(after)), out_shape=[jax.Sh...  35.7 us
    all_to_all x4, waiting for transfers between devices, to_owners(): came = lax.all_to_all(value, 'seq', split_axis=0, concat_axis=0, tiled=True)  31.5 us
    ppermute x11, starting transfers between devices, swap(): return lax.ppermute(value, 'section', [(0, 1), (1, 0)])  30.6 us
    all_to_all x3, starting transfers between devices, exchange(): lax.all_to_all(payload, 'seq', split_axis=0, concat_axis=0, tiled=True)  21.8 us
  transfers between devices with their start and end apart: 52, of which 30 were waited for; matrix products, arithmetic and copies ran while one was open for 13% of the time, Pallas kernels for 9%

commit v1 on v0

--- a/solution.py
+++ b/solution.py
@@ -573,15 +573,19 @@
         [(2, T, D), (T, DIN), (T, DIN)],
         "top",
         5,
+        () if earlier is None else earlier[1:],
     )
     grad_out = dot_tn(normed, upstream_low).astype(bf16)
     leaving = exchange(payload, True)
     out_total = in_chip(grad_out, 32)
     grad_out = to_layers(out_total).astype(bf16)
-    ordered = (grad_out,)
+    ordered, grad_gate = (grad_out,), None
     if earlier is not None:
-        leaving, earlier = lax.optimization_barrier((leaving, earlier))
-        ordered = (grad_out, earlier)
+        leaving, came = lax.optimization_barrier((leaving, earlier[0]))
+        came = to_owners(came)
+        total_gate = in_chip(dot_tn(hidden, d_gate).astype(bf16), 16)
+        ordered = (grad_out, came, total_gate)
+        grad_gate = to_layers(total_gate).astype(bf16)
     d_scaled, d_bc, d_cum = call(
         inner_kernel,
         [((T, DIN), f32), ((T, 2 * STATE), f32), ((T, T), f32)],
@@ -629,9 +633,12 @@
         6,
         ordered,
     )
-    grad_in = dot_tn(hidden, d_projected[:, :EINP]).astype(bf16)
+    start = 0 if earlier is None else DIN
+    grad_in = dot_tn(hidden, d_projected[:, start:EINP]).astype(bf16)
     small = pack_small(d_norm[0], d_taps, d_gain[0], d_heads)
-    return result, grad_in, grad_out, small, earlier
+    if earlier is None:
+        return result, grad_in, grad_out, small
+    return result, grad_gate, grad_in, grad_out, small, came
 
 
 def pack_small(grad_norm, d_taps, d_gain, d_heads):
@@ -677,13 +684,15 @@
 def first_projection(stream, shard, first):
     came = lax.ppermute(shard[8:16], "section", [(0, 1)])
     half = jnp.where(first, shard[0:8], came)
-    for axis in ("y", "x", "z"):
+    for axis in ("y", "x"):
         half = gathered_along(half, axis)
+    parts = normalised(stream).reshape(T, 64, 2, 8)
+    parts = parts[:, :, 0, :].reshape(T, 512), parts[:, :, 1, :].reshape(T, 512)
+    half, parts = lax.optimization_barrier((half, parts))
+    half = gathered_along(half, "z")
     half = half.reshape(512, XBC)
     other = swap(half)
     small = jnp.where(first, half[:, XBC - T :], other[:, XBC - T :]).reshape(64, 8, T)
-    parts = normalised(stream).reshape(T, 64, 2, 8)
-    parts = parts[:, :, 0, :].reshape(T, 512), parts[:, :, 1, :].reshape(T, 512)
     gain = small[:, 5, :16].astype(f32)
     gains = gain[:, :8].reshape(1, 512), gain[:, 8:].reshape(1, 512)
     low, high = [(part * g).astype(bf16) for part, g in zip(parts, gains)]
@@ -750,19 +759,20 @@
         return jnp.where(first, jnp.stack([keep, came]), jnp.stack([came, keep]))[:, None]
 
     out_part = by_features(outputs)
-    g, grad_in, out_1, small_1, _ = backward_layer(
-        kept[1], g, layers[1], None, (out_part,)
-    )
+    g, grad_in, out_1, small_1 = backward_layer(kept[1], g, layers[1], None, (out_part,))
+    out_1 = to_owners(out_1)
     in_1 = to_layers(in_chip(grad_in, 16)).astype(bf16)
-    g, grad_in, out_0, small_0, in_1 = backward_layer(kept[0], g, layers[0], in_1)
-    in_1 = to_owners(in_1)
+    g, grad_gate, grad_in, out_0, small_0, in_1 = backward_layer(
+        kept[0], g, layers[0], (in_1, out_1)
+    )
     total_in = in_chip(grad_in, 16)
-    total_in, out_0, out_1 = lax.optimization_barrier((total_in, out_0, out_1))
-    in_1, small_0, small_1 = lax.optimization_barrier((in_1, small_0, small_1))
+    total_in, grad_gate, small_0, small_1 = lax.optimization_barrier(
+        (total_in, grad_gate, small_0, small_1)
+    )
     smalls = (small_0, small_1)
-    in_halves = (to_owners(to_layers(total_in).astype(bf16)), in_1)
-    outs = to_owners(jnp.concatenate([out_0, out_1], axis=1))
-    out_halves = (outs[0:16], outs[16:32])
+    grad_in = to_owners(to_layers(total_in).astype(bf16))
+    in_halves = (jnp.concatenate([to_owners(grad_gate), grad_in], axis=-1), in_1)
+    out_halves = (to_owners(out_0), out_1)
     grad_w_in = own_layer(in_halves, first)[:, :EIN]
     grad_w_out = own_layer(out_halves, first)
     small = jnp.where(first, smalls[0], smalls[1]) + swap(jnp.where(first, smalls[1], smalls[0]))

time: 554 us -> 597 us (1.078)
  local copies, waits for them, and re-layouts: 80.4 us -> 102 us
  starting transfers between devices: 136 us -> 146 us
  other arithmetic: 40.9 us -> 48.7 us
    all_to_all x4 -> x6, starting transfers between devices: 19.9 us -> 41.1 us  [to_owners(): came = lax.all_to_all(value, 'seq', split_axis=0, concat_axis=0, tiled=True)]
    unnamed x230 -> x258, local copies, waits for them, and re-layouts: 41.7 us -> 61.7 us
    ppermute x12 -> x15, waiting for transfers between devices: 44 us -> 53.5 us  [to_layers(): lax.ppermute(piece(steps), 'dp', [(i, (i + steps) % 4) for i in range(4)])]
    ppermute x11 -> x12, starting transfers between devices: 30.6 us -> 21.3 us  [swap(): return lax.ppermute(value, 'section', [(0, 1), (1, 0)])]
    ppermute x12 -> x15, starting transfers between devices: 14.7 us -> 16.4 us  [to_layers(): lax.ppermute(piece(steps), 'dp', [(i, (i + steps) % 4) for i in range(4)])]
    convert_element_type x4 -> x5, other arithmetic: 16.9 us -> 17.3 us  [in_chip(): total = (mine.astype(f32) + swap(theirs).astype(f32)).astype(bf16)]
    all_to_all x4 -> x6, waiting for transfers between devices: 31.5 us -> 31.3 us  [to_owners(): came = lax.all_to_all(value, 'seq', split_axis=0, concat_axis=0, tiled=True)]
  transfers between devices with their start and end apart: 52 -> 58, of which waited for: 30 -> 27; matrix products, arithmetic and copies ran while one was open for 13% -> 16% of each run, Pallas kernels for 9% -> 10%
where the time goes in v1:
time: 597 us; the launch traced here: 585 us
  waiting for transfers between devices  157 us (26%)
  starting transfers between devices  146 us (24%)
  local copies, waits for them, and re-layouts  102 us (17%)
  Pallas kernels  86 us (14%)
  other arithmetic  48.7 us (8%)
  between operations  16.4 us (3%)
  blocking collectives  16.3 us (3%)
  matrix products  12.8 us (2%)
    unnamed x258, local copies, waits for them, and re-layouts  61.7 us
    ppermute x15, waiting for transfers between devices, to_layers(): lax.ppermute(piece(steps), 'dp', [(i, (i + steps) % 4) for i in range(4)])  53.5 us
    pallas_call x8, Pallas kernels, call_tiled(): pl.pallas_call(dropping(kernel, len(args), len(after)), grid=(steps,), in...  52.1 us
    all_to_all x6, starting transfers between devices, to_owners(): came = lax.all_to_all(value, 'seq', split_axis=0, concat_axis=0, tiled=True)  41.1 us
    pallas_call x12, Pallas kernels, call(): pl.pallas_call(dropping(kernel, len(args), len(after)), out_shape=[jax.Sh...  33.9 us
    ppermute x3, waiting for transfers between devices, turned(): return lax.ppermute(value, 'dp', [(i, (i + steps) % 4) for i in range(4)])  31.7 us
    all_to_all x6, waiting for transfers between devices, to_owners(): came = lax.all_to_all(value, 'seq', split_axis=0, concat_axis=0, tiled=True)  31.3 us
    all_to_all x4, starting transfers between devices, exchange(): lax.all_to_all(entering, 'seq', split_axis=0, concat_axis=0, tiled=True)  21.3 us
  transfers between devices with their start and end apart: 58, of which 27 were waited for; matrix products, arithmetic and copies ran while one was open for 16% of the time, Pallas kernels for 10%

profile of v1, /device:TPU:1, one launch (start us, length us, event | category | flops | bytes accessed | tf_op | source)
XLA Modules:
  0.0 585.2 jit_solution(17051265207512138963)
XLA Ops:
  31.0 5.1 collective-permute-done.5
  38.1 3.6 collective-permute-start.8
  45.0 8.0 %collective-permute-done.7 = bf16[4,4,8,2560]{3,2,1,0:T(8,128)(2,1)S(1)} collective-permute-done((bf16[4,4,8,2560]{3,2,1,0:T(8,128)(2,1)S(1)}, bf16[4,4,8,2560]{3,2,1,0:T(8,128)(2,1)S(1)}, u32[]{:S(2)}, u32[]{:S(2)}) %collective-permute-start.7) | collective-permute-done | bytes 655392 | tf_op jit(solution)/shard_map/ppermute | solution.py:658
  53.9 19.1 %collective-permute-done.8 = bf16[4,4,8,2560]{3,2,1,0:T(8,128)(2,1)S(1)} collective-permute-done((bf16[4,4,8,2560]{3,2,1,0:T(8,128)(2,1)S(1)}, bf16[4,4,8,2560]{3,2,1,0:T(8,128)(2,1)S(1)}, u32[]{:S(2)}, u32[]{:S(2)}) %collective-permute-start.8) | collective-permute-done | bytes 655392 | tf_op jit(solution)/shard_map/ppermute | solution.py:658
  73.9 4.6 collective-permute-done.9
  79.4 3.1 collective-permute-start.10
  82.6 4.3 collective-permute-done.12
  102.2 8.2 %all-to-all-start = ((bf16[16,144,128]{2,1,0:T(8,128)(2,1)}), bf16[16,144,128]{2,1,0:T(8,128)(2,1)S(1)}, u32[]{:S(2)}, u32[]{:S(2)}) async-start(bf16[16,144,128]{2,1,0:T(8,128)(2,1)} %copy-done.65), calls=%async_computation | async-start | bytes 1179648 | tf_op jit(solution)/shard_map/all_to_all | solution.py:502
  112.2 13.9 %all-to-all-done.refs_0_ = bf16[16,144,128]{2,1,0:T(8,128)(2,1)S(1)} async-done(((bf16[16,144,128]{2,1,0:T(8,128)(2,1)}), bf16[16,144,128]{2,1,0:T(8,128)(2,1)S(1)}, u32[]{:S(2)}, u32[]{:S(2)}) %all-to-all-start) | async-done | bytes 589856 | tf_op jit(solution)/shard_map/all_to_all | solution.py:502
  127.0 6.5 %all-to-all-start.1 = ((bf16[16,128,128]{2,1,0:T(8,128)(2,1)}), bf16[16,128,128]{2,1,0:T(8,128)(2,1)S(1)}, u32[]{:S(2)}, u32[]{:S(2)}) async-start(bf16[16,128,128]{2,1,0:T(8,128)(2,1)} %scan.2), calls=%async_computation.1 | async-start | bytes 1048576 | tf_op jit(solution)/shard_map/all_to_all | solution.py:511
  138.7 3.7 project.2
  143.5 3.9 finish.2
  149.2 8.3 %project.3 = (bf16[128,1024]{1,0:T(8,128)(2,1)S(1)}, bf16[128,4608]{1,0:T(8,128)(2,1)S(1)}) custom-call(f32[128,1024]{1,0:T(8,128)S(1)} %get-tuple-element.77.refs_0_.refs_6_, f32[1,1024]{1,0:T(1,128)S(1)} %copy-done.85, bf16[2048,6656]{1,0:T(8,128)(2,1)} %all-gather.2.cloned.1.call-done.refs_2_.refs_7_.refs_8_.refs_1_.refs_5_), custom_call_target="tpu_custom_call" | custom-call | bytes 14000000 | tf_op jit(solution)/shard_map/project/pallas_call | solution.py:432
  158.2 3.3 collective-permute-start.13
  165.3 16.3 %all_to_all.70.refs_0_ = bf16[16,144,128]{2,1,0:T(8,128)(2,1)S(1)} all-to-all(bf16[16,144,128]{2,1,0:T(8,128)(2,1)S(1)} %get-tuple-element.83), channel_id=1, replica_groups=mesh['dp'=4,'section'=2,'seq'=16] {'seq'}, dimensions={0} | all-to-all | bytes 1179648 | tf_op jit(solution)/shard_map/all_to_all | solution.py:502
  182.5 3.6 all-to-all-start.3
  196.3 4.0 finish.3
  203.2 6.6 %collective-permute-start.15 = (bf16[64,16,1024]{2,1,0:T(8,128)(2,1)}, bf16[64,16,1024]{2,1,0:T(8,128)(2,1)}, u32[]{:S(2)}, u32[]{:S(2)}) collective-permute-start(bf16[64,16,1024]{2,1,0:T(8,128)(2,1)} %dynamic-slice_bitcast_fusion.4), channel_id=1, source_target_pairs={{0,16},{16,0},{1,17},{17,1},{2,18},{18,2},{3,19},{19,3},{4,20},{20... | collective-permute-start | bytes 6291464 | tf_op jit(solution)/shard_map/ppermute | solution.py:447
  209.8 6.4 %top.2 = (bf16[128,2048]{1,0:T(8,128)(2,1)S(1)}, bf16[128,2048]{1,0:T(8,128)(2,1)S(1)}, f32[8,2048]{1,0:T(8,128)S(1)}, bf16[16,144,128]{2,1,0:T(8,128)(2,1)}) custom-call(bf16[128,1024]{1,0:T(8,128)(2,1)S(1)} %get-tuple-element.146.refs_0_, bf16[2048,6656]{1,0:T(8,128)(2,1)} %all-gather.2.cloned.1.call-done.refs_2_.refs_7_.refs_8_.refs_1_.refs_5_, ...), custom_call_target="tpu_custom_call" | custom-call | bytes 17500000 | tf_op jit(solution)/shard_map/top/pallas_call | solution.py:432
  217.9 4.2 all-to-all-start.4
  222.2 3.2 fusion.4
  235.2 4.3 all-to-all-start.5
  247.4 7.6 %inner.2 = (f32[128,2048]{1,0:T(8,128)S(1)}, f32[128,256]{1,0:T(8,128)S(1)}, f32[128,128]{1,0:T(8,128)S(1)}) custom-call(f32[128,2048]{1,0:T(8,128)S(1)} %get-tuple-element.79.refs_0_.refs_4_, bf16[128,256]{1,0:T(8,128)(2,1)S(1)} %copy-done.40, f32[128,128]{1,0:T(8,128)S(1)} %copy-done.61, f32[128,128]{1,0:T(8,128)S(1)} %copy-done.43, ...), custom_call_target="tpu_custom_call" | custom-call | bytes 28000000 | tf_op jit(solution)/shard_map/inner/pallas_call | solution.py:409
  269.4 5.2 outer.2
  280.7 9.7 %bottom.2 = (bf16[128,4608]{1,0:T(8,128)(2,1)S(1)}, f32[128,1024]{1,0:T(8,128)S(1)}, f32[8,1024]{1,0:T(8,128)S(1)}) custom-call(f32[128,2304]{1,0:T(8,128)S(1)} %get-tuple-element.92.refs_0_, f32[8,2304]{1,0:T(8,128)S(1)} %collective-permute-done.16.refs_1_, f32[8,2304]{1,0:T(8,128)S(1)} %copy-done.50, bf16[128,2048]{1,0:T(8,128)(2,1)S(1)} %copy-done.69, ...), custom_call_target="tpu_custom_call" | custom-call | bytes 21000000 | tf_op jit(solution)/shard_map/bottom/pallas_call | solution.py:432
  305.6 8.6 %all-to-all-start.6 = ((bf16[16,16,1024]{2,1,0:T(8,128)(2,1)}), bf16[16,16,1024]{2,1,0:T(8,128)(2,1)S(1)}, u32[]{:S(2)}, u32[]{:S(2)}) async-start(bf16[16,16,1024]{2,1,0:T(8,128)(2,1)} %fusion.21.refs_9_), calls=%async_computation.6 | async-start | bytes 1048576 | tf_op jit(solution)/shard_map/all_to_all | solution.py:451
  314.9 9.7 %all-to-all-done.6 = bf16[16,16,1024]{2,1,0:T(8,128)(2,1)S(1)} async-done(((bf16[16,16,1024]{2,1,0:T(8,128)(2,1)}), bf16[16,16,1024]{2,1,0:T(8,128)(2,1)S(1)}, u32[]{:S(2)}, u32[]{:S(2)}) %all-to-all-start.6) | async-done | bytes 524320 | tf_op jit(solution)/shard_map/all_to_all | solution.py:451
  324.7 6.4 %top.3 = (bf16[128,2048]{1,0:T(8,128)(2,1)S(1)}, bf16[128,2048]{1,0:T(8,128)(2,1)S(1)}, f32[8,2048]{1,0:T(8,128)S(1)}, bf16[16,144,128]{2,1,0:T(8,128)(2,1)}) custom-call(bf16[128,1024]{1,0:T(8,128)(2,1)S(1)} %convert_element_type.305.refs_0_, bf16[2048,6656]{1,0:T(8,128)(2,1)} %all-gather.2.cloned.1.call-done.refs_2_.refs_7_.refs_8_.refs_1_.refs_5_, ...), custom_call_target="tpu_custom_call" | custom-call | bytes 17500000 | tf_op jit(solution)/shard_map/top/pallas_call | solution.py:432
  333.4 3.7 all-to-all-start.7
  337.1 3.2 fusion.3
  344.9 4.8 fusion
  358.8 9.3 %collective-permute-done.27 = bf16[16,16,1024]{2,1,0:T(8,128)(2,1)S(1)} collective-permute-done((bf16[16,16,1024]{2,1,0:T(8,128)(2,1)S(1)}, bf16[16,16,1024]{2,1,0:T(8,128)(2,1)S(1)}, u32[]{:S(2)}, u32[]{:S(2)}) %collective-permute-start.27) | collective-permute-done | bytes 524320 | tf_op jit(solution)/shard_map/ppermute | solution.py:463
  371.2 6.9 %all-to-all-start.8 = ((bf16[16,128,128]{2,1,0:T(8,128)(2,1)}), bf16[16,128,128]{2,1,0:T(8,128)(2,1)S(1)}, u32[]{:S(2)}, u32[]{:S(2)}) async-start(bf16[16,128,128]{2,1,0:T(8,128)(2,1)} %copy-done.36), calls=%async_computation.8 | async-start | bytes 1048576 | tf_op jit(solution)/shard_map/all_to_all | solution.py:511
  378.2 39.4 %collective-permute-done.26 = bf16[16,16,1024]{2,1,0:T(8,128)(2,1)} collective-permute-done((bf16[16,16,1024]{2,1,0:T(8,128)(2,1)}, bf16[16,16,1024]{2,1,0:T(8,128)(2,1)}, u32[]{:S(2)}, u32[]{:S(2)}) %collective-permute-start.26) | collective-permute-done | bytes 524320 | tf_op jit(solution)/shard_map/ppermute | solution.py:463
  420.1 6.7 %all-to-all-start.13 = ((bf16[16,16,1024]{2,1,0:T(8,128)(2,1)}), bf16[16,16,1024]{2,1,0:T(8,128)(2,1)}, u32[]{:S(2)}, u32[]{:S(2)}) async-start(bf16[16,16,1024]{2,1,0:T(8,128)(2,1)} %fusion.18.refs_9_), calls=%async_computation.13 | async-start | bytes 1048576 | tf_op jit(solution)/shard_map/all_to_all | solution.py:451
  426.9 3.9 fusion.8
  430.8 6.5 %all-to-all-done.13 = bf16[16,16,1024]{2,1,0:T(8,128)(2,1)} async-done(((bf16[16,16,1024]{2,1,0:T(8,128)(2,1)}), bf16[16,16,1024]{2,1,0:T(8,128)(2,1)}, u32[]{:S(2)}, u32[]{:S(2)}) %all-to-all-start.13) | async-done | bytes 524320 | tf_op jit(solution)/shard_map/all_to_all | solution.py:451
  437.2 4.6 all-to-all-start.9
  447.7 7.6 %inner.3 = (f32[128,2048]{1,0:T(8,128)S(1)}, f32[128,256]{1,0:T(8,128)S(1)}, f32[128,128]{1,0:T(8,128)S(1)}) custom-call(f32[128,2048]{1,0:T(8,128)S(1)} %copy-done.3, bf16[128,256]{1,0:T(8,128)(2,1)S(1)} %get-tuple-element.72.refs_1_.refs_5_, f32[128,128]{1,0:T(8,128)S(1)} %copy-done.58, f32[128,128]{1,0:T(8,128)S(1)} %get-tuple-element.74.refs_3_.refs_2_.refs_6_.refs_7_, ...), custom_call_target="tpu_custom_call" | custom-call | bytes 28000000 | tf_op jit(solution)/shard_map/inner/pallas_call | solution.py:409
  466.0 4.1 outer.3
  485.0 9.7 %bottom.3 = (bf16[128,4608]{1,0:T(8,128)(2,1)S(1)}, f32[128,1024]{1,0:T(8,128)S(1)}, f32[8,1024]{1,0:T(8,128)S(1)}) custom-call(f32[128,2304]{1,0:T(8,128)S(1)} %copy-done.46, f32[8,2304]{1,0:T(8,128)S(1)} %collective-permute-done.25.refs_1_, f32[8,2304]{1,0:T(8,128)S(1)} %copy-done.53, bf16[128,2048]{1,0:T(8,128)(2,1)S(1)} %copy-done.23, ...), custom_call_target="tpu_custom_call" | custom-call | bytes 21000000 | tf_op jit(solution)/shard_map/bottom/pallas_call | solution.py:432
  498.5 3.7 collective-permute-start.31
  514.6 3.1 fusion.1
  523.5 8.8 %all-to-all-start.10 = ((f32[16,4,8,128]{3,1,2,0:T(4,128)}), f32[16,4,8,128]{3,1,2,0:T(4,128)S(1)}, u32[]{:S(2)}, u32[]{:S(2)}) async-start(f32[16,4,8,128]{3,1,2,0:T(4,128)} %bitcast.207), calls=%async_computation.10 | async-start | bytes 524288 | tf_op jit(solution)/shard_map/all_to_all | solution.py:451
  534.1 5.7 all-to-all-done.10
  539.8 3.7 all-to-all-start.11
  553.9 8.8 %all-to-all-start.12 = ((bf16[16,8,2432]{2,1,0:T(8,128)(2,1)}), bf16[16,8,2432]{2,1,0:T(8,128)(2,1)S(1)}, u32[]{:S(2)}, u32[]{:S(2)}) async-start(bf16[16,8,2432]{2,1,0:T(8,128)(2,1)} %fusion.11), calls=%async_computation.12 | async-start | bytes 1245184 | tf_op jit(solution)/shard_map/all_to_all | solution.py:451
  564.4 9.5 %all-to-all-done.12 = bf16[16,8,2432]{2,1,0:T(8,128)(2,1)S(1)} async-done(((bf16[16,8,2432]{2,1,0:T(8,128)(2,1)}), bf16[16,8,2432]{2,1,0:T(8,128)(2,1)S(1)}, u32[]{:S(2)}, u32[]{:S(2)}) %all-to-all-start.12) | async-done | bytes 622624 | tf_op jit(solution)/shard_map/all_to_all | solution.py:451
  (503 shorter events, 223.6 us)
Async XLA Ops:
  7.2 129.0 %all-gather.2.cloned.1.call-start = ((), (), s32[]{:S(2)}) async-start(), calls=%async_computation.14 | async-start | bytes 27475968 | tf_op jit(solution)/shard_map/all_gather | solution.py:716
  17.6 5.9 %collective-permute-start.1 = (bf16[8,2560]{1,0:T(8,128)(2,1)S(1)}, bf16[8,2560]{1,0:T(8,128)(2,1)S(1)}, u32[]{:S(2)}, u32[]{:S(2)}) collective-permute-start(bf16[8,2560]{1,0:T(8,128)(2,1)S(1)} %get-tuple-element.148), channel_id=1, source_target_pairs={{0,1},{1,2},{2,3},{3,0},{4,5},{5,6},{6,7},{7,4},{8,9},{9,10},{10,1... | collective-permute-start | bytes 122888 | tf_op jit(solution)/shard_map/ppermute | solution.py:666
  26.8 9.3 %collective-permute-start.5 = (bf16[4,8,2560]{2,1,0:T(8,128)(2,1)S(1)}, bf16[4,8,2560]{2,1,0:T(8,128)(2,1)S(1)}, u32[]{:S(2)}, u32[]{:S(2)}) collective-permute-start(bf16[4,8,2560]{2,1,0:T(8,128)(2,1)S(1)} %bitcast_dynamic-update-slice_fusion.9), channel_id=1, source_target_pairs={{0,8},{1,9},{2,10},{3,11},{4,12},{5,13},{6,14},{7,15},{8,0},{9,1},... | collective-permute-start | bytes 491528 | tf_op jit(solution)/shard_map/ppermute | solution.py:666
  29.3 6.9 %collective-permute-start.6 = (bf16[4,8,2560]{2,1,0:T(8,128)(2,1)S(1)}, bf16[4,8,2560]{2,1,0:T(8,128)(2,1)S(1)}, u32[]{:S(2)}, u32[]{:S(2)}) collective-permute-start(bf16[4,8,2560]{2,1,0:T(8,128)(2,1)S(1)} %bitcast_dynamic-update-slice_fusion.9), channel_id=1, source_target_pairs={{0,12},{1,13},{2,14},{3,15},{4,0},{5,1},{6,2},{7,3},{8,4},{9,5},{1... | collective-permute-start | bytes 491528 | tf_op jit(solution)/shard_map/ppermute | solution.py:666
  36.2 16.8 %collective-permute-start.7 = (bf16[4,4,8,2560]{3,2,1,0:T(8,128)(2,1)S(1)}, bf16[4,4,8,2560]{3,2,1,0:T(8,128)(2,1)S(1)}, u32[]{:S(2)}, u32[]{:S(2)}) collective-permute-start(bf16[4,4,8,2560]{3,2,1,0:T(8,128)(2,1)S(1)} %bitcast_dynamic-update-slice_fusion.4), channel_id=1, source_target_pairs={{0,32},{32,64},{64,96},{96,0},{1,33},{33,65},{65,97},{97,1},{2,34}... | collective-permute-start | bytes 1966088 | tf_op jit(solution)/shard_map/ppermute | solution.py:658
  38.1 34.9 %collective-permute-start.8 = (bf16[4,4,8,2560]{3,2,1,0:T(8,128)(2,1)S(1)}, bf16[4,4,8,2560]{3,2,1,0:T(8,128)(2,1)S(1)}, u32[]{:S(2)}, u32[]{:S(2)}) collective-permute-start(bf16[4,4,8,2560]{3,2,1,0:T(8,128)(2,1)S(1)} %bitcast_dynamic-update-slice_fusion.4), channel_id=1, source_target_pairs={{0,64},{32,96},{64,0},{96,32},{1,65},{33,97},{65,1},{97,33},{2,66}... | collective-permute-start | bytes 1966088 | tf_op jit(solution)/shard_map/ppermute | solution.py:658
  41.7 36.8 %collective-permute-start.9 = (bf16[4,4,8,2560]{3,2,1,0:T(8,128)(2,1)S(1)}, bf16[4,4,8,2560]{3,2,1,0:T(8,128)(2,1)S(1)}, u32[]{:S(2)}, u32[]{:S(2)}) collective-permute-start(bf16[4,4,8,2560]{3,2,1,0:T(8,128)(2,1)S(1)} %bitcast_dynamic-update-slice_fusion.4), channel_id=1, source_target_pairs={{0,96},{32,0},{64,32},{96,64},{1,97},{33,1},{65,33},{97,65},{2,98}... | collective-permute-start | bytes 1966088 | tf_op jit(solution)/shard_map/ppermute | solution.py:658
  79.4 8.0 %collective-permute-start.10 = (bf16[512,2560]{1,0:T(8,128)(2,1)}, bf16[512,2560]{1,0:T(8,128)(2,1)}, u32[]{:S(2)}, u32[]{:S(2)}) collective-permute-start(bf16[512,2560]{1,0:T(8,128)(2,1)} %bitcast.18), channel_id=1, source_target_pairs={{0,16},{16,0},{1,17},{17,1},{2,18},{18,2},{3,19},{19,3},{4,20},{20... | collective-permute-start | bytes 7864328 | tf_op jit(solution)/shard_map/ppermute | solution.py:447
  93.5 5.7 collective-permute-start.11
  102.2 23.8 %all-to-all-start = ((bf16[16,144,128]{2,1,0:T(8,128)(2,1)}), bf16[16,144,128]{2,1,0:T(8,128)(2,1)S(1)}, u32[]{:S(2)}, u32[]{:S(2)}) async-start(bf16[16,144,128]{2,1,0:T(8,128)(2,1)} %copy-done.65), calls=%async_computation | async-start | bytes 1179648 | tf_op jit(solution)/shard_map/all_to_all | solution.py:502
  127.0 16.5 %all-to-all-start.1 = ((bf16[16,128,128]{2,1,0:T(8,128)(2,1)}), bf16[16,128,128]{2,1,0:T(8,128)(2,1)S(1)}, u32[]{:S(2)}, u32[]{:S(2)}) async-start(bf16[16,128,128]{2,1,0:T(8,128)(2,1)} %scan.2), calls=%async_computation.1 | async-start | bytes 1048576 | tf_op jit(solution)/shard_map/all_to_all | solution.py:511
  182.5 12.5 %all-to-all-start.3 = ((bf16[16,128,128]{2,1,0:T(8,128)(2,1)}), bf16[16,128,128]{2,1,0:T(8,128)(2,1)S(1)}, u32[]{:S(2)}, u32[]{:S(2)}) async-start(bf16[16,128,128]{2,1,0:T(8,128)(2,1)} %scan.3), calls=%async_computation.3 | async-start | bytes 1048576 | tf_op jit(solution)/shard_map/all_to_all | solution.py:511
  203.2 18.9 %collective-permute-start.15 = (bf16[64,16,1024]{2,1,0:T(8,128)(2,1)}, bf16[64,16,1024]{2,1,0:T(8,128)(2,1)}, u32[]{:S(2)}, u32[]{:S(2)}) collective-permute-start(bf16[64,16,1024]{2,1,0:T(8,128)(2,1)} %dynamic-slice_bitcast_fusion.4), channel_id=1, source_target_pairs={{0,16},{16,0},{1,17},{17,1},{2,18},{18,2},{3,19},{19,3},{4,20},{20... | collective-permute-start | bytes 6291464 | tf_op jit(solution)/shard_map/ppermute | solution.py:447
  217.9 15.4 %all-to-all-start.4 = ((bf16[16,144,128]{2,1,0:T(8,128)(2,1)}), bf16[16,144,128]{2,1,0:T(8,128)(2,1)}, u32[]{:S(2)}, u32[]{:S(2)}) async-start(bf16[16,144,128]{2,1,0:T(8,128)(2,1)} %get-tuple-element.90), calls=%async_computation.4 | async-start | bytes 1179648 | tf_op jit(solution)/shard_map/all_to_all | solution.py:502
  226.6 49.8 %collective-permute-start.19 = (bf16[16,16,1024]{2,1,0:T(8,128)(2,1)}, bf16[16,16,1024]{2,1,0:T(8,128)(2,1)}, u32[]{:S(2)}, u32[]{:S(2)}) collective-permute-start(bf16[16,16,1024]{2,1,0:T(8,128)(2,1)} %get-tuple-element.162), channel_id=1, source_target_pairs={{0,64},{32,96},{64,0},{96,32},{1,65},{33,97},{65,1},{97,33},{2,66}... | collective-permute-start | bytes 1572872 | tf_op jit(solution)/shard_map/ppermute | solution.py:463
  229.0 47.4 %collective-permute-start.18 = (bf16[16,16,1024]{2,1,0:T(8,128)(2,1)}, bf16[16,16,1024]{2,1,0:T(8,128)(2,1)}, u32[]{:S(2)}, u32[]{:S(2)}) collective-permute-start(bf16[16,16,1024]{2,1,0:T(8,128)(2,1)} %get-tuple-element.163), channel_id=1, source_target_pairs={{0,96},{32,0},{64,32},{96,64},{1,97},{33,1},{65,33},{97,65},{2,98}... | collective-permute-start | bytes 1572872 | tf_op jit(solution)/shard_map/ppermute | solution.py:463
  229.9 46.5 %collective-permute-start.17 = (bf16[16,16,1024]{2,1,0:T(8,128)(2,1)}, bf16[16,16,1024]{2,1,0:T(8,128)(2,1)}, u32[]{:S(2)}, u32[]{:S(2)}) collective-permute-start(bf16[16,16,1024]{2,1,0:T(8,128)(2,1)} %get-tuple-element.161), channel_id=1, source_target_pairs={{0,32},{32,64},{64,96},{96,0},{1,33},{33,65},{65,97},{97,1},{2,34}... | collective-permute-start | bytes 1572872 | tf_op jit(solution)/shard_map/ppermute | solution.py:463
  235.2 22.8 %all-to-all-start.5 = ((bf16[16,128,128]{2,1,0:T(8,128)(2,1)}), bf16[16,128,128]{2,1,0:T(8,128)(2,1)}, u32[]{:S(2)}, u32[]{:S(2)}) async-start(bf16[16,128,128]{2,1,0:T(8,128)(2,1)} %copy-done.35), calls=%async_computation.5 | async-start | bytes 1048576 | tf_op jit(solution)/shard_map/all_to_all | solution.py:511
  240.7 16.6 %collective-permute-start.14 = (bf16[128,512]{1,0:T(8,128)(2,1)S(1)}, bf16[128,512]{1,0:T(8,128)(2,1)S(1)}, u32[]{:S(2)}, u32[]{:S(2)}) collective-permute-start(bf16[128,512]{1,0:T(8,128)(2,1)S(1)} %get-tuple-element.171), channel_id=1, source_target_pairs={{0,16},{16,0},{1,17},{17,1},{2,18},{18,2},{3,19},{19,3},{4,20},{20... | collective-permute-start | bytes 393224 | tf_op jit(solution)/shard_map/ppermute | solution.py:447
  274.7 5.9 %collective-permute-start.16 = (f32[8,2304]{1,0:T(8,128)S(1)}, f32[8,2304]{1,0:T(8,128)S(1)}, u32[]{:S(2)}, u32[]{:S(2)}) collective-permute-start(f32[8,2304]{1,0:T(8,128)S(1)} %slice.224), channel_id=1, source_target_pairs={{1,0},{2,1},{3,2},{4,3},{5,4},{6,5},{7,6},{8,7},{9,8},{10,9},{11,1... | collective-permute-start | bytes 221192 | tf_op jit(solution)/shard_map/ppermute | solution.py:624
  298.3 46.7 %collective-permute-start.20 = (bf16[64,8,4480]{2,1,0:T(8,128)(2,1)}, bf16[64,8,4480]{2,1,0:T(8,128)(2,1)}, u32[]{:S(2)}, u32[]{:S(2)}) collective-permute-start(bf16[64,8,4480]{2,1,0:T(8,128)(2,1)} %dynamic-slice_bitcast_fusion), channel_id=1, source_target_pairs={{0,16},{16,0},{1,17},{17,1},{2,18},{18,2},{3,19},{19,3},{4,20},{20... | collective-permute-start | bytes 13762568 | tf_op jit(solution)/shard_map/ppermute | solution.py:447
  303.9 33.2 %collective-permute-start.24 = (bf16[64,16,1024]{2,1,0:T(8,128)(2,1)}, bf16[64,16,1024]{2,1,0:T(8,128)(2,1)}, u32[]{:S(2)}, u32[]{:S(2)}) collective-permute-start(bf16[64,16,1024]{2,1,0:T(8,128)(2,1)} %dynamic-slice_bitcast_fusion.3), channel_id=1, source_target_pairs={{0,16},{16,0},{1,17},{17,1},{2,18},{18,2},{3,19},{19,3},{4,20},{20... | collective-permute-start | bytes 6291464 | tf_op jit(solution)/shard_map/ppermute | solution.py:447
  305.6 19.0 %all-to-all-start.6 = ((bf16[16,16,1024]{2,1,0:T(8,128)(2,1)}), bf16[16,16,1024]{2,1,0:T(8,128)(2,1)S(1)}, u32[]{:S(2)}, u32[]{:S(2)}) async-start(bf16[16,16,1024]{2,1,0:T(8,128)(2,1)} %fusion.21.refs_9_), calls=%async_computation.6 | async-start | bytes 1048576 | tf_op jit(solution)/shard_map/all_to_all | solution.py:451
  333.4 37.0 %all-to-all-start.7 = ((bf16[16,144,128]{2,1,0:T(8,128)(2,1)}), bf16[16,144,128]{2,1,0:T(8,128)(2,1)S(1)}, u32[]{:S(2)}, u32[]{:S(2)}) async-start(bf16[16,144,128]{2,1,0:T(8,128)(2,1)} %get-tuple-element.101), calls=%async_computation.7 | async-start | bytes 1179648 | tf_op jit(solution)/shard_map/all_to_all | solution.py:502
  341.3 15.8 %collective-permute-start.28 = (bf16[16,16,1024]{2,1,0:T(8,128)(2,1)S(1)}, bf16[16,16,1024]{2,1,0:T(8,128)(2,1)S(1)}, u32[]{:S(2)}, u32[]{:S(2)}) collective-permute-start(bf16[16,16,1024]{2,1,0:T(8,128)(2,1)S(1)} %get-tuple-element.159), channel_id=1, source_target_pairs={{0,64},{32,96},{64,0},{96,32},{1,65},{33,97},{65,1},{97,33},{2,66}... | collective-permute-start | bytes 1572872 | tf_op jit(solution)/shard_map/ppermute | solution.py:463
  343.6 24.5 %collective-permute-start.27 = (bf16[16,16,1024]{2,1,0:T(8,128)(2,1)S(1)}, bf16[16,16,1024]{2,1,0:T(8,128)(2,1)S(1)}, u32[]{:S(2)}, u32[]{:S(2)}) collective-permute-start(bf16[16,16,1024]{2,1,0:T(8,128)(2,1)S(1)} %get-tuple-element.160), channel_id=1, source_target_pairs={{0,96},{32,0},{64,32},{96,64},{1,97},{33,1},{65,33},{97,65},{2,98}... | collective-permute-start | bytes 1572872 | tf_op jit(solution)/shard_map/ppermute | solution.py:463
  352.8 74.0 %collective-permute-start.23 = (bf16[16,8,4480]{2,1,0:T(8,128)(2,1)}, bf16[16,8,4480]{2,1,0:T(8,128)(2,1)}, u32[]{:S(2)}, u32[]{:S(2)}) collective-permute-start(bf16[16,8,4480]{2,1,0:T(8,128)(2,1)} %get-tuple-element.150), channel_id=1, source_target_pairs={{0,64},{32,96},{64,0},{96,32},{1,65},{33,97},{65,1},{97,33},{2,66}... | collective-permute-start | bytes 3440648 | tf_op jit(solution)/shard_map/ppermute | solution.py:463
  353.6 73.2 %collective-permute-start.22 = (bf16[16,8,4480]{2,1,0:T(8,128)(2,1)}, bf16[16,8,4480]{2,1,0:T(8,128)(2,1)}, u32[]{:S(2)}, u32[]{:S(2)}) collective-permute-start(bf16[16,8,4480]{2,1,0:T(8,128)(2,1)} %get-tuple-element.151), channel_id=1, source_target_pairs={{0,96},{32,0},{64,32},{96,64},{1,97},{33,1},{65,33},{97,65},{2,98}... | collective-permute-start | bytes 3440648 | tf_op jit(solution)/shard_map/ppermute | solution.py:463
  355.7 71.1 %collective-permute-start.21 = (bf16[16,8,4480]{2,1,0:T(8,128)(2,1)}, bf16[16,8,4480]{2,1,0:T(8,128)(2,1)}, u32[]{:S(2)}, u32[]{:S(2)}) collective-permute-start(bf16[16,8,4480]{2,1,0:T(8,128)(2,1)} %get-tuple-element.149), channel_id=1, source_target_pairs={{0,32},{32,64},{64,96},{96,0},{1,33},{33,65},{65,97},{97,1},{2,34}... | collective-permute-start | bytes 3440648 | tf_op jit(solution)/shard_map/ppermute | solution.py:463
  357.1 60.6 %collective-permute-start.26 = (bf16[16,16,1024]{2,1,0:T(8,128)(2,1)}, bf16[16,16,1024]{2,1,0:T(8,128)(2,1)}, u32[]{:S(2)}, u32[]{:S(2)}) collective-permute-start(bf16[16,16,1024]{2,1,0:T(8,128)(2,1)} %get-tuple-element.158), channel_id=1, source_target_pairs={{0,32},{32,64},{64,96},{96,0},{1,33},{33,65},{65,97},{97,1},{2,34}... | collective-permute-start | bytes 1572872 | tf_op jit(solution)/shard_map/ppermute | solution.py:463
  368.1 87.2 %collective-permute-start.29 = (bf16[64,8,2048]{2,1,0:T(8,128)(2,1)}, bf16[64,8,2048]{2,1,0:T(8,128)(2,1)}, u32[]{:S(2)}, u32[]{:S(2)}) collective-permute-start(bf16[64,8,2048]{2,1,0:T(8,128)(2,1)} %dynamic-slice_bitcast_fusion.2), channel_id=1, source_target_pairs={{0,16},{16,0},{1,17},{17,1},{2,18},{18,2},{3,19},{19,3},{4,20},{20... | collective-permute-start | bytes 6291464 | tf_op jit(solution)/shard_map/ppermute | solution.py:447
  371.2 48.9 %all-to-all-start.8 = ((bf16[16,128,128]{2,1,0:T(8,128)(2,1)}), bf16[16,128,128]{2,1,0:T(8,128)(2,1)S(1)}, u32[]{:S(2)}, u32[]{:S(2)}) async-start(bf16[16,128,128]{2,1,0:T(8,128)(2,1)} %copy-done.36), calls=%async_computation.8 | async-start | bytes 1048576 | tf_op jit(solution)/shard_map/all_to_all | solution.py:511
  420.1 17.1 %all-to-all-start.13 = ((bf16[16,16,1024]{2,1,0:T(8,128)(2,1)}), bf16[16,16,1024]{2,1,0:T(8,128)(2,1)}, u32[]{:S(2)}, u32[]{:S(2)}) async-start(bf16[16,16,1024]{2,1,0:T(8,128)(2,1)} %fusion.18.refs_9_), calls=%async_computation.13 | async-start | bytes 1048576 | tf_op jit(solution)/shard_map/all_to_all | solution.py:451
  437.2 36.1 %all-to-all-start.9 = ((bf16[16,8,4480]{2,1,0:T(8,128)(2,1)}), bf16[16,8,4480]{2,1,0:T(8,128)(2,1)}, u32[]{:S(2)}, u32[]{:S(2)}) async-start(bf16[16,8,4480]{2,1,0:T(8,128)(2,1)} %fusion.8), calls=%async_computation.9 | async-start | bytes 2293760 | tf_op jit(solution)/shard_map/all_to_all | solution.py:451
  460.9 41.4 %collective-permute-start.34 = (bf16[16,8,2048]{2,1,0:T(8,128)(2,1)}, bf16[16,8,2048]{2,1,0:T(8,128)(2,1)}, u32[]{:S(2)}, u32[]{:S(2)}) collective-permute-start(bf16[16,8,2048]{2,1,0:T(8,128)(2,1)} %get-tuple-element.156), channel_id=1, source_target_pairs={{0,64},{32,96},{64,0},{96,32},{1,65},{33,97},{65,1},{97,33},{2,66}... | collective-permute-start | bytes 1572872 | tf_op jit(solution)/shard_map/ppermute | solution.py:463
  462.8 39.6 %collective-permute-start.33 = (bf16[16,8,2048]{2,1,0:T(8,128)(2,1)}, bf16[16,8,2048]{2,1,0:T(8,128)(2,1)}, u32[]{:S(2)}, u32[]{:S(2)}) collective-permute-start(bf16[16,8,2048]{2,1,0:T(8,128)(2,1)} %get-tuple-element.157), channel_id=1, source_target_pairs={{0,96},{32,0},{64,32},{96,64},{1,97},{33,1},{65,33},{97,65},{2,98}... | collective-permute-start | bytes 1572872 | tf_op jit(solution)/shard_map/ppermute | solution.py:463
  462.8 39.6 %collective-permute-start.32 = (bf16[16,8,2048]{2,1,0:T(8,128)(2,1)}, bf16[16,8,2048]{2,1,0:T(8,128)(2,1)}, u32[]{:S(2)}, u32[]{:S(2)}) collective-permute-start(bf16[16,8,2048]{2,1,0:T(8,128)(2,1)} %get-tuple-element.155), channel_id=1, source_target_pairs={{0,32},{32,64},{64,96},{96,0},{1,33},{33,65},{65,97},{97,1},{2,34}... | collective-permute-start | bytes 1572872 | tf_op jit(solution)/shard_map/ppermute | solution.py:463
  498.5 16.1 %collective-permute-start.31 = (bf16[64,8,2432]{2,1,0:T(8,128)(2,1)S(1)}, bf16[64,8,2432]{2,1,0:T(8,128)(2,1)}, u32[]{:S(2)}, u32[]{:S(2)}) collective-permute-start(bf16[64,8,2432]{2,1,0:T(8,128)(2,1)S(1)} %dynamic-slice_bitcast_fusion.1), channel_id=1, source_target_pairs={{0,16},{16,0},{1,17},{17,1},{2,18},{18,2},{3,19},{19,3},{4,20},{20... | collective-permute-start | bytes 7471112 | tf_op jit(solution)/shard_map/ppermute | solution.py:447
  511.7 20.6 %collective-permute-start.30 = (bf16[128,512]{1,0:T(8,128)(2,1)}, bf16[128,512]{1,0:T(8,128)(2,1)}, u32[]{:S(2)}, u32[]{:S(2)}) collective-permute-start(bf16[128,512]{1,0:T(8,128)(2,1)} %select_convert_fusion), channel_id=1, source_target_pairs={{0,16},{16,0},{1,17},{17,1},{2,18},{18,2},{3,19},{19,3},{4,20},{20... | collective-permute-start | bytes 393224 | tf_op jit(solution)/shard_map/ppermute | solution.py:447
  520.1 25.8 %collective-permute-start.41 = (bf16[16,8,2432]{2,1,0:T(8,128)(2,1)}, bf16[16,8,2432]{2,1,0:T(8,128)(2,1)}, u32[]{:S(2)}, u32[]{:S(2)}) collective-permute-start(bf16[16,8,2432]{2,1,0:T(8,128)(2,1)} %get-tuple-element.153), channel_id=1, source_target_pairs={{0,64},{32,96},{64,0},{96,32},{1,65},{33,97},{65,1},{97,33},{2,66}... | collective-permute-start | bytes 1867784 | tf_op jit(solution)/shard_map/ppermute | solution.py:463
  521.2 27.9 %collective-permute-start.40 = (bf16[16,8,2432]{2,1,0:T(8,128)(2,1)}, bf16[16,8,2432]{2,1,0:T(8,128)(2,1)}, u32[]{:S(2)}, u32[]{:S(2)}) collective-permute-start(bf16[16,8,2432]{2,1,0:T(8,128)(2,1)} %get-tuple-element.154), channel_id=1, source_target_pairs={{0,96},{32,0},{64,32},{96,64},{1,97},{33,1},{65,33},{97,65},{2,98}... | collective-permute-start | bytes 1867784 | tf_op jit(solution)/shard_map/ppermute | solution.py:463
  522.2 29.0 %collective-permute-start.39 = (bf16[16,8,2432]{2,1,0:T(8,128)(2,1)}, bf16[16,8,2432]{2,1,0:T(8,128)(2,1)}, u32[]{:S(2)}, u32[]{:S(2)}) collective-permute-start(bf16[16,8,2432]{2,1,0:T(8,128)(2,1)} %get-tuple-element.152), channel_id=1, source_target_pairs={{0,32},{32,64},{64,96},{96,0},{1,33},{33,65},{65,97},{97,1},{2,34}... | collective-permute-start | bytes 1867784 | tf_op jit(solution)/shard_map/ppermute | solution.py:463
  523.5 16.2 %all-to-all-start.10 = ((f32[16,4,8,128]{3,1,2,0:T(4,128)}), f32[16,4,8,128]{3,1,2,0:T(4,128)S(1)}, u32[]{:S(2)}, u32[]{:S(2)}) async-start(f32[16,4,8,128]{3,1,2,0:T(4,128)} %bitcast.207), calls=%async_computation.10 | async-start | bytes 524288 | tf_op jit(solution)/shard_map/all_to_all | solution.py:451
  539.8 14.1 %all-to-all-start.11 = ((bf16[16,8,2048]{2,1,0:T(8,128)(2,1)}), bf16[16,8,2048]{2,1,0:T(8,128)(2,1)S(1)}, u32[]{:S(2)}, u32[]{:S(2)}) async-start(bf16[16,8,2048]{2,1,0:T(8,128)(2,1)} %fusion.15), calls=%async_computation.11 | async-start | bytes 1048576 | tf_op jit(solution)/shard_map/all_to_all | solution.py:451
  543.5 19.2 %collective-permute-start.38 = (f32[8,128]{1,0:T(8,128)S(1)}, f32[8,128]{1,0:T(8,128)S(1)}, u32[]{:S(2)}, u32[]{:S(2)}) collective-permute-start(f32[8,128]{1,0:T(8,128)S(1)} %bitcast.245), channel_id=1, source_target_pairs={{0,96},{32,0},{64,32},{96,64},{1,97},{33,1},{65,33},{97,65},{2,98}... | collective-permute-start | bytes 12296 | tf_op jit(solution)/shard_map/ppermute | solution.py:473
  545.8 16.9 %collective-permute-start.37 = (f32[8,128]{1,0:T(8,128)S(1)}, f32[8,128]{1,0:T(8,128)S(1)}, u32[]{:S(2)}, u32[]{:S(2)}) collective-permute-start(f32[8,128]{1,0:T(8,128)S(1)} %bitcast.244), channel_id=1, source_target_pairs={{0,64},{32,96},{64,0},{96,32},{1,65},{33,97},{65,1},{97,33},{2,66}... | collective-permute-start | bytes 12296 | tf_op jit(solution)/shard_map/ppermute | solution.py:473
  545.9 16.8 %collective-permute-start.36 = (f32[8,128]{1,0:T(8,128)S(1)}, f32[8,128]{1,0:T(8,128)S(1)}, u32[]{:S(2)}, u32[]{:S(2)}) collective-permute-start(f32[8,128]{1,0:T(8,128)S(1)} %bitcast.243), channel_id=1, source_target_pairs={{0,32},{32,64},{64,96},{96,0},{1,33},{33,65},{65,97},{97,1},{2,34}... | collective-permute-start | bytes 12296 | tf_op jit(solution)/shard_map/ppermute | solution.py:473
  553.9 20.0 %all-to-all-start.12 = ((bf16[16,8,2432]{2,1,0:T(8,128)(2,1)}), bf16[16,8,2432]{2,1,0:T(8,128)(2,1)S(1)}, u32[]{:S(2)}, u32[]{:S(2)}) async-start(bf16[16,8,2432]{2,1,0:T(8,128)(2,1)} %fusion.11), calls=%async_computation.12 | async-start | bytes 1245184 | tf_op jit(solution)/shard_map/all_to_all | solution.py:451
  (130 other events, 1133.9 us)
Sparse Core Ops, SparseCore 0:
  14.2 121.2 all-gather.1

commit v2 on v0

--- a/solution.py
+++ b/solution.py
@@ -677,13 +677,15 @@
 def first_projection(stream, shard, first):
     came = lax.ppermute(shard[8:16], "section", [(0, 1)])
     half = jnp.where(first, shard[0:8], came)
-    for axis in ("y", "x", "z"):
+    for axis in ("y", "x"):
         half = gathered_along(half, axis)
+    parts = normalised(stream).reshape(T, 64, 2, 8)
+    parts = parts[:, :, 0, :].reshape(T, 512), parts[:, :, 1, :].reshape(T, 512)
+    half, parts = lax.optimization_barrier((half, parts))
+    half = gathered_along(half, "z")
     half = half.reshape(512, XBC)
     other = swap(half)
     small = jnp.where(first, half[:, XBC - T :], other[:, XBC - T :]).reshape(64, 8, T)
-    parts = normalised(stream).reshape(T, 64, 2, 8)
-    parts = parts[:, :, 0, :].reshape(T, 512), parts[:, :, 1, :].reshape(T, 512)
     gain = small[:, 5, :16].astype(f32)
     gains = gain[:, :8].reshape(1, 512), gain[:, 8:].reshape(1, 512)
     low, high = [(part * g).astype(bf16) for part, g in zip(parts, gains)]
@@ -755,9 +757,9 @@
     )
     in_1 = to_layers(in_chip(grad_in, 16)).astype(bf16)
     g, grad_in, out_0, small_0, in_1 = backward_layer(kept[0], g, layers[0], in_1)
+    total_in = in_chip(grad_in, 16)
+    total_in, in_1, out_0, out_1 = lax.optimization_barrier((total_in, in_1, out_0, out_1))
     in_1 = to_owners(in_1)
-    total_in = in_chip(grad_in, 16)
-    total_in, out_0, out_1 = lax.optimization_barrier((total_in, out_0, out_1))
     in_1, small_0, small_1 = lax.optimization_barrier((in_1, small_0, small_1))
     smalls = (small_0, small_1)
     in_halves = (to_owners(to_layers(total_in).astype(bf16)), in_1)

time: 554 us -> 542 us (0.978)
  waiting for transfers between devices: 157 us -> 139 us
    ppermute x12, waiting for transfers between devices: 44 us -> 30.3 us  [to_layers(): lax.ppermute(piece(steps), 'dp', [(i, (i + steps) % 4) for i in range(4)])]
    all_to_all x4, waiting for transfers between devices: 31.5 us -> 23.3 us  [to_owners(): came = lax.all_to_all(value, 'seq', split_axis=0, concat_axis=0, tiled=True)]
    ppermute x11, waiting for transfers between devices: 4.97 us -> 12 us  [swap(): return lax.ppermute(value, 'section', [(0, 1), (1, 0)])]
    all_to_all x4, starting transfers between devices: 19.9 us -> 25.9 us  [to_owners(): came = lax.all_to_all(value, 'seq', split_axis=0, concat_axis=0, tiled=True)]
    unnamed x230 -> x228, local copies, waits for them, and re-layouts: 41.7 us -> 41.2 us
  transfers between devices with their start and end apart: 52 -> 52, of which waited for: 30 -> 32; matrix products, arithmetic and copies ran while one was open for 13% -> 15% of each run, Pallas kernels for 9% -> 9%
where the time goes in v2:
time: 542 us; the launch traced here: 536 us
  starting transfers between devices  140 us (26%)
  waiting for transfers between devices  139 us (26%)
  Pallas kernels  88 us (16%)
  local copies, waits for them, and re-layouts  79.6 us (15%)
  other arithmetic  43.5 us (8%)
  blocking collectives  16.3 us (3%)
  between operations  16.1 us (3%)
  matrix products  12.9 us (2%)
    pallas_call x8, Pallas kernels, call_tiled(): pl.pallas_call(dropping(kernel, len(args), len(after)), grid=(steps,), in...  52.3 us
    unnamed x228, local copies, waits for them, and re-layouts  41.2 us
    ppermute x3, waiting for transfers between devices, turned(): return lax.ppermute(value, 'dp', [(i, (i + steps) % 4) for i in range(4)])  35.7 us
    pallas_call x12, Pallas kernels, call(): pl.pallas_call(dropping(kernel, len(args), len(after)), out_shape=[jax.Sh...  35.7 us
    ppermute x12, waiting for transfers between devices, to_layers(): lax.ppermute(piece(steps), 'dp', [(i, (i + steps) % 4) for i in range(4)])  30.3 us
    ppermute x11, starting transfers between devices, swap(): return lax.ppermute(value, 'section', [(0, 1), (1, 0)])  28.6 us
    all_to_all x4, starting transfers between devices, to_owners(): came = lax.all_to_all(value, 'seq', split_axis=0, concat_axis=0, tiled=True)  25.9 us
    all_to_all x4, waiting for transfers between devices, to_owners(): came = lax.all_to_all(value, 'seq', split_axis=0, concat_axis=0, tiled=True)  23.3 us
  transfers between devices with their start and end apart: 52, of which 32 were waited for; matrix products, arithmetic and copies ran while one was open for 15% of the time, Pallas kernels for 9%

profile of v2, /device:TPU:1, one launch (start us, length us, event | category | flops | bytes accessed | tf_op | source)
XLA Modules:
  0.0 536.1 jit_solution(12755421382917254144)
XLA Ops:
  31.5 5.2 collective-permute-done.5
  38.9 3.6 collective-permute-start.8
  43.5 10.5 %collective-permute-done.7 = bf16[4,4,8,2560]{3,2,1,0:T(8,128)(2,1)S(1)} collective-permute-done((bf16[4,4,8,2560]{3,2,1,0:T(8,128)(2,1)S(1)}, bf16[4,4,8,2560]{3,2,1,0:T(8,128)(2,1)S(1)}, u32[]{:S(2)}, u32[]{:S(2)}) %collective-permute-start.7) | collective-permute-done | bytes 655392 | tf_op jit(solution)/shard_map/ppermute | solution.py:651
  54.0 23.3 %collective-permute-done.8 = bf16[4,4,8,2560]{3,2,1,0:T(8,128)(2,1)S(1)} collective-permute-done((bf16[4,4,8,2560]{3,2,1,0:T(8,128)(2,1)S(1)}, bf16[4,4,8,2560]{3,2,1,0:T(8,128)(2,1)S(1)}, u32[]{:S(2)}, u32[]{:S(2)}) %collective-permute-start.8) | collective-permute-done | bytes 655392 | tf_op jit(solution)/shard_map/ppermute | solution.py:651
  81.8 4.3 collective-permute-done.12
  104.3 8.0 %all-to-all-start = ((bf16[16,144,128]{2,1,0:T(8,128)(2,1)}), bf16[16,144,128]{2,1,0:T(8,128)(2,1)S(1)}, u32[]{:S(2)}, u32[]{:S(2)}) async-start(bf16[16,144,128]{2,1,0:T(8,128)(2,1)} %copy-done.44), calls=%async_computation | async-start | bytes 1179648 | tf_op jit(solution)/shard_map/all_to_all | solution.py:502
  113.1 14.9 %all-to-all-done.refs_0_ = bf16[16,144,128]{2,1,0:T(8,128)(2,1)S(1)} async-done(((bf16[16,144,128]{2,1,0:T(8,128)(2,1)}), bf16[16,144,128]{2,1,0:T(8,128)(2,1)S(1)}, u32[]{:S(2)}, u32[]{:S(2)}) %all-to-all-start) | async-done | bytes 589856 | tf_op jit(solution)/shard_map/all_to_all | solution.py:502
  128.9 6.4 %all-to-all-start.1 = ((bf16[16,128,128]{2,1,0:T(8,128)(2,1)}), bf16[16,128,128]{2,1,0:T(8,128)(2,1)S(1)}, u32[]{:S(2)}, u32[]{:S(2)}) async-start(bf16[16,128,128]{2,1,0:T(8,128)(2,1)} %scan.2), calls=%async_computation.1 | async-start | bytes 1048576 | tf_op jit(solution)/shard_map/all_to_all | solution.py:511
  139.6 3.7 project.2
  145.2 3.9 finish.2
  150.0 8.4 %project.3 = (bf16[128,1024]{1,0:T(8,128)(2,1)S(1)}, bf16[128,4608]{1,0:T(8,128)(2,1)S(1)}) custom-call(f32[128,1024]{1,0:T(8,128)S(1)} %get-tuple-element.80.refs_0_.refs_6_, f32[1,1024]{1,0:T(1,128)S(1)} %reshape.365.refs_1_.refs_7_, bf16[2048,6656]{1,0:T(8,128)(2,1)} %all-gather.2.cloned.1.call-done.refs_2_.refs_7_.refs_8_.refs_1_.refs_5_), custom_call_target="tpu_custom_call" | custom-call | bytes 14000000 | tf_op jit(solution)/shard_map/project/pallas_call | solution.py:432
  158.5 3.4 collective-permute-start.13
  165.6 16.3 %all_to_all.60.refs_0_ = bf16[16,144,128]{2,1,0:T(8,128)(2,1)S(1)} all-to-all(bf16[16,144,128]{2,1,0:T(8,128)(2,1)S(1)} %get-tuple-element.86), channel_id=1, replica_groups=mesh['dp'=4,'section'=2,'seq'=16] {'seq'}, dimensions={0} | all-to-all | bytes 1179648 | tf_op jit(solution)/shard_map/all_to_all | solution.py:502
  182.9 3.6 all-to-all-start.3
  196.6 4.0 finish.3
  203.5 16.2 %collective-permute-start.15 = (bf16[64,16,1024]{2,1,0:T(8,128)(2,1)}, bf16[64,16,1024]{2,1,0:T(8,128)(2,1)}, u32[]{:S(2)}, u32[]{:S(2)}) collective-permute-start(bf16[64,16,1024]{2,1,0:T(8,128)(2,1)} %dynamic-slice_bitcast_fusion.3), channel_id=1, source_target_pairs={{0,16},{16,0},{1,17},{17,1},{2,18},{18,2},{3,19},{19,3},{4,20},{20... | collective-permute-start | bytes 6291464 | tf_op jit(solution)/shard_map/ppermute | solution.py:447
  219.7 6.4 %top.2 = (bf16[128,2048]{1,0:T(8,128)(2,1)S(1)}, bf16[128,2048]{1,0:T(8,128)(2,1)S(1)}, f32[8,2048]{1,0:T(8,128)S(1)}, bf16[16,144,128]{2,1,0:T(8,128)(2,1)}) custom-call(bf16[128,1024]{1,0:T(8,128)(2,1)S(1)} %get-tuple-element.152.refs_0_, bf16[2048,6656]{1,0:T(8,128)(2,1)} %all-gather.2.cloned.1.call-done.refs_2_.refs_7_.refs_8_.refs_1_.refs_5_, ...), custom_call_target="tpu_custom_call" | custom-call | bytes 17500000 | tf_op jit(solution)/shard_map/top/pallas_call | solution.py:432
  227.6 4.2 all-to-all-start.4
  240.3 3.3 all-to-all-done.4.refs_0_
  245.6 4.2 all-to-all-start.5
  255.5 7.6 %inner.2 = (f32[128,2048]{1,0:T(8,128)S(1)}, f32[128,256]{1,0:T(8,128)S(1)}, f32[128,128]{1,0:T(8,128)S(1)}) custom-call(f32[128,2048]{1,0:T(8,128)S(1)} %get-tuple-element.82.refs_0_.refs_4_, bf16[128,256]{1,0:T(8,128)(2,1)S(1)} %get-tuple-element.83.refs_1_.refs_5_, f32[128,128]{1,0:T(8,128)S(1)} %copy-done.42, ...), custom_call_target="tpu_custom_call" | custom-call | bytes 28000000 | tf_op jit(solution)/shard_map/inner/pallas_call | solution.py:409
  275.6 5.2 outer.2
  288.0 9.7 %bottom.2 = (bf16[128,4608]{1,0:T(8,128)(2,1)S(1)}, f32[128,1024]{1,0:T(8,128)S(1)}, f32[8,1024]{1,0:T(8,128)S(1)}) custom-call(f32[128,2304]{1,0:T(8,128)S(1)} %get-tuple-element.95.refs_0_, f32[8,2304]{1,0:T(8,128)S(1)} %collective-permute-done.16.refs_1_, f32[8,2304]{1,0:T(8,128)S(1)} %pad_convert_fusion.refs_2_, bf16[128,2048]{1,0:T(8,128)(2,1)S(1)} %copy-done.48, ...), custom_call_target="tpu_custom_call" | custom-call | bytes 21000000 | tf_op jit(solution)/shard_map/bottom/pallas_call | solution.py:432
  305.3 3.9 collective-permute-done.20
  309.3 5.6 %fusion.1 = bf16[64,8,4480]{2,1,0:T(8,128)(2,1)} fusion(bf16[64,8,4480]{2,1,0:T(8,128)(2,1)} %collective-permute-done.20, bf16[64,2,8,4480]{3,2,1,0:T(8,128)(2,1)S(1)} %bitcast.199, s32[]{:T(128)S(6)} %select_n.366), kind=kLoop, calls=%fused_computation.5 | loop fusion | flops 9175040 | bytes 13762564 | tf_op jit(solution)/shard_map/convert_element_type | solution.py:487
  314.9 3.9 dynamic-slice_bitcast_fusion.9
  322.7 6.5 %top.3 = (bf16[128,2048]{1,0:T(8,128)(2,1)S(1)}, bf16[128,2048]{1,0:T(8,128)(2,1)S(1)}, f32[8,2048]{1,0:T(8,128)S(1)}, bf16[16,144,128]{2,1,0:T(8,128)(2,1)}) custom-call(bf16[128,1024]{1,0:T(8,128)(2,1)S(1)} %convert_element_type.266.refs_0_, bf16[2048,6656]{1,0:T(8,128)(2,1)} %all-gather.2.cloned.1.call-done.refs_2_.refs_7_.refs_8_.refs_1_.refs_5_, ...), custom_call_target="tpu_custom_call" | custom-call | bytes 17500000 | tf_op jit(solution)/shard_map/top/pallas_call | solution.py:432
  330.7 8.8 %all-to-all-start.6 = ((bf16[16,144,128]{2,1,0:T(8,128)(2,1)}), bf16[16,144,128]{2,1,0:T(8,128)(2,1)S(1)}, u32[]{:S(2)}, u32[]{:S(2)}) async-start(bf16[16,144,128]{2,1,0:T(8,128)(2,1)} %get-tuple-element.104), calls=%async_computation.6 | async-start | bytes 1179648 | tf_op jit(solution)/shard_map/all_to_all | solution.py:502
  339.5 7.6 %inner.3 = (f32[128,2048]{1,0:T(8,128)S(1)}, f32[128,256]{1,0:T(8,128)S(1)}, f32[128,128]{1,0:T(8,128)S(1)}) custom-call(f32[128,2048]{1,0:T(8,128)S(1)} %copy-done.1, bf16[128,256]{1,0:T(8,128)(2,1)S(1)} %get-tuple-element.75.refs_1_.refs_5_, f32[128,128]{1,0:T(8,128)S(1)} %copy-done.40, f32[128,128]{1,0:T(8,128)S(1)} %get-tuple-element.77.refs_3_.refs_2_.refs_6_.refs_7_, ...), custom_call_target="tpu_custom_call" | custom-call | bytes 28000000 | tf_op jit(solution)/shard_map/inner/pallas_call | solution.py:409
  350.7 5.9 %all-to-all-start.7 = ((bf16[16,128,128]{2,1,0:T(8,128)(2,1)}), bf16[16,128,128]{2,1,0:T(8,128)(2,1)}, u32[]{:S(2)}, u32[]{:S(2)}) async-start(bf16[16,128,128]{2,1,0:T(8,128)(2,1)} %scan_back.3), calls=%async_computation.7 | async-start | bytes 1048576 | tf_op jit(solution)/shard_map/all_to_all | solution.py:511
  356.6 3.2 fusion.2
  363.8 7.8 %collective-permute-done.22 = bf16[16,8,4480]{2,1,0:T(8,128)(2,1)} collective-permute-done((bf16[16,8,4480]{2,1,0:T(8,128)(2,1)}, bf16[16,8,4480]{2,1,0:T(8,128)(2,1)}, u32[]{:S(2)}, u32[]{:S(2)}) %collective-permute-start.22) | collective-permute-done | bytes 1146912 | tf_op jit(solution)/shard_map/ppermute | solution.py:463
  373.1 3.9 fusion.10.refs_10_
  383.1 5.2 outer.3
  390.6 3.5 collective-permute-done.27
  396.6 9.7 %bottom.3 = (bf16[128,4608]{1,0:T(8,128)(2,1)S(1)}, f32[128,1024]{1,0:T(8,128)S(1)}, f32[8,1024]{1,0:T(8,128)S(1)}) custom-call(f32[128,2304]{1,0:T(8,128)S(1)} %get-tuple-element.109.refs_0_, f32[8,2304]{1,0:T(8,128)S(1)} %collective-permute-done.25.refs_1_, f32[8,2304]{1,0:T(8,128)S(1)} %pad_convert_fusion.1.refs_2_, bf16[128,2048]{1,0:T(8,128)(2,1)S(1)} %copy-done.50, ...), custom_call_target="tpu_custom_call" | custom-call | bytes 21000000 | tf_op jit(solution)/shard_map/bottom/pallas_call | solution.py:432
  422.3 6.9 %fusion = bf16[64,8,4480]{2,1,0:T(8,128)(2,1)} fusion(bf16[64,8,4480]{2,1,0:T(8,128)(2,1)} %collective-permute-done.30, bf16[64,2,8,4480]{3,2,1,0:T(8,128)(2,1)} %bitcast.197, s32[]{:T(128)S(6)} %select_n.366), kind=kLoop, calls=%fused_computation.3 | loop fusion | flops 9175040 | bytes 13762564 | tf_op jit(solution)/shard_map/convert_element_type | solution.py:487
  429.2 9.7 %all-to-all-start.8 = ((bf16[16,8,4480]{2,1,0:T(8,128)(2,1)}), bf16[16,8,4480]{2,1,0:T(8,128)(2,1)S(1)}, u32[]{:S(2)}, u32[]{:S(2)}) async-start(bf16[16,8,4480]{2,1,0:T(8,128)(2,1)} %fusion.10.refs_10_), calls=%async_computation.8 | async-start | bytes 2293760 | tf_op jit(solution)/shard_map/all_to_all | solution.py:451
  438.9 3.9 dynamic-slice_bitcast_fusion.6
  447.9 7.7 %all-to-all-done.8 = bf16[16,8,4480]{2,1,0:T(8,128)(2,1)S(1)} async-done(((bf16[16,8,4480]{2,1,0:T(8,128)(2,1)}), bf16[16,8,4480]{2,1,0:T(8,128)(2,1)S(1)}, u32[]{:S(2)}, u32[]{:S(2)}) %all-to-all-start.8) | async-done | bytes 1146912 | tf_op jit(solution)/shard_map/all_to_all | solution.py:451
  455.6 4.6 all-to-all-start.11
  465.3 9.6 %all-to-all-done.11 = bf16[16,32,1024]{2,1,0:T(8,128)(2,1)S(1)} async-done(((bf16[16,32,1024]{2,1,0:T(8,128)(2,1)}), bf16[16,32,1024]{2,1,0:T(8,128)(2,1)S(1)}, u32[]{:S(2)}, u32[]{:S(2)}) %all-to-all-start.11) | async-done | bytes 1048608 | tf_op jit(solution)/shard_map/all_to_all | solution.py:451
  474.9 4.8 all-to-all-start.9
  479.7 15.6 %collective-permute-done.36 = bf16[16,8,4480]{2,1,0:T(8,128)(2,1)} collective-permute-done((bf16[16,8,4480]{2,1,0:T(8,128)(2,1)}, bf16[16,8,4480]{2,1,0:T(8,128)(2,1)}, u32[]{:S(2)}, u32[]{:S(2)}) %collective-permute-start.36) | collective-permute-done | bytes 1146912 | tf_op jit(solution)/shard_map/ppermute | solution.py:463
  496.4 3.9 fusion.7
  500.3 6.8 %all-to-all-start.10 = ((bf16[16,8,4480]{2,1,0:T(8,128)(2,1)}), bf16[16,8,4480]{2,1,0:T(8,128)(2,1)S(1)}, u32[]{:S(2)}, u32[]{:S(2)}) async-start(bf16[16,8,4480]{2,1,0:T(8,128)(2,1)} %fusion.7), calls=%async_computation.10 | async-start | bytes 2293760 | tf_op jit(solution)/shard_map/all_to_all | solution.py:451
  517.6 6.1 %all-to-all-done.10 = bf16[16,8,4480]{2,1,0:T(8,128)(2,1)S(1)} async-done(((bf16[16,8,4480]{2,1,0:T(8,128)(2,1)}), bf16[16,8,4480]{2,1,0:T(8,128)(2,1)S(1)}, u32[]{:S(2)}, u32[]{:S(2)}) %all-to-all-start.10) | async-done | bytes 1146912 | tf_op jit(solution)/shard_map/all_to_all | solution.py:451
  523.9 3.4 collective-permute-start.38
  (455 shorter events, 185.2 us)
Async XLA Ops:
  7.2 130.6 %all-gather.2.cloned.1.call-start = ((), (), s32[]{:S(2)}) async-start(), calls=%async_computation.12 | async-start | bytes 27475968 | tf_op jit(solution)/shard_map/all_gather | solution.py:709
  17.6 6.4 %collective-permute-start.1 = (bf16[8,2560]{1,0:T(8,128)(2,1)S(1)}, bf16[8,2560]{1,0:T(8,128)(2,1)S(1)}, u32[]{:S(2)}, u32[]{:S(2)}) collective-permute-start(bf16[8,2560]{1,0:T(8,128)(2,1)S(1)} %get-tuple-element.154), channel_id=1, source_target_pairs={{0,1},{1,2},{2,3},{3,0},{4,5},{5,6},{6,7},{7,4},{8,9},{9,10},{10,1... | collective-permute-start | bytes 122888 | tf_op jit(solution)/shard_map/ppermute | solution.py:659
  20.3 4.6 collective-permute-start.2
  26.1 5.4 %collective-permute-start.4 = (bf16[4,8,2560]{2,1,0:T(8,128)(2,1)S(1)}, bf16[4,8,2560]{2,1,0:T(8,128)(2,1)S(1)}, u32[]{:S(2)}, u32[]{:S(2)}) collective-permute-start(bf16[4,8,2560]{2,1,0:T(8,128)(2,1)S(1)} %bitcast_dynamic-update-slice_fusion.9), channel_id=1, source_target_pairs={{0,4},{1,5},{2,6},{3,7},{4,8},{5,9},{6,10},{7,11},{8,12},{9,13},{1... | collective-permute-start | bytes 491528 | tf_op jit(solution)/shard_map/ppermute | solution.py:659
  27.3 9.4 %collective-permute-start.5 = (bf16[4,8,2560]{2,1,0:T(8,128)(2,1)S(1)}, bf16[4,8,2560]{2,1,0:T(8,128)(2,1)S(1)}, u32[]{:S(2)}, u32[]{:S(2)}) collective-permute-start(bf16[4,8,2560]{2,1,0:T(8,128)(2,1)S(1)} %bitcast_dynamic-update-slice_fusion.9), channel_id=1, source_target_pairs={{0,8},{1,9},{2,10},{3,11},{4,12},{5,13},{6,14},{7,15},{8,0},{9,1},... | collective-permute-start | bytes 491528 | tf_op jit(solution)/shard_map/ppermute | solution.py:659
  29.7 7.2 %collective-permute-start.6 = (bf16[4,8,2560]{2,1,0:T(8,128)(2,1)S(1)}, bf16[4,8,2560]{2,1,0:T(8,128)(2,1)S(1)}, u32[]{:S(2)}, u32[]{:S(2)}) collective-permute-start(bf16[4,8,2560]{2,1,0:T(8,128)(2,1)S(1)} %bitcast_dynamic-update-slice_fusion.9), channel_id=1, source_target_pairs={{0,12},{1,13},{2,14},{3,15},{4,0},{5,1},{6,2},{7,3},{8,4},{9,5},{1... | collective-permute-start | bytes 491528 | tf_op jit(solution)/shard_map/ppermute | solution.py:659
  36.9 17.0 %collective-permute-start.7 = (bf16[4,4,8,2560]{3,2,1,0:T(8,128)(2,1)S(1)}, bf16[4,4,8,2560]{3,2,1,0:T(8,128)(2,1)S(1)}, u32[]{:S(2)}, u32[]{:S(2)}) collective-permute-start(bf16[4,4,8,2560]{3,2,1,0:T(8,128)(2,1)S(1)} %bitcast_dynamic-update-slice_fusion.4), channel_id=1, source_target_pairs={{0,32},{32,64},{64,96},{96,0},{1,33},{33,65},{65,97},{97,1},{2,34}... | collective-permute-start | bytes 1966088 | tf_op jit(solution)/shard_map/ppermute | solution.py:651
  38.9 38.5 %collective-permute-start.8 = (bf16[4,4,8,2560]{3,2,1,0:T(8,128)(2,1)S(1)}, bf16[4,4,8,2560]{3,2,1,0:T(8,128)(2,1)S(1)}, u32[]{:S(2)}, u32[]{:S(2)}) collective-permute-start(bf16[4,4,8,2560]{3,2,1,0:T(8,128)(2,1)S(1)} %bitcast_dynamic-update-slice_fusion.4), channel_id=1, source_target_pairs={{0,64},{32,96},{64,0},{96,32},{1,65},{33,97},{65,1},{97,33},{2,66}... | collective-permute-start | bytes 1966088 | tf_op jit(solution)/shard_map/ppermute | solution.py:651
  42.5 36.8 %collective-permute-start.9 = (bf16[4,4,8,2560]{3,2,1,0:T(8,128)(2,1)S(1)}, bf16[4,4,8,2560]{3,2,1,0:T(8,128)(2,1)S(1)}, u32[]{:S(2)}, u32[]{:S(2)}) collective-permute-start(bf16[4,4,8,2560]{3,2,1,0:T(8,128)(2,1)S(1)} %bitcast_dynamic-update-slice_fusion.4), channel_id=1, source_target_pairs={{0,96},{32,0},{64,32},{96,64},{1,97},{33,1},{65,33},{97,65},{2,98}... | collective-permute-start | bytes 1966088 | tf_op jit(solution)/shard_map/ppermute | solution.py:651
  79.4 10.2 %collective-permute-start.10 = (bf16[512,2560]{1,0:T(8,128)(2,1)S(1)}, bf16[512,2560]{1,0:T(8,128)(2,1)}, u32[]{:S(2)}, u32[]{:S(2)}) collective-permute-start(bf16[512,2560]{1,0:T(8,128)(2,1)S(1)} %bitcast.208), channel_id=1, source_target_pairs={{0,16},{16,0},{1,17},{17,1},{2,18},{18,2},{3,19},{19,3},{4,20},{20... | collective-permute-start | bytes 7864328 | tf_op jit(solution)/shard_map/ppermute | solution.py:447
  81.7 4.4 collective-permute-start.12
  96.3 5.6 %collective-permute-start.11 = (bf16[16,2304]{1,0:T(8,128)(2,1)S(1)}, bf16[16,2304]{1,0:T(8,128)(2,1)S(1)}, u32[]{:S(2)}, u32[]{:S(2)}) collective-permute-start(bf16[16,2304]{1,0:T(8,128)(2,1)S(1)} %slice.271), channel_id=1, source_target_pairs={{0,1},{1,2},{2,3},{3,4},{4,5},{5,6},{6,7},{7,8},{8,9},{9,10},{10,1... | collective-permute-start | bytes 221192 | tf_op jit(solution)/shard_map/ppermute | solution.py:529
  104.3 23.7 %all-to-all-start = ((bf16[16,144,128]{2,1,0:T(8,128)(2,1)}), bf16[16,144,128]{2,1,0:T(8,128)(2,1)S(1)}, u32[]{:S(2)}, u32[]{:S(2)}) async-start(bf16[16,144,128]{2,1,0:T(8,128)(2,1)} %copy-done.44), calls=%async_computation | async-start | bytes 1179648 | tf_op jit(solution)/shard_map/all_to_all | solution.py:502
  128.9 16.3 %all-to-all-start.1 = ((bf16[16,128,128]{2,1,0:T(8,128)(2,1)}), bf16[16,128,128]{2,1,0:T(8,128)(2,1)S(1)}, u32[]{:S(2)}, u32[]{:S(2)}) async-start(bf16[16,128,128]{2,1,0:T(8,128)(2,1)} %scan.2), calls=%async_computation.1 | async-start | bytes 1048576 | tf_op jit(solution)/shard_map/all_to_all | solution.py:511
  158.5 4.8 collective-permute-start.13
  182.9 12.5 %all-to-all-start.3 = ((bf16[16,128,128]{2,1,0:T(8,128)(2,1)}), bf16[16,128,128]{2,1,0:T(8,128)(2,1)S(1)}, u32[]{:S(2)}, u32[]{:S(2)}) async-start(bf16[16,128,128]{2,1,0:T(8,128)(2,1)} %scan.3), calls=%async_computation.3 | async-start | bytes 1048576 | tf_op jit(solution)/shard_map/all_to_all | solution.py:511
  203.5 28.5 %collective-permute-start.15 = (bf16[64,16,1024]{2,1,0:T(8,128)(2,1)}, bf16[64,16,1024]{2,1,0:T(8,128)(2,1)}, u32[]{:S(2)}, u32[]{:S(2)}) collective-permute-start(bf16[64,16,1024]{2,1,0:T(8,128)(2,1)} %dynamic-slice_bitcast_fusion.3), channel_id=1, source_target_pairs={{0,16},{16,0},{1,17},{17,1},{2,18},{18,2},{3,19},{19,3},{4,20},{20... | collective-permute-start | bytes 6291464 | tf_op jit(solution)/shard_map/ppermute | solution.py:447
  227.6 16.0 %all-to-all-start.4 = ((bf16[16,144,128]{2,1,0:T(8,128)(2,1)}), bf16[16,144,128]{2,1,0:T(8,128)(2,1)}, u32[]{:S(2)}, u32[]{:S(2)}) async-start(bf16[16,144,128]{2,1,0:T(8,128)(2,1)} %get-tuple-element.93), calls=%async_computation.4 | async-start | bytes 1179648 | tf_op jit(solution)/shard_map/all_to_all | solution.py:502
  236.4 47.5 %collective-permute-start.19 = (bf16[16,16,1024]{2,1,0:T(8,128)(2,1)}, bf16[16,16,1024]{2,1,0:T(8,128)(2,1)}, u32[]{:S(2)}, u32[]{:S(2)}) collective-permute-start(bf16[16,16,1024]{2,1,0:T(8,128)(2,1)} %get-tuple-element.165), channel_id=1, source_target_pairs={{0,64},{32,96},{64,0},{96,32},{1,65},{33,97},{65,1},{97,33},{2,66}... | collective-permute-start | bytes 1572872 | tf_op jit(solution)/shard_map/ppermute | solution.py:463
  238.9 45.1 %collective-permute-start.18 = (bf16[16,16,1024]{2,1,0:T(8,128)(2,1)}, bf16[16,16,1024]{2,1,0:T(8,128)(2,1)}, u32[]{:S(2)}, u32[]{:S(2)}) collective-permute-start(bf16[16,16,1024]{2,1,0:T(8,128)(2,1)} %get-tuple-element.166), channel_id=1, source_target_pairs={{0,96},{32,0},{64,32},{96,64},{1,97},{33,1},{65,33},{97,65},{2,98}... | collective-permute-start | bytes 1572872 | tf_op jit(solution)/shard_map/ppermute | solution.py:463
  239.8 44.2 %collective-permute-start.17 = (bf16[16,16,1024]{2,1,0:T(8,128)(2,1)}, bf16[16,16,1024]{2,1,0:T(8,128)(2,1)}, u32[]{:S(2)}, u32[]{:S(2)}) collective-permute-start(bf16[16,16,1024]{2,1,0:T(8,128)(2,1)} %get-tuple-element.164), channel_id=1, source_target_pairs={{0,32},{32,64},{64,96},{96,0},{1,33},{33,65},{65,97},{97,1},{2,34}... | collective-permute-start | bytes 1572872 | tf_op jit(solution)/shard_map/ppermute | solution.py:463
  245.6 20.5 %all-to-all-start.5 = ((bf16[16,128,128]{2,1,0:T(8,128)(2,1)}), bf16[16,128,128]{2,1,0:T(8,128)(2,1)}, u32[]{:S(2)}, u32[]{:S(2)}) async-start(bf16[16,128,128]{2,1,0:T(8,128)(2,1)} %copy-done.30), calls=%async_computation.5 | async-start | bytes 1048576 | tf_op jit(solution)/shard_map/all_to_all | solution.py:511
  251.0 14.4 %collective-permute-start.14 = (bf16[128,512]{1,0:T(8,128)(2,1)S(1)}, bf16[128,512]{1,0:T(8,128)(2,1)S(1)}, u32[]{:S(2)}, u32[]{:S(2)}) collective-permute-start(bf16[128,512]{1,0:T(8,128)(2,1)S(1)} %get-tuple-element.174), channel_id=1, source_target_pairs={{0,16},{16,0},{1,17},{17,1},{2,18},{18,2},{3,19},{19,3},{4,20},{20... | collective-permute-start | bytes 393224 | tf_op jit(solution)/shard_map/ppermute | solution.py:447
  282.1 5.9 %collective-permute-start.16 = (f32[8,2304]{1,0:T(8,128)S(1)}, f32[8,2304]{1,0:T(8,128)S(1)}, u32[]{:S(2)}, u32[]{:S(2)}) collective-permute-start(f32[8,2304]{1,0:T(8,128)S(1)} %slice.230), channel_id=1, source_target_pairs={{1,0},{2,1},{3,2},{4,3},{5,4},{6,5},{7,6},{8,7},{9,8},{10,9},{11,1... | collective-permute-start | bytes 221192 | tf_op jit(solution)/shard_map/ppermute | solution.py:620
  300.9 8.3 %collective-permute-start.20 = (bf16[64,8,4480]{2,1,0:T(8,128)(2,1)S(1)}, bf16[64,8,4480]{2,1,0:T(8,128)(2,1)}, u32[]{:S(2)}, u32[]{:S(2)}) collective-permute-start(bf16[64,8,4480]{2,1,0:T(8,128)(2,1)S(1)} %dynamic-slice_bitcast_fusion.1), channel_id=1, source_target_pairs={{0,16},{16,0},{1,17},{17,1},{2,18},{18,2},{3,19},{19,3},{4,20},{20... | collective-permute-start | bytes 13762568 | tf_op jit(solution)/shard_map/ppermute | solution.py:447
  304.7 51.8 %collective-permute-start.24 = (bf16[64,16,1024]{2,1,0:T(8,128)(2,1)}, bf16[64,16,1024]{2,1,0:T(8,128)(2,1)}, u32[]{:S(2)}, u32[]{:S(2)}) collective-permute-start(bf16[64,16,1024]{2,1,0:T(8,128)(2,1)} %dynamic-slice_bitcast_fusion.2), channel_id=1, source_target_pairs={{0,16},{16,0},{1,17},{17,1},{2,18},{18,2},{3,19},{19,3},{4,20},{20... | collective-permute-start | bytes 6291464 | tf_op jit(solution)/shard_map/ppermute | solution.py:447
  318.8 45.0 %collective-permute-start.23 = (bf16[16,8,4480]{2,1,0:T(8,128)(2,1)}, bf16[16,8,4480]{2,1,0:T(8,128)(2,1)}, u32[]{:S(2)}, u32[]{:S(2)}) collective-permute-start(bf16[16,8,4480]{2,1,0:T(8,128)(2,1)} %get-tuple-element.159), channel_id=1, source_target_pairs={{0,64},{32,96},{64,0},{96,32},{1,65},{33,97},{65,1},{97,33},{2,66}... | collective-permute-start | bytes 3440648 | tf_op jit(solution)/shard_map/ppermute | solution.py:463
  321.2 50.3 %collective-permute-start.22 = (bf16[16,8,4480]{2,1,0:T(8,128)(2,1)}, bf16[16,8,4480]{2,1,0:T(8,128)(2,1)}, u32[]{:S(2)}, u32[]{:S(2)}) collective-permute-start(bf16[16,8,4480]{2,1,0:T(8,128)(2,1)} %get-tuple-element.160), channel_id=1, source_target_pairs={{0,96},{32,0},{64,32},{96,64},{1,97},{33,1},{65,33},{97,65},{2,98}... | collective-permute-start | bytes 3440648 | tf_op jit(solution)/shard_map/ppermute | solution.py:463
  322.2 50.9 %collective-permute-start.21 = (bf16[16,8,4480]{2,1,0:T(8,128)(2,1)}, bf16[16,8,4480]{2,1,0:T(8,128)(2,1)}, u32[]{:S(2)}, u32[]{:S(2)}) collective-permute-start(bf16[16,8,4480]{2,1,0:T(8,128)(2,1)} %get-tuple-element.158), channel_id=1, source_target_pairs={{0,32},{32,64},{64,96},{96,0},{1,33},{33,65},{65,97},{97,1},{2,34}... | collective-permute-start | bytes 3440648 | tf_op jit(solution)/shard_map/ppermute | solution.py:463
  330.7 19.1 %all-to-all-start.6 = ((bf16[16,144,128]{2,1,0:T(8,128)(2,1)}), bf16[16,144,128]{2,1,0:T(8,128)(2,1)S(1)}, u32[]{:S(2)}, u32[]{:S(2)}) async-start(bf16[16,144,128]{2,1,0:T(8,128)(2,1)} %get-tuple-element.104), calls=%async_computation.6 | async-start | bytes 1179648 | tf_op jit(solution)/shard_map/all_to_all | solution.py:502
  350.7 26.3 %all-to-all-start.7 = ((bf16[16,128,128]{2,1,0:T(8,128)(2,1)}), bf16[16,128,128]{2,1,0:T(8,128)(2,1)}, u32[]{:S(2)}, u32[]{:S(2)}) async-start(bf16[16,128,128]{2,1,0:T(8,128)(2,1)} %scan_back.3), calls=%async_computation.7 | async-start | bytes 1048576 | tf_op jit(solution)/shard_map/all_to_all | solution.py:511
  361.0 29.6 %collective-permute-start.28 = (bf16[16,16,1024]{2,1,0:T(8,128)(2,1)}, bf16[16,16,1024]{2,1,0:T(8,128)(2,1)}, u32[]{:S(2)}, u32[]{:S(2)}) collective-permute-start(bf16[16,16,1024]{2,1,0:T(8,128)(2,1)} %get-tuple-element.162), channel_id=1, source_target_pairs={{0,64},{32,96},{64,0},{96,32},{1,65},{33,97},{65,1},{97,33},{2,66}... | collective-permute-start | bytes 1572872 | tf_op jit(solution)/shard_map/ppermute | solution.py:463
  361.7 32.4 %collective-permute-start.27 = (bf16[16,16,1024]{2,1,0:T(8,128)(2,1)}, bf16[16,16,1024]{2,1,0:T(8,128)(2,1)}, u32[]{:S(2)}, u32[]{:S(2)}) collective-permute-start(bf16[16,16,1024]{2,1,0:T(8,128)(2,1)} %get-tuple-element.163), channel_id=1, source_target_pairs={{0,96},{32,0},{64,32},{96,64},{1,97},{33,1},{65,33},{97,65},{2,98}... | collective-permute-start | bytes 1572872 | tf_op jit(solution)/shard_map/ppermute | solution.py:463
  363.8 31.1 %collective-permute-start.26 = (bf16[16,16,1024]{2,1,0:T(8,128)(2,1)}, bf16[16,16,1024]{2,1,0:T(8,128)(2,1)}, u32[]{:S(2)}, u32[]{:S(2)}) collective-permute-start(bf16[16,16,1024]{2,1,0:T(8,128)(2,1)} %get-tuple-element.161), channel_id=1, source_target_pairs={{0,32},{32,64},{64,96},{96,0},{1,33},{33,65},{65,97},{97,1},{2,34}... | collective-permute-start | bytes 1572872 | tf_op jit(solution)/shard_map/ppermute | solution.py:463
  388.9 7.6 %collective-permute-start.25 = (f32[8,2304]{1,0:T(8,128)S(1)}, f32[8,2304]{1,0:T(8,128)S(1)}, u32[]{:S(2)}, u32[]{:S(2)}) collective-permute-start(f32[8,2304]{1,0:T(8,128)S(1)} %slice.232), channel_id=1, source_target_pairs={{1,0},{2,1},{3,2},{4,3},{5,4},{6,5},{7,6},{8,7},{9,8},{10,9},{11,1... | collective-permute-start | bytes 221192 | tf_op jit(solution)/shard_map/ppermute | solution.py:620
  414.1 8.2 %collective-permute-start.30 = (bf16[64,8,4480]{2,1,0:T(8,128)(2,1)}, bf16[64,8,4480]{2,1,0:T(8,128)(2,1)}, u32[]{:S(2)}, u32[]{:S(2)}) collective-permute-start(bf16[64,8,4480]{2,1,0:T(8,128)(2,1)} %dynamic-slice_bitcast_fusion), channel_id=1, source_target_pairs={{0,16},{16,0},{1,17},{17,1},{2,18},{18,2},{3,19},{19,3},{4,20},{20... | collective-permute-start | bytes 13762568 | tf_op jit(solution)/shard_map/ppermute | solution.py:447
  418.9 44.4 %collective-permute-start.29 = (bf16[128,512]{1,0:T(8,128)(2,1)}, bf16[128,512]{1,0:T(8,128)(2,1)}, u32[]{:S(2)}, u32[]{:S(2)}) collective-permute-start(bf16[128,512]{1,0:T(8,128)(2,1)} %select_convert_fusion), channel_id=1, source_target_pairs={{0,16},{16,0},{1,17},{17,1},{2,18},{18,2},{3,19},{19,3},{4,20},{20... | collective-permute-start | bytes 393224 | tf_op jit(solution)/shard_map/ppermute | solution.py:447
  429.2 26.4 %all-to-all-start.8 = ((bf16[16,8,4480]{2,1,0:T(8,128)(2,1)}), bf16[16,8,4480]{2,1,0:T(8,128)(2,1)S(1)}, u32[]{:S(2)}, u32[]{:S(2)}) async-start(bf16[16,8,4480]{2,1,0:T(8,128)(2,1)} %fusion.10.refs_10_), calls=%async_computation.8 | async-start | bytes 2293760 | tf_op jit(solution)/shard_map/all_to_all | solution.py:451
  442.8 36.9 %collective-permute-start.37 = (bf16[16,8,4480]{2,1,0:T(8,128)(2,1)}, bf16[16,8,4480]{2,1,0:T(8,128)(2,1)}, u32[]{:S(2)}, u32[]{:S(2)}) collective-permute-start(bf16[16,8,4480]{2,1,0:T(8,128)(2,1)} %get-tuple-element.156), channel_id=1, source_target_pairs={{0,64},{32,96},{64,0},{96,32},{1,65},{33,97},{65,1},{97,33},{2,66}... | collective-permute-start | bytes 3440648 | tf_op jit(solution)/shard_map/ppermute | solution.py:463
  445.3 50.0 %collective-permute-start.36 = (bf16[16,8,4480]{2,1,0:T(8,128)(2,1)}, bf16[16,8,4480]{2,1,0:T(8,128)(2,1)}, u32[]{:S(2)}, u32[]{:S(2)}) collective-permute-start(bf16[16,8,4480]{2,1,0:T(8,128)(2,1)} %get-tuple-element.157), channel_id=1, source_target_pairs={{0,96},{32,0},{64,32},{96,64},{1,97},{33,1},{65,33},{97,65},{2,98}... | collective-permute-start | bytes 3440648 | tf_op jit(solution)/shard_map/ppermute | solution.py:463
  446.2 50.2 %collective-permute-start.35 = (bf16[16,8,4480]{2,1,0:T(8,128)(2,1)}, bf16[16,8,4480]{2,1,0:T(8,128)(2,1)}, u32[]{:S(2)}, u32[]{:S(2)}) collective-permute-start(bf16[16,8,4480]{2,1,0:T(8,128)(2,1)} %get-tuple-element.155), channel_id=1, source_target_pairs={{0,32},{32,64},{64,96},{96,0},{1,33},{33,65},{65,97},{97,1},{2,34}... | collective-permute-start | bytes 3440648 | tf_op jit(solution)/shard_map/ppermute | solution.py:463
  455.6 19.3 %all-to-all-start.11 = ((bf16[16,32,1024]{2,1,0:T(8,128)(2,1)}), bf16[16,32,1024]{2,1,0:T(8,128)(2,1)S(1)}, u32[]{:S(2)}, u32[]{:S(2)}) async-start(bf16[16,32,1024]{2,1,0:T(8,128)(2,1)} %pad_maximum_fusion), calls=%async_computation.11 | async-start | bytes 2097152 | tf_op jit(solution)/shard_map/all_to_all | solution.py:451
  474.9 25.4 %all-to-all-start.9 = ((f32[16,4,8,128]{3,1,2,0:T(4,128)}), f32[16,4,8,128]{3,1,2,0:T(4,128)S(1)}, u32[]{:S(2)}, u32[]{:S(2)}) async-start(f32[16,4,8,128]{3,1,2,0:T(4,128)} %bitcast.189), calls=%async_computation.9 | async-start | bytes 524288 | tf_op jit(solution)/shard_map/all_to_all | solution.py:451
  500.3 23.4 %all-to-all-start.10 = ((bf16[16,8,4480]{2,1,0:T(8,128)(2,1)}), bf16[16,8,4480]{2,1,0:T(8,128)(2,1)S(1)}, u32[]{:S(2)}, u32[]{:S(2)}) async-start(bf16[16,8,4480]{2,1,0:T(8,128)(2,1)} %fusion.7), calls=%async_computation.10 | async-start | bytes 2293760 | tf_op jit(solution)/shard_map/all_to_all | solution.py:451
  508.2 4.3 collective-permute-start.39
  509.1 4.1 collective-permute-start.34
  512.0 4.0 collective-permute-start.32
  523.9 4.4 collective-permute-start.38
  (109 other events, 1011.0 us)
Sparse Core Ops, SparseCore 0:
  14.2 122.8 all-gather.1

commit v3 on v2

--- a/solution.py
+++ b/solution.py
@@ -479,13 +479,21 @@
 
 
 def in_chip(grad, rows):
+    return chip_sum(*chip_parts(grad, rows))
+
+
+def chip_parts(grad, rows):
     columns = grad.shape[1]
     shaped = grad.reshape(64, 2, rows // 2, columns)
     section = lax.axis_index("section")
     mine = lax.dynamic_index_in_dim(shaped, section, 1, keepdims=False)
     theirs = lax.dynamic_index_in_dim(shaped, 1 - section, 1, keepdims=False)
-    total = (mine.astype(f32) + swap(theirs).astype(f32)).astype(bf16)
-    return total.reshape(4, 16, rows // 2, columns)
+    return mine, swap(theirs)
+
+
+def chip_sum(mine, came):
+    total = (mine.astype(f32) + came.astype(f32)).astype(bf16)
+    return total.reshape(4, 16, *mine.shape[1:])
 
 
 def own_layer(halves_of, first):
@@ -575,6 +583,9 @@
         5,
     )
     grad_out = dot_tn(normed, upstream_low).astype(bf16)
+    if earlier is not None:
+        payload, earlier = lax.optimization_barrier((payload, earlier))
+        earlier = to_layers(chip_sum(*earlier)).astype(bf16)
     leaving = exchange(payload, True)
     out_total = in_chip(grad_out, 32)
     grad_out = to_layers(out_total).astype(bf16)
@@ -755,7 +766,7 @@
     g, grad_in, out_1, small_1, _ = backward_layer(
         kept[1], g, layers[1], None, (out_part,)
     )
-    in_1 = to_layers(in_chip(grad_in, 16)).astype(bf16)
+    in_1 = chip_parts(grad_in, 16)
     g, grad_in, out_0, small_0, in_1 = backward_layer(kept[0], g, layers[0], in_1)
     total_in = in_chip(grad_in, 16)
     total_in, in_1, out_0, out_1 = lax.optimization_barrier((total_in, in_1, out_0, out_1))

time: 542 us -> 548 us (1.011)
    ppermute x12, waiting for transfers between devices: 30.3 us -> 37.6 us  [to_layers(): lax.ppermute(piece(steps), 'dp', [(i, (i + steps) % 4) for i in range(4)])]
    unnamed x228 -> x238, local copies, waits for them, and re-layouts: 41.2 us -> 43.9 us
  transfers between devices with their start and end apart: 52 -> 52, of which waited for: 32 -> 30; matrix products, arithmetic and copies ran while one was open for 15% -> 14% of each run, Pallas kernels for 9% -> 9%
where the time goes in v3:
time: 548 us; the launch traced here: 542 us
  waiting for transfers between devices  142 us (26%)
  starting transfers between devices  141 us (26%)
  Pallas kernels  88.3 us (16%)
  local copies, waits for them, and re-layouts  84 us (15%)
  other arithmetic  41.7 us (8%)
  blocking collectives  16.3 us (3%)
  between operations  16.2 us (3%)
  matrix products  12.9 us (2%)
    pallas_call x8, Pallas kernels, call_tiled(): pl.pallas_call(dropping(kernel, len(args), len(after)), grid=(steps,), in...  52.4 us
    unnamed x238, local copies, waits for them, and re-layouts  43.9 us
    ppermute x12, waiting for transfers between devices, to_layers(): lax.ppermute(piece(steps), 'dp', [(i, (i + steps) % 4) for i in range(4)])  37.6 us
    pallas_call x12, Pallas kernels, call(): pl.pallas_call(dropping(kernel, len(args), len(after)), out_shape=[jax.Sh...  35.9 us
    ppermute x3, waiting for transfers between devices, turned(): return lax.ppermute(value, 'dp', [(i, (i + steps) % 4) for i in range(4)])  35.7 us
    ppermute x11, starting transfers between devices, swap(): return lax.ppermute(value, 'section', [(0, 1), (1, 0)])  28.5 us
    all_to_all x4, starting transfers between devices, to_owners(): came = lax.all_to_all(value, 'seq', split_axis=0, concat_axis=0, tiled=True)  25.4 us
    all_to_all x4, waiting for transfers between devices, to_owners(): came = lax.all_to_all(value, 'seq', split_axis=0, concat_axis=0, tiled=True)  23.4 us
  transfers between devices with their start and end apart: 52, of which 30 were waited for; matrix products, arithmetic and copies ran while one was open for 14% of the time, Pallas kernels for 9%

profile of v3, /device:TPU:1, one launch (start us, length us, event | category | flops | bytes accessed | tf_op | source)
XLA Modules:
  0.0 542.2 jit_solution(13359128146352946800)
XLA Ops:
  31.5 5.2 collective-permute-done.5
  38.9 3.6 collective-permute-start.8
  43.5 10.5 %collective-permute-done.7 = bf16[4,4,8,2560]{3,2,1,0:T(8,128)(2,1)S(1)} collective-permute-done((bf16[4,4,8,2560]{3,2,1,0:T(8,128)(2,1)S(1)}, bf16[4,4,8,2560]{3,2,1,0:T(8,128)(2,1)S(1)}, u32[]{:S(2)}, u32[]{:S(2)}) %collective-permute-start.7) | collective-permute-done | bytes 655392 | tf_op jit(solution)/shard_map/ppermute | solution.py:662
  54.0 23.3 %collective-permute-done.8 = bf16[4,4,8,2560]{3,2,1,0:T(8,128)(2,1)S(1)} collective-permute-done((bf16[4,4,8,2560]{3,2,1,0:T(8,128)(2,1)S(1)}, bf16[4,4,8,2560]{3,2,1,0:T(8,128)(2,1)S(1)}, u32[]{:S(2)}, u32[]{:S(2)}) %collective-permute-start.8) | collective-permute-done | bytes 655392 | tf_op jit(solution)/shard_map/ppermute | solution.py:662
  81.8 4.3 collective-permute-done.12
  104.3 8.0 %all-to-all-start = ((bf16[16,144,128]{2,1,0:T(8,128)(2,1)}), bf16[16,144,128]{2,1,0:T(8,128)(2,1)S(1)}, u32[]{:S(2)}, u32[]{:S(2)}) async-start(bf16[16,144,128]{2,1,0:T(8,128)(2,1)} %copy-done.45), calls=%async_computation | async-start | bytes 1179648 | tf_op jit(solution)/shard_map/all_to_all | solution.py:510
  113.1 14.9 %all-to-all-done.refs_0_ = bf16[16,144,128]{2,1,0:T(8,128)(2,1)S(1)} async-done(((bf16[16,144,128]{2,1,0:T(8,128)(2,1)}), bf16[16,144,128]{2,1,0:T(8,128)(2,1)S(1)}, u32[]{:S(2)}, u32[]{:S(2)}) %all-to-all-start) | async-done | bytes 589856 | tf_op jit(solution)/shard_map/all_to_all | solution.py:510
  128.9 6.4 %all-to-all-start.1 = ((bf16[16,128,128]{2,1,0:T(8,128)(2,1)}), bf16[16,128,128]{2,1,0:T(8,128)(2,1)S(1)}, u32[]{:S(2)}, u32[]{:S(2)}) async-start(bf16[16,128,128]{2,1,0:T(8,128)(2,1)} %scan.2), calls=%async_computation.1 | async-start | bytes 1048576 | tf_op jit(solution)/shard_map/all_to_all | solution.py:519
  139.6 3.7 project.2
  145.2 3.9 finish.2
  150.0 8.4 %project.3 = (bf16[128,1024]{1,0:T(8,128)(2,1)S(1)}, bf16[128,4608]{1,0:T(8,128)(2,1)S(1)}) custom-call(f32[128,1024]{1,0:T(8,128)S(1)} %get-tuple-element.83.refs_0_.refs_6_, f32[1,1024]{1,0:T(1,128)S(1)} %reshape.363.refs_1_.refs_7_, bf16[2048,6656]{1,0:T(8,128)(2,1)} %all-gather.2.cloned.1.call-done.refs_2_.refs_7_.refs_8_.refs_1_.refs_5_), custom_call_target="tpu_custom_call" | custom-call | bytes 14000000 | tf_op jit(solution)/shard_map/project/pallas_call | solution.py:432
  158.4 3.4 collective-permute-start.13
  165.6 16.3 %all_to_all.60.refs_0_ = bf16[16,144,128]{2,1,0:T(8,128)(2,1)S(1)} all-to-all(bf16[16,144,128]{2,1,0:T(8,128)(2,1)S(1)} %get-tuple-element.89), channel_id=1, replica_groups=mesh['dp'=4,'section'=2,'seq'=16] {'seq'}, dimensions={0} | all-to-all | bytes 1179648 | tf_op jit(solution)/shard_map/all_to_all | solution.py:510
  182.8 3.6 all-to-all-start.3
  196.5 4.0 finish.3
  203.5 16.2 %collective-permute-start.15 = (bf16[64,16,1024]{2,1,0:T(8,128)(2,1)}, bf16[64,16,1024]{2,1,0:T(8,128)(2,1)}, u32[]{:S(2)}, u32[]{:S(2)}) collective-permute-start(bf16[64,16,1024]{2,1,0:T(8,128)(2,1)} %dynamic-slice_bitcast_fusion.4), channel_id=1, source_target_pairs={{0,16},{16,0},{1,17},{17,1},{2,18},{18,2},{3,19},{19,3},{4,20},{20... | collective-permute-start | bytes 6291464 | tf_op jit(solution)/shard_map/ppermute | solution.py:447
  219.7 6.4 %top.2 = (bf16[128,2048]{1,0:T(8,128)(2,1)S(1)}, bf16[128,2048]{1,0:T(8,128)(2,1)S(1)}, f32[8,2048]{1,0:T(8,128)S(1)}, bf16[16,144,128]{2,1,0:T(8,128)(2,1)}) custom-call(bf16[128,1024]{1,0:T(8,128)(2,1)S(1)} %get-tuple-element.158.refs_0_, bf16[2048,6656]{1,0:T(8,128)(2,1)} %all-gather.2.cloned.1.call-done.refs_2_.refs_7_.refs_8_.refs_1_.refs_5_, ...), custom_call_target="tpu_custom_call" | custom-call | bytes 17500000 | tf_op jit(solution)/shard_map/top/pallas_call | solution.py:432
  227.7 4.3 all-to-all-start.4
  232.0 3.2 fusion.2
  240.3 3.4 all-to-all-done.4.refs_0_
  245.7 4.2 all-to-all-start.5
  255.5 7.6 %inner.2 = (f32[128,2048]{1,0:T(8,128)S(1)}, f32[128,256]{1,0:T(8,128)S(1)}, f32[128,128]{1,0:T(8,128)S(1)}) custom-call(f32[128,2048]{1,0:T(8,128)S(1)} %get-tuple-element.85.refs_0_.refs_4_, bf16[128,256]{1,0:T(8,128)(2,1)S(1)} %get-tuple-element.86.refs_1_.refs_5_, f32[128,128]{1,0:T(8,128)S(1)} %copy-done.43, ...), custom_call_target="tpu_custom_call" | custom-call | bytes 28000000 | tf_op jit(solution)/shard_map/inner/pallas_call | solution.py:409
  275.6 5.2 outer.2
  288.0 9.7 %bottom.2 = (bf16[128,4608]{1,0:T(8,128)(2,1)S(1)}, f32[128,1024]{1,0:T(8,128)S(1)}, f32[8,1024]{1,0:T(8,128)S(1)}) custom-call(f32[128,2304]{1,0:T(8,128)S(1)} %get-tuple-element.98.refs_0_, f32[8,2304]{1,0:T(8,128)S(1)} %collective-permute-done.16.refs_1_, f32[8,2304]{1,0:T(8,128)S(1)} %pad_convert_fusion.refs_2_, bf16[128,2048]{1,0:T(8,128)(2,1)S(1)} %copy-done.49, ...), custom_call_target="tpu_custom_call" | custom-call | bytes 21000000 | tf_op jit(solution)/shard_map/bottom/pallas_call | solution.py:432
  300.5 4.1 dynamic-slice_bitcast_fusion.1
  309.9 6.6 %top.3 = (bf16[128,2048]{1,0:T(8,128)(2,1)S(1)}, bf16[128,2048]{1,0:T(8,128)(2,1)S(1)}, f32[8,2048]{1,0:T(8,128)S(1)}, bf16[16,144,128]{2,1,0:T(8,128)(2,1)}) custom-call(bf16[128,1024]{1,0:T(8,128)(2,1)S(1)} %convert_element_type.263.refs_0_, bf16[2048,6656]{1,0:T(8,128)(2,1)} %all-gather.2.cloned.1.call-done.refs_2_.refs_7_.refs_8_.refs_1_.refs_5_, ...), custom_call_target="tpu_custom_call" | custom-call | bytes 17500000 | tf_op jit(solution)/shard_map/top/pallas_call | solution.py:432
  318.7 3.4 add_convert_fusion
  329.2 8.9 %all-to-all-start.6 = ((bf16[16,144,128]{2,1,0:T(8,128)(2,1)}), bf16[16,144,128]{2,1,0:T(8,128)(2,1)}, u32[]{:S(2)}, u32[]{:S(2)}) async-start(bf16[16,144,128]{2,1,0:T(8,128)(2,1)} %get-tuple-element.110), calls=%async_computation.6 | async-start | bytes 1179648 | tf_op jit(solution)/shard_map/all_to_all | solution.py:510
  338.1 7.6 %inner.3 = (f32[128,2048]{1,0:T(8,128)S(1)}, f32[128,256]{1,0:T(8,128)S(1)}, f32[128,128]{1,0:T(8,128)S(1)}) custom-call(f32[128,2048]{1,0:T(8,128)S(1)} %copy-done.1, bf16[128,256]{1,0:T(8,128)(2,1)S(1)} %get-tuple-element.78.refs_1_.refs_5_, f32[128,128]{1,0:T(8,128)S(1)} %copy-done.41, f32[128,128]{1,0:T(8,128)S(1)} %get-tuple-element.80.refs_3_.refs_2_.refs_6_.refs_7_, ...), custom_call_target="tpu_custom_call" | custom-call | bytes 28000000 | tf_op jit(solution)/shard_map/inner/pallas_call | solution.py:409
  346.4 3.7 fusion.1
  356.0 6.8 %all-to-all-start.7 = ((bf16[16,128,128]{2,1,0:T(8,128)(2,1)}), bf16[16,128,128]{2,1,0:T(8,128)(2,1)}, u32[]{:S(2)}, u32[]{:S(2)}) async-start(bf16[16,128,128]{2,1,0:T(8,128)(2,1)} %copy-done.31), calls=%async_computation.7 | async-start | bytes 1048576 | tf_op jit(solution)/shard_map/all_to_all | solution.py:519
  363.0 15.6 %collective-permute-done.22 = bf16[16,8,4480]{2,1,0:T(8,128)(2,1)} collective-permute-done((bf16[16,8,4480]{2,1,0:T(8,128)(2,1)}, bf16[16,8,4480]{2,1,0:T(8,128)(2,1)}, u32[]{:S(2)}, u32[]{:S(2)}) %collective-permute-start.22) | collective-permute-done | bytes 1146912 | tf_op jit(solution)/shard_map/ppermute | solution.py:463
  379.2 3.9 fusion.9.refs_10_
  389.2 5.2 outer.3
  396.7 4.3 collective-permute-done.27
  403.2 9.7 %bottom.3 = (bf16[128,4608]{1,0:T(8,128)(2,1)S(1)}, f32[128,1024]{1,0:T(8,128)S(1)}, f32[8,1024]{1,0:T(8,128)S(1)}) custom-call(f32[128,2304]{1,0:T(8,128)S(1)} %get-tuple-element.115.refs_0_, f32[8,2304]{1,0:T(8,128)S(1)} %collective-permute-done.25.refs_1_, f32[8,2304]{1,0:T(8,128)S(1)} %pad_convert_fusion.1.refs_2_, bf16[128,2048]{1,0:T(8,128)(2,1)S(1)} %copy-done.51, ...), custom_call_target="tpu_custom_call" | custom-call | bytes 21000000 | tf_op jit(solution)/shard_map/bottom/pallas_call | solution.py:432
  428.8 6.9 %fusion = bf16[64,8,4480]{2,1,0:T(8,128)(2,1)} fusion(bf16[64,8,4480]{2,1,0:T(8,128)(2,1)} %collective-permute-done.30, bf16[64,2,8,4480]{3,2,1,0:T(8,128)(2,1)} %bitcast.194, s32[]{:T(128)S(6)} %select_n.366), kind=kLoop, calls=%fused_computation.3 | loop fusion | flops 9175040 | bytes 13762564 | tf_op jit(solution)/shard_map/convert_element_type | solution.py:495
  435.8 9.3 %all-to-all-start.8 = ((bf16[16,8,4480]{2,1,0:T(8,128)(2,1)}), bf16[16,8,4480]{2,1,0:T(8,128)(2,1)S(1)}, u32[]{:S(2)}, u32[]{:S(2)}) async-start(bf16[16,8,4480]{2,1,0:T(8,128)(2,1)} %fusion.9.refs_10_), calls=%async_computation.8 | async-start | bytes 2293760 | tf_op jit(solution)/shard_map/all_to_all | solution.py:451
  445.1 3.9 dynamic-slice_bitcast_fusion.7
  454.0 7.7 %all-to-all-done.8 = bf16[16,8,4480]{2,1,0:T(8,128)(2,1)S(1)} async-done(((bf16[16,8,4480]{2,1,0:T(8,128)(2,1)}), bf16[16,8,4480]{2,1,0:T(8,128)(2,1)S(1)}, u32[]{:S(2)}, u32[]{:S(2)}) %all-to-all-start.8) | async-done | bytes 1146912 | tf_op jit(solution)/shard_map/all_to_all | solution.py:451
  461.7 4.6 all-to-all-start.11
  471.5 9.6 %all-to-all-done.11 = bf16[16,32,1024]{2,1,0:T(8,128)(2,1)S(1)} async-done(((bf16[16,32,1024]{2,1,0:T(8,128)(2,1)}), bf16[16,32,1024]{2,1,0:T(8,128)(2,1)S(1)}, u32[]{:S(2)}, u32[]{:S(2)}) %all-to-all-start.11) | async-done | bytes 1048608 | tf_op jit(solution)/shard_map/all_to_all | solution.py:451
  481.1 4.8 all-to-all-start.9
  485.9 15.6 %collective-permute-done.36 = bf16[16,8,4480]{2,1,0:T(8,128)(2,1)} collective-permute-done((bf16[16,8,4480]{2,1,0:T(8,128)(2,1)}, bf16[16,8,4480]{2,1,0:T(8,128)(2,1)}, u32[]{:S(2)}, u32[]{:S(2)}) %collective-permute-start.36) | collective-permute-done | bytes 1146912 | tf_op jit(solution)/shard_map/ppermute | solution.py:463
  502.6 3.9 fusion.6
  506.5 6.8 %all-to-all-start.10 = ((bf16[16,8,4480]{2,1,0:T(8,128)(2,1)}), bf16[16,8,4480]{2,1,0:T(8,128)(2,1)S(1)}, u32[]{:S(2)}, u32[]{:S(2)}) async-start(bf16[16,8,4480]{2,1,0:T(8,128)(2,1)} %fusion.6), calls=%async_computation.10 | async-start | bytes 2293760 | tf_op jit(solution)/shard_map/all_to_all | solution.py:451
  523.7 6.1 %all-to-all-done.10 = bf16[16,8,4480]{2,1,0:T(8,128)(2,1)S(1)} async-done(((bf16[16,8,4480]{2,1,0:T(8,128)(2,1)}), bf16[16,8,4480]{2,1,0:T(8,128)(2,1)S(1)}, u32[]{:S(2)}, u32[]{:S(2)}) %all-to-all-start.10) | async-done | bytes 1146912 | tf_op jit(solution)/shard_map/all_to_all | solution.py:451
  530.1 3.4 collective-permute-start.38
  (466 shorter events, 184.2 us)
Async XLA Ops:
  7.2 130.6 %all-gather.2.cloned.1.call-start = ((), (), s32[]{:S(2)}) async-start(), calls=%async_computation.12 | async-start | bytes 27475968 | tf_op jit(solution)/shard_map/all_gather | solution.py:720
  17.6 6.4 %collective-permute-start.1 = (bf16[8,2560]{1,0:T(8,128)(2,1)S(1)}, bf16[8,2560]{1,0:T(8,128)(2,1)S(1)}, u32[]{:S(2)}, u32[]{:S(2)}) collective-permute-start(bf16[8,2560]{1,0:T(8,128)(2,1)S(1)} %get-tuple-element.160), channel_id=1, source_target_pairs={{0,1},{1,2},{2,3},{3,0},{4,5},{5,6},{6,7},{7,4},{8,9},{9,10},{10,1... | collective-permute-start | bytes 122888 | tf_op jit(solution)/shard_map/ppermute | solution.py:670
  20.3 4.6 collective-permute-start.2
  26.1 5.4 collective-permute-start.4
  27.3 9.4 %collective-permute-start.5 = (bf16[4,8,2560]{2,1,0:T(8,128)(2,1)S(1)}, bf16[4,8,2560]{2,1,0:T(8,128)(2,1)S(1)}, u32[]{:S(2)}, u32[]{:S(2)}) collective-permute-start(bf16[4,8,2560]{2,1,0:T(8,128)(2,1)S(1)} %bitcast_dynamic-update-slice_fusion.9), channel_id=1, source_target_pairs={{0,8},{1,9},{2,10},{3,11},{4,12},{5,13},{6,14},{7,15},{8,0},{9,1},... | collective-permute-start | bytes 491528 | tf_op jit(solution)/shard_map/ppermute | solution.py:670
  29.7 7.2 %collective-permute-start.6 = (bf16[4,8,2560]{2,1,0:T(8,128)(2,1)S(1)}, bf16[4,8,2560]{2,1,0:T(8,128)(2,1)S(1)}, u32[]{:S(2)}, u32[]{:S(2)}) collective-permute-start(bf16[4,8,2560]{2,1,0:T(8,128)(2,1)S(1)} %bitcast_dynamic-update-slice_fusion.9), channel_id=1, source_target_pairs={{0,12},{1,13},{2,14},{3,15},{4,0},{5,1},{6,2},{7,3},{8,4},{9,5},{1... | collective-permute-start | bytes 491528 | tf_op jit(solution)/shard_map/ppermute | solution.py:670
  37.0 17.0 %collective-permute-start.7 = (bf16[4,4,8,2560]{3,2,1,0:T(8,128)(2,1)S(1)}, bf16[4,4,8,2560]{3,2,1,0:T(8,128)(2,1)S(1)}, u32[]{:S(2)}, u32[]{:S(2)}) collective-permute-start(bf16[4,4,8,2560]{3,2,1,0:T(8,128)(2,1)S(1)} %bitcast_dynamic-update-slice_fusion.4), channel_id=1, source_target_pairs={{0,32},{32,64},{64,96},{96,0},{1,33},{33,65},{65,97},{97,1},{2,34}... | collective-permute-start | bytes 1966088 | tf_op jit(solution)/shard_map/ppermute | solution.py:662
  38.9 38.5 %collective-permute-start.8 = (bf16[4,4,8,2560]{3,2,1,0:T(8,128)(2,1)S(1)}, bf16[4,4,8,2560]{3,2,1,0:T(8,128)(2,1)S(1)}, u32[]{:S(2)}, u32[]{:S(2)}) collective-permute-start(bf16[4,4,8,2560]{3,2,1,0:T(8,128)(2,1)S(1)} %bitcast_dynamic-update-slice_fusion.4), channel_id=1, source_target_pairs={{0,64},{32,96},{64,0},{96,32},{1,65},{33,97},{65,1},{97,33},{2,66}... | collective-permute-start | bytes 1966088 | tf_op jit(solution)/shard_map/ppermute | solution.py:662
  42.5 36.8 %collective-permute-start.9 = (bf16[4,4,8,2560]{3,2,1,0:T(8,128)(2,1)S(1)}, bf16[4,4,8,2560]{3,2,1,0:T(8,128)(2,1)S(1)}, u32[]{:S(2)}, u32[]{:S(2)}) collective-permute-start(bf16[4,4,8,2560]{3,2,1,0:T(8,128)(2,1)S(1)} %bitcast_dynamic-update-slice_fusion.4), channel_id=1, source_target_pairs={{0,96},{32,0},{64,32},{96,64},{1,97},{33,1},{65,33},{97,65},{2,98}... | collective-permute-start | bytes 1966088 | tf_op jit(solution)/shard_map/ppermute | solution.py:662
  79.4 10.2 %collective-permute-start.10 = (bf16[512,2560]{1,0:T(8,128)(2,1)S(1)}, bf16[512,2560]{1,0:T(8,128)(2,1)}, u32[]{:S(2)}, u32[]{:S(2)}) collective-permute-start(bf16[512,2560]{1,0:T(8,128)(2,1)S(1)} %bitcast.206), channel_id=1, source_target_pairs={{0,16},{16,0},{1,17},{17,1},{2,18},{18,2},{3,19},{19,3},{4,20},{20... | collective-permute-start | bytes 7864328 | tf_op jit(solution)/shard_map/ppermute | solution.py:447
  81.7 4.4 collective-permute-start.12
  96.3 5.6 %collective-permute-start.11 = (bf16[16,2304]{1,0:T(8,128)(2,1)S(1)}, bf16[16,2304]{1,0:T(8,128)(2,1)S(1)}, u32[]{:S(2)}, u32[]{:S(2)}) collective-permute-start(bf16[16,2304]{1,0:T(8,128)(2,1)S(1)} %slice.271), channel_id=1, source_target_pairs={{0,1},{1,2},{2,3},{3,4},{4,5},{5,6},{6,7},{7,8},{8,9},{9,10},{10,1... | collective-permute-start | bytes 221192 | tf_op jit(solution)/shard_map/ppermute | solution.py:537
  104.3 23.7 %all-to-all-start = ((bf16[16,144,128]{2,1,0:T(8,128)(2,1)}), bf16[16,144,128]{2,1,0:T(8,128)(2,1)S(1)}, u32[]{:S(2)}, u32[]{:S(2)}) async-start(bf16[16,144,128]{2,1,0:T(8,128)(2,1)} %copy-done.45), calls=%async_computation | async-start | bytes 1179648 | tf_op jit(solution)/shard_map/all_to_all | solution.py:510
  128.9 16.2 %all-to-all-start.1 = ((bf16[16,128,128]{2,1,0:T(8,128)(2,1)}), bf16[16,128,128]{2,1,0:T(8,128)(2,1)S(1)}, u32[]{:S(2)}, u32[]{:S(2)}) async-start(bf16[16,128,128]{2,1,0:T(8,128)(2,1)} %scan.2), calls=%async_computation.1 | async-start | bytes 1048576 | tf_op jit(solution)/shard_map/all_to_all | solution.py:519
  158.4 4.8 collective-permute-start.13
  182.8 12.5 %all-to-all-start.3 = ((bf16[16,128,128]{2,1,0:T(8,128)(2,1)}), bf16[16,128,128]{2,1,0:T(8,128)(2,1)S(1)}, u32[]{:S(2)}, u32[]{:S(2)}) async-start(bf16[16,128,128]{2,1,0:T(8,128)(2,1)} %scan.3), calls=%async_computation.3 | async-start | bytes 1048576 | tf_op jit(solution)/shard_map/all_to_all | solution.py:519
  203.5 28.5 %collective-permute-start.15 = (bf16[64,16,1024]{2,1,0:T(8,128)(2,1)}, bf16[64,16,1024]{2,1,0:T(8,128)(2,1)}, u32[]{:S(2)}, u32[]{:S(2)}) collective-permute-start(bf16[64,16,1024]{2,1,0:T(8,128)(2,1)} %dynamic-slice_bitcast_fusion.4), channel_id=1, source_target_pairs={{0,16},{16,0},{1,17},{17,1},{2,18},{18,2},{3,19},{19,3},{4,20},{20... | collective-permute-start | bytes 6291464 | tf_op jit(solution)/shard_map/ppermute | solution.py:447
  227.7 16.0 %all-to-all-start.4 = ((bf16[16,144,128]{2,1,0:T(8,128)(2,1)}), bf16[16,144,128]{2,1,0:T(8,128)(2,1)}, u32[]{:S(2)}, u32[]{:S(2)}) async-start(bf16[16,144,128]{2,1,0:T(8,128)(2,1)} %get-tuple-element.96), calls=%async_computation.4 | async-start | bytes 1179648 | tf_op jit(solution)/shard_map/all_to_all | solution.py:510
  236.4 47.5 %collective-permute-start.19 = (bf16[16,16,1024]{2,1,0:T(8,128)(2,1)}, bf16[16,16,1024]{2,1,0:T(8,128)(2,1)}, u32[]{:S(2)}, u32[]{:S(2)}) collective-permute-start(bf16[16,16,1024]{2,1,0:T(8,128)(2,1)} %get-tuple-element.173), channel_id=1, source_target_pairs={{0,64},{32,96},{64,0},{96,32},{1,65},{33,97},{65,1},{97,33},{2,66}... | collective-permute-start | bytes 1572872 | tf_op jit(solution)/shard_map/ppermute | solution.py:463
  238.9 45.0 %collective-permute-start.18 = (bf16[16,16,1024]{2,1,0:T(8,128)(2,1)}, bf16[16,16,1024]{2,1,0:T(8,128)(2,1)}, u32[]{:S(2)}, u32[]{:S(2)}) collective-permute-start(bf16[16,16,1024]{2,1,0:T(8,128)(2,1)} %get-tuple-element.174), channel_id=1, source_target_pairs={{0,96},{32,0},{64,32},{96,64},{1,97},{33,1},{65,33},{97,65},{2,98}... | collective-permute-start | bytes 1572872 | tf_op jit(solution)/shard_map/ppermute | solution.py:463
  239.8 44.1 %collective-permute-start.17 = (bf16[16,16,1024]{2,1,0:T(8,128)(2,1)}, bf16[16,16,1024]{2,1,0:T(8,128)(2,1)}, u32[]{:S(2)}, u32[]{:S(2)}) collective-permute-start(bf16[16,16,1024]{2,1,0:T(8,128)(2,1)} %get-tuple-element.172), channel_id=1, source_target_pairs={{0,32},{32,64},{64,96},{96,0},{1,33},{33,65},{65,97},{97,1},{2,34}... | collective-permute-start | bytes 1572872 | tf_op jit(solution)/shard_map/ppermute | solution.py:463
  245.7 20.5 %all-to-all-start.5 = ((bf16[16,128,128]{2,1,0:T(8,128)(2,1)}), bf16[16,128,128]{2,1,0:T(8,128)(2,1)}, u32[]{:S(2)}, u32[]{:S(2)}) async-start(bf16[16,128,128]{2,1,0:T(8,128)(2,1)} %copy-done.30), calls=%async_computation.5 | async-start | bytes 1048576 | tf_op jit(solution)/shard_map/all_to_all | solution.py:519
  251.0 14.4 %collective-permute-start.14 = (bf16[128,512]{1,0:T(8,128)(2,1)S(1)}, bf16[128,512]{1,0:T(8,128)(2,1)S(1)}, u32[]{:S(2)}, u32[]{:S(2)}) collective-permute-start(bf16[128,512]{1,0:T(8,128)(2,1)S(1)} %get-tuple-element.182), channel_id=1, source_target_pairs={{0,16},{16,0},{1,17},{17,1},{2,18},{18,2},{3,19},{19,3},{4,20},{20... | collective-permute-start | bytes 393224 | tf_op jit(solution)/shard_map/ppermute | solution.py:447
  282.0 5.9 %collective-permute-start.16 = (f32[8,2304]{1,0:T(8,128)S(1)}, f32[8,2304]{1,0:T(8,128)S(1)}, u32[]{:S(2)}, u32[]{:S(2)}) collective-permute-start(f32[8,2304]{1,0:T(8,128)S(1)} %slice.230), channel_id=1, source_target_pairs={{1,0},{2,1},{3,2},{4,3},{5,4},{6,5},{7,6},{8,7},{9,8},{10,9},{11,1... | collective-permute-start | bytes 221192 | tf_op jit(solution)/shard_map/ppermute | solution.py:631
  304.6 11.9 %collective-permute-start.20 = (bf16[64,8,4480]{2,1,0:T(8,128)(2,1)}, bf16[64,8,4480]{2,1,0:T(8,128)(2,1)S(1)}, u32[]{:S(2)}, u32[]{:S(2)}) collective-permute-start(bf16[64,8,4480]{2,1,0:T(8,128)(2,1)} %get-tuple-element.161), channel_id=1, source_target_pairs={{0,16},{16,0},{1,17},{17,1},{2,18},{18,2},{3,19},{19,3},{4,20},{20... | collective-permute-start | bytes 13762568 | tf_op jit(solution)/shard_map/ppermute | solution.py:447
  309.0 37.4 %collective-permute-start.24 = (bf16[64,16,1024]{2,1,0:T(8,128)(2,1)}, bf16[64,16,1024]{2,1,0:T(8,128)(2,1)}, u32[]{:S(2)}, u32[]{:S(2)}) collective-permute-start(bf16[64,16,1024]{2,1,0:T(8,128)(2,1)} %dynamic-slice_bitcast_fusion.3), channel_id=1, source_target_pairs={{0,16},{16,0},{1,17},{17,1},{2,18},{18,2},{3,19},{19,3},{4,20},{20... | collective-permute-start | bytes 6291464 | tf_op jit(solution)/shard_map/ppermute | solution.py:447
  325.3 37.5 %collective-permute-start.23 = (bf16[16,8,4480]{2,1,0:T(8,128)(2,1)}, bf16[16,8,4480]{2,1,0:T(8,128)(2,1)}, u32[]{:S(2)}, u32[]{:S(2)}) collective-permute-start(bf16[16,8,4480]{2,1,0:T(8,128)(2,1)} %get-tuple-element.167), channel_id=1, source_target_pairs={{0,64},{32,96},{64,0},{96,32},{1,65},{33,97},{65,1},{97,33},{2,66}... | collective-permute-start | bytes 3440648 | tf_op jit(solution)/shard_map/ppermute | solution.py:463
  327.8 50.8 %collective-permute-start.22 = (bf16[16,8,4480]{2,1,0:T(8,128)(2,1)}, bf16[16,8,4480]{2,1,0:T(8,128)(2,1)}, u32[]{:S(2)}, u32[]{:S(2)}) collective-permute-start(bf16[16,8,4480]{2,1,0:T(8,128)(2,1)} %get-tuple-element.168), channel_id=1, source_target_pairs={{0,96},{32,0},{64,32},{96,64},{1,97},{33,1},{65,33},{97,65},{2,98}... | collective-permute-start | bytes 3440648 | tf_op jit(solution)/shard_map/ppermute | solution.py:463
  328.7 50.5 %collective-permute-start.21 = (bf16[16,8,4480]{2,1,0:T(8,128)(2,1)}, bf16[16,8,4480]{2,1,0:T(8,128)(2,1)}, u32[]{:S(2)}, u32[]{:S(2)}) collective-permute-start(bf16[16,8,4480]{2,1,0:T(8,128)(2,1)} %get-tuple-element.166), channel_id=1, source_target_pairs={{0,32},{32,64},{64,96},{96,0},{1,33},{33,65},{65,97},{97,1},{2,34}... | collective-permute-start | bytes 3440648 | tf_op jit(solution)/shard_map/ppermute | solution.py:463
  329.2 24.8 %all-to-all-start.6 = ((bf16[16,144,128]{2,1,0:T(8,128)(2,1)}), bf16[16,144,128]{2,1,0:T(8,128)(2,1)}, u32[]{:S(2)}, u32[]{:S(2)}) async-start(bf16[16,144,128]{2,1,0:T(8,128)(2,1)} %get-tuple-element.110), calls=%async_computation.6 | async-start | bytes 1179648 | tf_op jit(solution)/shard_map/all_to_all | solution.py:510
  351.3 45.4 %collective-permute-start.28 = (bf16[16,16,1024]{2,1,0:T(8,128)(2,1)}, bf16[16,16,1024]{2,1,0:T(8,128)(2,1)}, u32[]{:S(2)}, u32[]{:S(2)}) collective-permute-start(bf16[16,16,1024]{2,1,0:T(8,128)(2,1)} %get-tuple-element.170), channel_id=1, source_target_pairs={{0,64},{32,96},{64,0},{96,32},{1,65},{33,97},{65,1},{97,33},{2,66}... | collective-permute-start | bytes 1572872 | tf_op jit(solution)/shard_map/ppermute | solution.py:463
  352.0 49.1 %collective-permute-start.27 = (bf16[16,16,1024]{2,1,0:T(8,128)(2,1)}, bf16[16,16,1024]{2,1,0:T(8,128)(2,1)}, u32[]{:S(2)}, u32[]{:S(2)}) collective-permute-start(bf16[16,16,1024]{2,1,0:T(8,128)(2,1)} %get-tuple-element.171), channel_id=1, source_target_pairs={{0,96},{32,0},{64,32},{96,64},{1,97},{33,1},{65,33},{97,65},{2,98}... | collective-permute-start | bytes 1572872 | tf_op jit(solution)/shard_map/ppermute | solution.py:463
  356.0 27.0 %all-to-all-start.7 = ((bf16[16,128,128]{2,1,0:T(8,128)(2,1)}), bf16[16,128,128]{2,1,0:T(8,128)(2,1)}, u32[]{:S(2)}, u32[]{:S(2)}) async-start(bf16[16,128,128]{2,1,0:T(8,128)(2,1)} %copy-done.31), calls=%async_computation.7 | async-start | bytes 1048576 | tf_op jit(solution)/shard_map/all_to_all | solution.py:519
  362.9 38.5 %collective-permute-start.26 = (bf16[16,16,1024]{2,1,0:T(8,128)(2,1)}, bf16[16,16,1024]{2,1,0:T(8,128)(2,1)}, u32[]{:S(2)}, u32[]{:S(2)}) collective-permute-start(bf16[16,16,1024]{2,1,0:T(8,128)(2,1)} %get-tuple-element.169), channel_id=1, source_target_pairs={{0,32},{32,64},{64,96},{96,0},{1,33},{33,65},{65,97},{97,1},{2,34}... | collective-permute-start | bytes 1572872 | tf_op jit(solution)/shard_map/ppermute | solution.py:463
  395.1 8.1 %collective-permute-start.25 = (f32[8,2304]{1,0:T(8,128)S(1)}, f32[8,2304]{1,0:T(8,128)S(1)}, u32[]{:S(2)}, u32[]{:S(2)}) collective-permute-start(f32[8,2304]{1,0:T(8,128)S(1)} %slice.232), channel_id=1, source_target_pairs={{1,0},{2,1},{3,2},{4,3},{5,4},{6,5},{7,6},{8,7},{9,8},{10,9},{11,1... | collective-permute-start | bytes 221192 | tf_op jit(solution)/shard_map/ppermute | solution.py:631
  420.6 8.2 %collective-permute-start.30 = (bf16[64,8,4480]{2,1,0:T(8,128)(2,1)}, bf16[64,8,4480]{2,1,0:T(8,128)(2,1)}, u32[]{:S(2)}, u32[]{:S(2)}) collective-permute-start(bf16[64,8,4480]{2,1,0:T(8,128)(2,1)} %dynamic-slice_bitcast_fusion), channel_id=1, source_target_pairs={{0,16},{16,0},{1,17},{17,1},{2,18},{18,2},{3,19},{19,3},{4,20},{20... | collective-permute-start | bytes 13762568 | tf_op jit(solution)/shard_map/ppermute | solution.py:447
  425.5 44.0 %collective-permute-start.29 = (bf16[128,512]{1,0:T(8,128)(2,1)}, bf16[128,512]{1,0:T(8,128)(2,1)}, u32[]{:S(2)}, u32[]{:S(2)}) collective-permute-start(bf16[128,512]{1,0:T(8,128)(2,1)} %select_convert_fusion), channel_id=1, source_target_pairs={{0,16},{16,0},{1,17},{17,1},{2,18},{18,2},{3,19},{19,3},{4,20},{20... | collective-permute-start | bytes 393224 | tf_op jit(solution)/shard_map/ppermute | solution.py:447
  435.8 26.0 %all-to-all-start.8 = ((bf16[16,8,4480]{2,1,0:T(8,128)(2,1)}), bf16[16,8,4480]{2,1,0:T(8,128)(2,1)S(1)}, u32[]{:S(2)}, u32[]{:S(2)}) async-start(bf16[16,8,4480]{2,1,0:T(8,128)(2,1)} %fusion.9.refs_10_), calls=%async_computation.8 | async-start | bytes 2293760 | tf_op jit(solution)/shard_map/all_to_all | solution.py:451
  449.0 36.9 %collective-permute-start.37 = (bf16[16,8,4480]{2,1,0:T(8,128)(2,1)}, bf16[16,8,4480]{2,1,0:T(8,128)(2,1)}, u32[]{:S(2)}, u32[]{:S(2)}) collective-permute-start(bf16[16,8,4480]{2,1,0:T(8,128)(2,1)} %get-tuple-element.164), channel_id=1, source_target_pairs={{0,64},{32,96},{64,0},{96,32},{1,65},{33,97},{65,1},{97,33},{2,66}... | collective-permute-start | bytes 3440648 | tf_op jit(solution)/shard_map/ppermute | solution.py:463
  451.4 50.0 %collective-permute-start.36 = (bf16[16,8,4480]{2,1,0:T(8,128)(2,1)}, bf16[16,8,4480]{2,1,0:T(8,128)(2,1)}, u32[]{:S(2)}, u32[]{:S(2)}) collective-permute-start(bf16[16,8,4480]{2,1,0:T(8,128)(2,1)} %get-tuple-element.165), channel_id=1, source_target_pairs={{0,96},{32,0},{64,32},{96,64},{1,97},{33,1},{65,33},{97,65},{2,98}... | collective-permute-start | bytes 3440648 | tf_op jit(solution)/shard_map/ppermute | solution.py:463
  452.3 50.3 %collective-permute-start.35 = (bf16[16,8,4480]{2,1,0:T(8,128)(2,1)}, bf16[16,8,4480]{2,1,0:T(8,128)(2,1)}, u32[]{:S(2)}, u32[]{:S(2)}) collective-permute-start(bf16[16,8,4480]{2,1,0:T(8,128)(2,1)} %get-tuple-element.163), channel_id=1, source_target_pairs={{0,32},{32,64},{64,96},{96,0},{1,33},{33,65},{65,97},{97,1},{2,34}... | collective-permute-start | bytes 3440648 | tf_op jit(solution)/shard_map/ppermute | solution.py:463
  461.7 19.3 %all-to-all-start.11 = ((bf16[16,32,1024]{2,1,0:T(8,128)(2,1)}), bf16[16,32,1024]{2,1,0:T(8,128)(2,1)S(1)}, u32[]{:S(2)}, u32[]{:S(2)}) async-start(bf16[16,32,1024]{2,1,0:T(8,128)(2,1)} %pad_maximum_fusion), calls=%async_computation.11 | async-start | bytes 2097152 | tf_op jit(solution)/shard_map/all_to_all | solution.py:451
  481.1 25.4 %all-to-all-start.9 = ((f32[16,4,8,128]{3,1,2,0:T(4,128)}), f32[16,4,8,128]{3,1,2,0:T(4,128)S(1)}, u32[]{:S(2)}, u32[]{:S(2)}) async-start(f32[16,4,8,128]{3,1,2,0:T(4,128)} %bitcast.186), calls=%async_computation.9 | async-start | bytes 524288 | tf_op jit(solution)/shard_map/all_to_all | solution.py:451
  506.5 23.4 %all-to-all-start.10 = ((bf16[16,8,4480]{2,1,0:T(8,128)(2,1)}), bf16[16,8,4480]{2,1,0:T(8,128)(2,1)S(1)}, u32[]{:S(2)}, u32[]{:S(2)}) async-start(bf16[16,8,4480]{2,1,0:T(8,128)(2,1)} %fusion.6), calls=%async_computation.10 | async-start | bytes 2293760 | tf_op jit(solution)/shard_map/all_to_all | solution.py:451
  514.3 4.3 collective-permute-start.39
  515.3 4.0 collective-permute-start.34
  518.1 4.0 collective-permute-start.32
  530.1 4.4 collective-permute-start.38
  (114 other events, 1023.6 us)
Sparse Core Ops, SparseCore 0:
  14.2 122.8 all-gather.1
